TPU v7x, 256 devices: a whole 4x4x8 slice. The times are simulated.
256 devices in a mesh: ep: 64 (over x, z, core), cp: 4 (over y).
Axes of the slice: x: 4, y: 4, z: 8, core: 2. Of those that a mesh axis runs over, the one named last changes fastest.
Arguments:
- grad_out: bfloat16 [32768, 4096], P('ep', 'cp'), may hold values from -6 to 6
- route_ids: int32 [32768, 4], P('ep'), may hold values from 0 to 63, as said below
- fallback_ids: int32 [32768, 4], P('ep'), may hold values from 0 to 63
- slot_ids: int32 [32768, 4], P('ep'), may hold values from 0 to 79, as said below
- route_probs: float32 [32768, 4], P('ep'), may hold values from 0.05 to 0.5
- w_gate: bfloat16 [64, 768, 4096], P('ep', None, 'cp'), may hold values from -0.09375 to 0.09375
- w_up: bfloat16 [64, 768, 4096], P('ep', None, 'cp'), may hold values from -0.09375 to 0.09375
- w_down: bfloat16 [64, 768, 4096], P('ep', None, 'cp'), may hold values from -0.21875 to 0.21875
- gate_pre: bfloat16 [64, 768, 2560], P('ep', 'cp'), may hold values from -5 to 5
- up_pre: bfloat16 [64, 768, 2560], P('ep', 'cp'), may hold values from -5 to 5
- queries: bfloat16 [32768, 4096], P(('ep', 'cp')), may hold values from -5 to 5
- key_vectors: bfloat16 [32768, 256], P('ep'), may hold values from -5 to 5
- value_vectors: bfloat16 [32768, 256], P('ep'), may hold values from -6 to 6
- block_mask: int32 [64, 8, 8], P('ep'), may hold values 0 or 1
Outputs:
- grad_hidden: bfloat16 [32768, 4096], P(('ep', 'cp'))
- grad_queries: bfloat16 [32768, 4096], P(('ep', 'cp'))
- grad_keys: bfloat16 [32768, 256], P(('ep', 'cp'))
- grad_values: bfloat16 [32768, 256], P(('ep', 'cp'))
Inputs may be any that keep to these rules, and one draw needn't show every extreme that they name: `route_ids`: each row names 4 different experts. `slot_ids`: a value below 40 is a slot at the route's expert in route_ids, a value of 40 or more is 40 plus a slot at its expert in fallback_ids; within one sequence shard no two routes take the same slot of the same expert.
All inputs are finite; a program needn't handle non-finite values. No bound on the sum of `block_mask` on one device may be relied on, other than what follows from the above.
Results may differ from a plain program's by a relative error of at most 0.034.
Values may be sent and summed in bfloat16 or wider, within the bound.
No kernel may reach another device: no remote copies, remote signals or barrier semaphores. Data moves between devices by JAX's collectives and lax.ppermute only.
A program may use at most 128 MiB of HBM per device.

v0:
```python
import jax
import jax.numpy as jnp
from jax import lax
from jax.sharding import PartitionSpec as P

HEAD_DIM = 128


def silu_grads(hidden_grad, gate_saved, up_saved):
    gate_value = gate_saved.astype(jnp.float32)
    up_value = up_saved.astype(jnp.float32)
    sigmoid_gate = jax.nn.sigmoid(gate_value)
    gate_grad = hidden_grad * up_value * sigmoid_gate * (1.0 + gate_value * (1.0 - sigmoid_gate))
    up_grad = hidden_grad * gate_value * sigmoid_gate
    return (gate_grad.astype(jnp.bfloat16), up_grad.astype(jnp.bfloat16))


def attend(queries, key_vectors, value_vectors, out_grad, mask_table, query_pos):
    rows_here = queries.shape[0]
    key_count = key_vectors.shape[0]
    kv_heads = key_vectors.shape[1] // HEAD_DIM
    group_size = queries.shape[1] // HEAD_DIM // kv_heads
    block_count = mask_table.shape[0]
    block_len = key_count // block_count
    score_scale = HEAD_DIM ** (-0.5)
    query_heads = queries.reshape(rows_here, kv_heads, group_size, HEAD_DIM)
    grad_heads = out_grad.reshape(rows_here, kv_heads, group_size, HEAD_DIM)
    key_heads = key_vectors.reshape(key_count, kv_heads, HEAD_DIM)
    value_heads = value_vectors.reshape(key_count, kv_heads, HEAD_DIM)
    key_pos = jnp.arange(key_count, dtype=jnp.int32)
    query_block = query_pos // block_len
    chosen = (query_block[:, None] == jnp.arange(block_count, dtype=jnp.int32)[None, :]).astype(
        jnp.float32
    )
    row_flags = jnp.dot(chosen, mask_table.astype(jnp.float32))
    near_block = (
        jnp.broadcast_to(row_flags[:, :, None], (rows_here, block_count, block_len)).reshape(
            rows_here, key_count
        )
        > 0.5
    )
    same_block = query_block[:, None] == (key_pos // block_len)[None, :]
    visible = (key_pos[None, :] <= query_pos[:, None]) & (same_block | near_block)
    scores = (
        jnp.einsum("qhgd,khd->hgqk", query_heads, key_heads, preferred_element_type=jnp.float32)
        * score_scale
    )
    scores = jnp.where(visible, scores, -jnp.inf)
    row_peak = jnp.max(scores, axis=-1, keepdims=True)
    exponent = jnp.exp(scores - row_peak)
    prob_rows = exponent / jnp.sum(exponent, axis=-1, keepdims=True)
    probs_low = prob_rows.astype(jnp.bfloat16)
    prob_grad = jnp.einsum(
        "qhgd,khd->hgqk", grad_heads, value_heads, preferred_element_type=jnp.float32
    )
    row_total = jnp.sum(prob_rows * prob_grad, axis=-1, keepdims=True)
    score_grad = (prob_rows * (prob_grad - row_total)).astype(jnp.bfloat16)
    grad_query = (
        jnp.einsum("hgqk,khd->qhgd", score_grad, key_heads, preferred_element_type=jnp.float32)
        * score_scale
    )
    key_part = (
        jnp.einsum("hgqk,qhgd->khd", score_grad, query_heads, preferred_element_type=jnp.float32)
        * score_scale
    )
    value_part = jnp.einsum(
        "hgqk,qhgd->khd", probs_low, grad_heads, preferred_element_type=jnp.float32
    )
    return (
        grad_query.astype(jnp.bfloat16).reshape(rows_here, -1),
        key_part.reshape(key_count, -1),
        value_part.reshape(key_count, -1),
    )


def on_device(
    grad_out,
    route_ids,
    fallback_ids,
    slot_ids,
    route_probs,
    w_gate,
    w_up,
    w_down,
    gate_pre,
    up_pre,
    queries,
    key_vectors,
    value_vectors,
    block_mask,
):
    experts = lax.axis_size("ep")
    shard_tokens, quarter = grad_out.shape
    top_count = route_ids.shape[1]
    slot_count = gate_pre.shape[2]
    capacity = slot_count // experts
    route_count = shard_tokens * top_count
    overflow = slot_ids >= capacity
    target = (
        jnp.where(overflow, fallback_ids, route_ids) * capacity
        + jnp.where(overflow, slot_ids - capacity, slot_ids)
    ).reshape(-1)
    owners = (
        jnp.full((slot_count,), -1, jnp.int32)
        .at[target]
        .set(jnp.arange(route_count, dtype=jnp.int32))
    )
    filled = owners >= 0
    source_route = jnp.maximum(owners, 0)
    source_token = source_route // top_count
    weight = jnp.where(filled, route_probs.reshape(-1)[source_route], 0.0)
    outgoing = (grad_out[source_token].astype(jnp.float32) * weight[:, None]).astype(jnp.bfloat16)
    arrived = lax.all_to_all(
        outgoing.reshape(experts, capacity, quarter), "ep", split_axis=0, concat_axis=0, tiled=True
    ).reshape(slot_count, quarter)
    down_rows = w_down[0]
    gate_rows = w_gate[0]
    up_rows = w_up[0]
    contract_rows = (((0,), (0,)), ((), ()))
    partial_sum = lax.dot_general(
        down_rows, arrived, (((1,), (1,)), ((), ())), preferred_element_type=jnp.float32
    )
    hidden_grad = lax.psum(partial_sum.astype(jnp.bfloat16), "cp").astype(jnp.float32)
    gate_saved, up_saved = (
        lax.all_gather(gate_pre[0], "cp", axis=0, tiled=True),
        lax.all_gather(up_pre[0], "cp", axis=0, tiled=True),
    )
    gate_grad, up_grad = silu_grads(hidden_grad, gate_saved, up_saved)
    expert_grad = lax.dot_general(
        gate_grad, gate_rows, contract_rows, preferred_element_type=jnp.float32
    )
    expert_grad = expert_grad + lax.dot_general(
        up_grad, up_rows, contract_rows, preferred_element_type=jnp.float32
    )
    returned = lax.all_to_all(
        expert_grad.astype(jnp.bfloat16).reshape(experts, capacity, quarter),
        "ep",
        split_axis=0,
        concat_axis=0,
        tiled=True,
    ).reshape(slot_count, quarter)
    per_route = returned[target].reshape(shard_tokens, top_count, quarter)
    moe_grad = jnp.sum(per_route.astype(jnp.float32), axis=1)
    local_grad = (grad_out.astype(jnp.float32) + moe_grad).astype(jnp.bfloat16)
    grad_hidden = lax.all_to_all(local_grad, "cp", split_axis=0, concat_axis=1, tiled=True)
    rows_here = queries.shape[0]
    query_pos = lax.axis_index("cp") * rows_here + jnp.arange(rows_here, dtype=jnp.int32)
    grad_query, key_part, value_part = attend(
        queries, key_vectors, value_vectors, grad_hidden, block_mask[0], query_pos
    )
    key_sum, value_sum = (
        lax.psum_scatter(
            key_part.astype(jnp.bfloat16), "cp", scatter_dimension=0, tiled=True
        ).astype(jnp.float32),
        lax.psum_scatter(
            value_part.astype(jnp.bfloat16), "cp", scatter_dimension=0, tiled=True
        ).astype(jnp.float32),
    )
    return (grad_hidden, grad_query, key_sum.astype(jnp.bfloat16), value_sum.astype(jnp.bfloat16))


def solution(mesh):
    in_specs = (
        P("ep", "cp"),
        P("ep", None),
        P("ep", None),
        P("ep", None),
        P("ep", None),
        P("ep", None, "cp"),
        P("ep", None, "cp"),
        P("ep", None, "cp"),
        P("ep", "cp", None),
        P("ep", "cp", None),
        P(("ep", "cp"), None),
        P("ep", None),
        P("ep", None),
        P("ep", None, None),
    )
    out_specs = (
        P(("ep", "cp"), None),
        P(("ep", "cp"), None),
        P(("ep", "cp"), None),
        P(("ep", "cp"), None),
    )
    return jax.shard_map(
        on_device, mesh=mesh, in_specs=in_specs, out_specs=out_specs, check_vma=False
    )
```

profile of v0, /device:TPU:6, one launch (start us, length us, event | category | flops | bytes accessed | tf_op | source)
XLA Modules:
  0.0 547.3 jit_solution(13358107950190454512)
XLA Ops:
  7.2 0.7 all-gather.7.cloned.1.call-update
  7.9 0.7 fusion.44
  8.7 0.1 copy.90
  8.8 0.2 reshape.129
  9.0 8.1 %scatter_custom_fusion = s32[2560]{0:T(1024)S(1)} fusion(s32[2048]{0:T(1024)S(1)} %bitcast.110, s32[2048]{0:T(1024)S(1)} %iota.22, s32[]{:T(128)} %constant.55.clone.1), kind=kCustom, calls=%fused_computation.72 | custom fusion | bytes 10244 | tf_op jit(solution)/shard_map/scatter | solution.py:106
  17.1 0.8 copy.91
  18.0 0.2 reshape.130
  18.1 13.6 %gather_fusion.1 = f32[2560]{0:T(1024)S(1)} fusion(f32[2048]{0:T(1024)S(1)} %reshape.130, s32[3072]{0:T(1024)S(1)} %get-tuple-element.30), kind=kCustom, calls=%fused_computation.1 | custom fusion | bytes 30720 | tf_op jit(solution)/shard_map/gather | solution.py:111
  31.8 0.1 mul.65
  31.9 8.8 %gather_fusion = bf16[2560,1024]{1,0:T(8,128)(2,1)} fusion(bf16[512,1024]{1,0:T(8,128)(2,1)S(1)} %copy-done.2, s32[3072]{0:T(1024)S(1)} %get-tuple-element.31), kind=kCustom, calls=%fused_computation | custom fusion | bytes 10496000 | tf_op jit(solution)/shard_map/gather | solution.py:112
  40.7 5.8 %fusion.1 = bf16[64,40,1024]{2,1,0:T(8,128)(2,1)} fusion(bf16[64,40,1024]{2,1,0:T(8,128)(2,1)} %bitcast.94, f32[64,40]{1,0:T(8,128)S(1)} %mul.65), kind=kLoop, calls=%fused_computation.9 | loop fusion | flops 7864320 | bytes 10496000 | tf_op jit(solution)/shard_map/convert_element_type | solution.py:112
  46.6 12.3 %all-to-all-start = ((bf16[64,40,1024]{2,1,0:T(8,128)(2,1)}), bf16[64,40,1024]{2,1,0:T(8,128)(2,1)}, u32[]{:S(2)}, u32[]{:S(2)}) async-start(bf16[64,40,1024]{2,1,0:T(8,128)(2,1)} %fusion.1), calls=%async_computation | async-start | bytes 10485760 | tf_op jit(solution)/shard_map/all_to_all | solution.py:113
  58.9 0.7 all-gather.5.cloned.1.call-update
  59.7 115.4 %all-to-all-done = bf16[64,40,1024]{2,1,0:T(8,128)(2,1)} async-done(((bf16[64,40,1024]{2,1,0:T(8,128)(2,1)}), bf16[64,40,1024]{2,1,0:T(8,128)(2,1)}, u32[]{:S(2)}, u32[]{:S(2)}) %all-to-all-start) | async-done | bytes 5242912 | tf_op jit(solution)/shard_map/all_to_all | solution.py:113
  175.1 9.2 %fusion.15 = bf16[768,2560]{0,1:T(8,128)(2,1)} fusion(bf16[2560,1024]{1,0:T(8,128)(2,1)} %bitcast.2, bf16[1,768,1024]{2,1,0:T(8,128)(2,1)} %param.21), kind=kOutput, calls=%fused_computation.30 | convolution fusion | flops 4028497920 | bytes 10747904 | tf_op jit(solution)/shard_map/dot_general | solution.py:120
  184.4 6.5 %copy.93 = bf16[1,768,2560]{1,2,0:T(8,128)(2,1)} copy(bf16[1,768,2560]{2,1,0:T(8,128)(2,1)} %all-gather.7.cloned.1.call-done) | data formatting | bytes 7864320 | tf_op jit(solution)/shard_map/all_gather | solution.py:125
  190.9 6.1 %copy.92 = bf16[1,768,2560]{1,2,0:T(8,128)(2,1)} copy(bf16[1,768,2560]{2,1,0:T(8,128)(2,1)} %all-gather.5.cloned.1.call-done) | data formatting | bytes 7864320 | tf_op jit(solution)/shard_map/all_gather | solution.py:126
  197.0 80.0 %all-reduce.2.cloned.1.call-done = bf16[768,2560]{0,1:T(8,128)(2,1)} async-done(((bf16[768,2560]{0,1:T(8,128)(2,1)}), bf16[768,2560]{0,1:T(8,128)(2,1)}) %all-reduce.2.cloned.1.call-update) | async-done | bytes 3932176 | tf_op jit(solution)/shard_map/psum | solution.py:123
  276.9 14.8 %fusion.23 = f32[2560,1024]{1,0:T(8,128)} fusion(bf16[768,2560]{0,1:T(8,128)(2,1)} %all-reduce.2.cloned.1.call-done, bf16[1,768,2560]{1,2,0:T(8,128)(2,1)} %copy.92, bf16[1,768,2560]{1,2,0:T(8,128)(2,1)} %copy.93, bf16[1,768,1024]{2,1,0:T(8,128)(2,1)S(1)} %copy-done), kind=kOutput, calls=%fused_computation.38 | convolution fusion | flops 4052090880 | bytes 23855104 | tf_op jit(solution)/shard_map/dot_general | solution.py:129
  291.8 9.0 %add_convert_fusion = bf16[2560,1024]{1,0:T(8,128)(2,1)} fusion(f32[2560,1024]{1,0:T(8,128)} %fusion.23, bf16[768,2560]{0,1:T(8,128)(2,1)S(1)} %copy-done.9, bf16[1,768,2560]{1,2,0:T(8,128)(2,1)S(1)} %copy-done.5, bf16[1,768,1024]{2,1,0:T(8,128)(2,1)S(1)} %copy-done.10), kind=kOutput, calls=%fused_computation.10 | convolution fusion | flops 4047503360 | bytes 25165824 | tf_op jit(solution)/shard_map/dot_general | solution.py:132
  300.8 11.1 %all-to-all-start.1 = ((bf16[64,40,1024]{2,1,0:T(8,128)(2,1)}), bf16[64,40,1024]{2,1,0:T(8,128)(2,1)}, u32[]{:S(2)}, u32[]{:S(2)}) async-start(bf16[64,40,1024]{2,1,0:T(8,128)(2,1)} %bitcast.97), calls=%async_computation.1 | async-start | bytes 10485760 | tf_op jit(solution)/shard_map/all_to_all | solution.py:135
  311.8 1.3 copy.126
  313.2 0.2 copy.115
  313.4 0.1 reshape.137
  313.5 114.6 %all-to-all-done.1 = bf16[64,40,1024]{2,1,0:T(8,128)(2,1)} async-done(((bf16[64,40,1024]{2,1,0:T(8,128)(2,1)}), bf16[64,40,1024]{2,1,0:T(8,128)(2,1)}, u32[]{:S(2)}, u32[]{:S(2)}) %all-to-all-start.1) | async-done | bytes 5242912 | tf_op jit(solution)/shard_map/all_to_all | solution.py:135
  428.1 14.1 %gather_fusion.2 = bf16[2048,1024]{1,0:T(8,128)(2,1)} fusion(bf16[2560,1024]{1,0:T(8,128)(2,1)} %bitcast.11, s32[2048]{0:T(1024)S(1)} %broadcast_clamp_fusion), kind=kCustom, calls=%fused_computation.2 | custom fusion | bytes 8396800 | tf_op jit(solution)/shard_map/gather | solution.py:142
  442.2 8.4 %reshape.140 = f32[512,4,1024]{2,1,0:T(4,128)} reshape(bf16[2048,1024]{1,0:T(8,128)(2,1)} %gather_fusion.2) | data formatting | bytes 12582912 | tf_op jit(solution)/shard_map/convert_element_type | solution.py:143
  450.5 9.9 %reduce_sum.27 = f32[512,1024]{1,0:T(8,128)} reduce(f32[512,4,1024]{2,1,0:T(4,128)} %reshape.140, f32[]{:T(128)} %constant.64.clone.1), dimensions={1}, to_apply=%region_2.3 | reduce | flops 1572864 | bytes 10485764 | tf_op jit(solution)/shard_map/reduce_sum | solution.py:143
  460.4 2.9 add_convert_fusion.1
  463.4 3.5 all-to-all-start.2
  467.0 0.2 convolution_compare_fusion
  467.2 0.2 fusion.40
  467.3 7.1 %fusion.56 = (f32[2,16,128]{2,1,0:T(8,128)S(1)}, f32[2,16,128,512]{2,3,1,0:T(8,128)}) fusion(pred[128,512]{0,1:T(8,128)(4,1)S(1)} %fusion.40, bf16[512,2,128,1]{0,2,3,1:T(8,128)(2,1)S(1)} %copy.115, bf16[128,2,16,128]{0,3,2,1:T(8,128)(2,1)} %bitcast.102), kind=kOutput, calls=%fused_computation.93 | convolution fusion | flops 545260032 | bytes 9781248 | tf_op jit(solution)/shard_map/sub | solution.py:50
  474.4 7.7 %all-to-all-done.2 = bf16[4,128,1024]{2,1,0:T(8,128)(2,1)S(1)} async-done(((bf16[4,128,1024]{2,1,0:T(8,128)(2,1)}), bf16[4,128,1024]{2,1,0:T(8,128)(2,1)S(1)}, u32[]{:S(2)}, u32[]{:S(2)}) %all-to-all-start.2) | async-done | bytes 1048608 | tf_op jit(solution)/shard_map/all_to_all | solution.py:145
  482.2 0.7 copy.94
  482.8 4.8 fusion.2
  487.6 1.0 slice-done.1
  488.7 1.6 fusion.4
  490.3 2.0 copy-done.3
  492.2 1.5 fusion.32
  493.7 0.9 copy.105
  494.7 4.9 fusion.33
  499.6 0.8 copy.107
  500.4 3.9 multiply_convert_fusion
  504.3 2.3 copy.109
  506.6 1.3 copy.108
  507.9 6.9 %reduce-scatter.3.cloned.1.call-done = bf16[128,256]{1,0:T(8,128)(2,1)} async-done(((bf16[512,256]{1,0:T(8,128)(2,1)}), bf16[128,256]{1,0:T(8,128)(2,1)}) %reduce-scatter.3.cloned.1.call-update) | async-done | bytes 65552 | tf_op jit(solution)/shard_map/reduce_scatter | solution.py:152
  514.8 26.0 %reduce-scatter.5.cloned.1.call-done = bf16[128,256]{1,0:T(8,128)(2,1)} async-done(((bf16[512,256]{1,0:T(8,128)(2,1)}), bf16[128,256]{1,0:T(8,128)(2,1)}) %reduce-scatter.5.cloned.1.call-update) | async-done | bytes 65552 | tf_op jit(solution)/shard_map/reduce_scatter | solution.py:155
  (46 shorter events, 0.5 us)
Async XLA Ops:
  7.2 269.8 %copy-start = (bf16[1,768,1024]{2,1,0:T(8,128)(2,1)S(1)}, bf16[1,768,1024]{2,1,0:T(8,128)(2,1)}, u32[]{:S(2)}) copy-start(bf16[1,768,1024]{2,1,0:T(8,128)(2,1)} %param.19) | copy-start | bytes 4718596
  7.2 177.2 %all-gather.7.cloned.1.call-start = ((), (), s32[]{:S(2)}) async-start(), calls=%async_computation.9 | async-start | bytes 4915200 | tf_op jit(solution)/shard_map/all_gather | solution.py:125
  18.1 13.7 %copy-start.2 = (bf16[512,1024]{1,0:T(8,128)(2,1)S(1)}, bf16[512,1024]{1,0:T(8,128)(2,1)}, u32[]{:S(2)}) copy-start(bf16[512,1024]{1,0:T(8,128)(2,1)} %param.14) | copy-start | bytes 3145732
  46.6 128.5 %all-to-all-start = ((bf16[64,40,1024]{2,1,0:T(8,128)(2,1)}), bf16[64,40,1024]{2,1,0:T(8,128)(2,1)}, u32[]{:S(2)}, u32[]{:S(2)}) async-start(bf16[64,40,1024]{2,1,0:T(8,128)(2,1)} %fusion.1), calls=%async_computation | async-start | bytes 10485760 | tf_op jit(solution)/shard_map/all_to_all | solution.py:113
  58.9 132.1 %all-gather.5.cloned.1.call-start = ((), (), s32[]{:S(2)}) async-start(), calls=%async_computation.8 | async-start | bytes 4915200 | tf_op jit(solution)/shard_map/all_gather | solution.py:126
  59.6 217.3 %all-reduce.2.cloned.1.call-start = ((), (), s32[]{:S(2)}) async-start(), calls=%async_computation.5 | async-start | bytes 7864320 | tf_op jit(solution)/shard_map/psum | solution.py:123
  276.9 14.8 %copy-start.5 = (bf16[1,768,2560]{1,2,0:T(8,128)(2,1)S(1)}, bf16[1,768,2560]{1,2,0:T(8,128)(2,1)}, u32[]{:S(2)}) copy-start(bf16[1,768,2560]{1,2,0:T(8,128)(2,1)} %copy.93) | copy-start | bytes 11796484
  276.9 14.8 %copy-start.9 = (bf16[768,2560]{0,1:T(8,128)(2,1)S(1)}, bf16[768,2560]{0,1:T(8,128)(2,1)}, u32[]{:S(2)}) copy-start(bf16[768,2560]{0,1:T(8,128)(2,1)} %all-reduce.2.cloned.1.call-done) | copy-start | bytes 11796484
  276.9 14.8 %copy-start.10 = (bf16[1,768,1024]{2,1,0:T(8,128)(2,1)S(1)}, bf16[1,768,1024]{2,1,0:T(8,128)(2,1)}, u32[]{:S(2)}) copy-start(bf16[1,768,1024]{2,1,0:T(8,128)(2,1)} %param.20) | copy-start | bytes 4718596
  300.8 11.1 %copy-start.6 = (bf16[128,4096]{1,0:T(8,128)(2,1)S(1)}, bf16[128,4096]{1,0:T(8,128)(2,1)}, u32[]{:S(2)}) copy-start(bf16[128,4096]{1,0:T(8,128)(2,1)} %param.24) | copy-start | bytes 3145732
  300.8 12.4 %copy-start.7 = (bf16[512,256]{1,0:T(8,128)(2,1)S(1)}, bf16[512,256]{1,0:T(8,128)(2,1)}, u32[]{:S(2)}) copy-start(bf16[512,256]{1,0:T(8,128)(2,1)} %param.25) | copy-start | bytes 786436
  300.8 12.6 %copy-start.8 = (bf16[512,256]{1,0:T(8,128)(2,1)S(1)}, bf16[512,256]{1,0:T(8,128)(2,1)}, u32[]{:S(2)}) copy-start(bf16[512,256]{1,0:T(8,128)(2,1)} %param.26) | copy-start | bytes 786436
  300.8 127.3 %all-to-all-start.1 = ((bf16[64,40,1024]{2,1,0:T(8,128)(2,1)}), bf16[64,40,1024]{2,1,0:T(8,128)(2,1)}, u32[]{:S(2)}, u32[]{:S(2)}) async-start(bf16[64,40,1024]{2,1,0:T(8,128)(2,1)} %bitcast.97), calls=%async_computation.1 | async-start | bytes 10485760 | tf_op jit(solution)/shard_map/all_to_all | solution.py:135
  460.4 6.5 %copy-start.11 = (s32[1,8,8]{2,1,0:T(8,128)S(1)}, s32[1,8,8]{2,1,0:T(8,128)}, u32[]{:S(2)}) copy-start(s32[1,8,8]{2,1,0:T(8,128)} %param.27) | copy-start | bytes 772
  463.4 18.8 %all-to-all-start.2 = ((bf16[4,128,1024]{2,1,0:T(8,128)(2,1)}), bf16[4,128,1024]{2,1,0:T(8,128)(2,1)S(1)}, u32[]{:S(2)}, u32[]{:S(2)}) async-start(bf16[4,128,1024]{2,1,0:T(8,128)(2,1)} %bitcast.104), calls=%async_computation.2 | async-start | bytes 2097152 | tf_op jit(solution)/shard_map/all_to_all | solution.py:145
  466.9 47.9 %reduce-scatter.3.cloned.1.call-start = ((), (), s32[]{:S(2)}) async-start(), calls=%async_computation.6 | async-start | bytes 327680 | tf_op jit(solution)/shard_map/reduce_scatter | solution.py:152
  482.8 4.8 slice-start
  482.8 5.8 %slice-start.1 = ((s8[8388608]{0:T(1024)(128)(4,1)}), s8[4194304]{0:T(1024)(128)(4,1)S(1)}, s32[]{:S(2)}) async-start(s8[8388608]{0:T(1024)(128)(4,1)} %bitcast.95), calls=%async_computation.11 | async-start | bytes 8388608
  488.7 3.5 copy-start.4
  490.2 2.0 copy-start.3
  494.6 46.2 %reduce-scatter.5.cloned.1.call-start = ((), (), s32[]{:S(2)}) async-start(), calls=%async_computation.7 | async-start | bytes 327680 | tf_op jit(solution)/shard_map/reduce_scatter | solution.py:155
  499.5 41.2 %copy-start.1 = (bf16[1,768,1024]{2,1,0:T(8,128)(2,1)S(1)}, bf16[1,768,1024]{2,1,0:T(8,128)(2,1)}, u32[]{:S(2)}) copy-start(bf16[1,768,1024]{2,1,0:T(8,128)(2,1)} %param.19) | copy-start | bytes 4718596
Sparse Core Ops, SparseCore 0:
  9.8 51.5 all-gather.6
  63.2 48.9 all-gather.4
  184.5 92.4 all-reduce.1
  494.7 20.0 reduce-scatter.2
  517.9 22.8 reduce-scatter.4
where the time goes:
time: 548 us; the launch traced here: 547 us
  waiting for transfers between devices  352 us (64%)
  local copies, waits for them, and re-layouts  77.6 us (14%)
  matrix products  55.4 us (10%)
  starting transfers between devices  27.1 us (5%)
  other arithmetic  21.1 us (4%)
  between operations  14.1 us (3%)
    all_to_all x1, waiting for transfers between devices, on_device(): lax.all_to_all(outgoing.reshape(experts, capacity, quarter), 'ep', split_...  115 us
    all_to_all x1, waiting for transfers between devices, on_device(): lax.all_to_all(expert_grad.astype(jnp.bfloat16).reshape(experts, capacity...  115 us
    psum x1, waiting for transfers between devices, on_device(): lax.psum(partial_sum.astype(jnp.bfloat16), 'cp').astype(jnp.float32)  80 us
    reduce_scatter x1, waiting for transfers between devices, on_device(): lax.psum_scatter(value_part.astype(jnp.bfloat16), 'cp', scatter_dimension...  26 us
    dot_general x1, matrix products, on_device(): lax.dot_general(gate_grad, gate_rows, contract_rows, preferred_element_ty...  14.8 us
    gather x1, local copies, waits for them, and re-layouts, on_device(): per_route = returned[target].reshape(shard_tokens, top_count, quarter)  14.1 us
    gather x1, local copies, waits for them, and re-layouts, on_device(): weight = jnp.where(filled, route_probs.reshape(-1)[source_route], 0.0)  13.6 us
    all_to_all x1, starting transfers between devices, on_device(): lax.all_to_all(outgoing.reshape(experts, capacity, quarter), 'ep', split_...  12.3 us
  transfers between devices with their start and end apart: 8, of which 6 were waited for; matrix products, arithmetic and copies ran while one was open for 15% of the time, Pallas kernels for 0%

commit v1 on v0

v1 whole, which is shorter than its diff:
```python
import functools

import jax
import jax.numpy as jnp
from jax import lax
from jax.experimental import pallas as pl
from jax.experimental.pallas import tpu as pltpu
from jax.sharding import PartitionSpec as P

HEAD_DIM = 128
LANES = 128
PARTS = 2
STEPS = 4
VMEM_LIMIT = 60 * 1024 * 1024

f32 = jnp.float32
bf16 = jnp.bfloat16


def params():
    return pltpu.CompilerParams(vmem_limit_bytes=VMEM_LIMIT)


def cost(flops, moved, exps=0):
    return pl.CostEstimate(flops=flops, bytes_accessed=moved, transcendentals=exps)


def weave(out_ref, wide, low, high):
    rows = low.shape[0]
    for j in range(wide.shape[0]):
        cols = slice(j * LANES, (j + 1) * LANES)
        wide[j, pl.ds(0, rows, 2), :] = low[:, cols]
        wide[j, pl.ds(1, rows, 2), :] = high[:, cols]
        out_ref[:, cols] = wide[j].astype(bf16)


def unweave(rows_ref, wide):
    slabs, rows = wide.shape[0], wide.shape[1] // 2
    for j in range(slabs):
        wide[j] = rows_ref[:, j * LANES : (j + 1) * LANES].astype(f32)
    low = [wide[j, pl.ds(0, rows, 2), :].astype(bf16) for j in range(slabs)]
    high = [wide[j, pl.ds(1, rows, 2), :].astype(bf16) for j in range(slabs)]
    return jnp.concatenate(low, axis=1), jnp.concatenate(high, axis=1)


def woven(rows, half):
    return pltpu.VMEM((half // LANES, 2 * rows, LANES), f32)


def split_by(row, size, count):
    factor = (1 << 16) // size + 1
    assert all((r * factor) >> 16 == r // size for r in range(count))
    return (row * factor) >> 16


def route_rows(part, capacity, ids_ref, spare_ref, slot_ref, probs_ref, grad_ref, out_ref, wide):
    rows, half = out_ref.shape[0] // 2, out_ref.shape[1]
    tokens = grad_ref.shape[0]
    share = capacity // PARTS
    overflow = slot_ref[...] >= capacity
    expert = jnp.where(overflow, spare_ref[...], ids_ref[...])
    target = expert * capacity + slot_ref[...] - jnp.where(overflow, capacity, 0)
    row = lax.broadcasted_iota(jnp.int32, (rows, 1), 0) + pl.program_id(0) * rows
    group = split_by(row, share, rows * STEPS)
    dest = group * (capacity - share) + row + part * share
    weights = jnp.zeros((rows, tokens), f32)
    for k in range(target.shape[0]):
        weights = jnp.where(target[k : k + 1, :] == dest, probs_ref[k : k + 1, :], weights)
    weight = jnp.sum(weights, axis=1, keepdims=True)
    chosen = jnp.where(weights != 0.0, 1.0, 0.0).astype(bf16)
    picked = jnp.dot(chosen, grad_ref[...], preferred_element_type=f32)
    picked = picked * weight
    weave(out_ref, wide, picked[:, :half], picked[:, half:])


def send_rows(part, experts, capacity, ids, spare, slots, probs, grad):
    rows, (tokens, width) = experts * capacity // PARTS, grad.shape
    step, half = rows // STEPS, width // 2
    routes = pl.BlockSpec(slots.shape, lambda i: (0, 0))
    return pl.pallas_call(
        functools.partial(route_rows, part, capacity),
        grid=(STEPS,),
        in_specs=[routes] * 4 + [pl.BlockSpec(grad.shape, lambda i: (0, 0))],
        out_specs=pl.BlockSpec((2 * step, half), lambda i: (i, 0)),
        out_shape=jax.ShapeDtypeStruct((2 * rows, half), bf16),
        scratch_shapes=[woven(step, half)],
        compiler_params=params(),
        cost_estimate=cost(2 * rows * tokens * width, 4 * rows * width),
        name="send_rows",
    )(ids, spare, slots, probs, grad)


def turn_kernel(share, saved_ref, *refs):
    outs, tall = refs[:-1], refs[-1]
    quarters, kinds = saved_ref.shape[:2]
    groups = saved_ref.shape[3] // (PARTS * share)
    for kind in range(kinds):
        hidden = jnp.concatenate([saved_ref[c, kind] for c in range(quarters)], axis=0)
        rows = hidden.astype(f32).T
        for part in range(PARTS):
            for g in range(groups):
                start = (g * PARTS + part) * share
                tall[g * share : (g + 1) * share, :] = rows[start : start + share, :]
            outs[part * kinds + kind][...] = tall[...].astype(bf16)


def turn_saved(saved, share):
    quarters, kinds, units, slots = saved.shape
    hidden, rows = quarters * units, slots // PARTS
    step = rows // STEPS
    return pl.pallas_call(
        functools.partial(turn_kernel, share),
        grid=(STEPS,),
        in_specs=[pl.BlockSpec((quarters, kinds, units, PARTS * step), lambda i: (0, 0, 0, i))],
        out_specs=[pl.BlockSpec((step, hidden), lambda i: (i, 0))] * (PARTS * kinds),
        out_shape=[jax.ShapeDtypeStruct((rows, hidden), bf16)] * (PARTS * kinds),
        scratch_shapes=[pltpu.VMEM((step, hidden), f32)],
        compiler_params=params(),
        cost_estimate=cost(saved.size, 4 * saved.size),
        name="turn_saved",
    )(saved)


def down_rows_kernel(rows_ref, down_ref, out_ref, wide):
    half = rows_ref.shape[1]
    low, high = unweave(rows_ref, wide)
    total = jnp.dot(low, down_ref[:half, :], preferred_element_type=f32)
    total = total + jnp.dot(high, down_ref[half:, :], preferred_element_type=f32)
    out_ref[...] = total.astype(bf16)


def project_down(arrived, down_t):
    rows, half = arrived.shape[0] // 2, arrived.shape[1]
    width, hidden = down_t.shape
    step = rows // STEPS
    return pl.pallas_call(
        down_rows_kernel,
        grid=(STEPS,),
        in_specs=[
            pl.BlockSpec((2 * step, half), lambda i: (i, 0)),
            pl.BlockSpec(down_t.shape, lambda i: (0, 0)),
        ],
        out_specs=pl.BlockSpec((step, hidden), lambda i: (i, 0)),
        out_shape=jax.ShapeDtypeStruct((rows, hidden), bf16),
        scratch_shapes=[woven(step, half)],
        compiler_params=params(),
        cost_estimate=cost(2 * rows * width * hidden, 2 * rows * (width + hidden)),
        name="project_down",
    )(arrived, down_t)


def expert_kernel(hidden_ref, gate_ref, up_ref, wg_ref, wu_ref, out_ref, wide):
    rows, half = hidden_ref.shape[0], out_ref.shape[1]
    grad = hidden_ref[...].astype(f32)
    gate = gate_ref[...].astype(f32)
    up = up_ref[...].astype(f32)
    sig = 1.0 / (1.0 + jnp.exp(-gate))
    shared = grad * sig
    gate_grad = (shared * up * (1.0 + gate * (1.0 - sig))).astype(bf16)
    up_grad = (shared * gate).astype(bf16)
    total = jnp.dot(gate_grad, wg_ref[...], preferred_element_type=f32)
    total = total + jnp.dot(up_grad, wu_ref[...], preferred_element_type=f32)
    weave(out_ref, wide, total[:, :half], total[:, half:])


def expert_rows(hidden_grad, gate, up, w_gate, w_up):
    rows, hidden = hidden_grad.shape
    width = w_gate.shape[1]
    step, half = rows // STEPS, width // 2
    row_block = pl.BlockSpec((step, hidden), lambda i: (i, 0))
    whole = pl.BlockSpec(w_gate.shape, lambda i: (0, 0))
    return pl.pallas_call(
        expert_kernel,
        grid=(STEPS,),
        in_specs=[row_block, row_block, row_block, whole, whole],
        out_specs=pl.BlockSpec((2 * step, half), lambda i: (i, 0)),
        out_shape=jax.ShapeDtypeStruct((2 * rows, half), bf16),
        scratch_shapes=[woven(step, half)],
        compiler_params=params(),
        cost_estimate=cost(
            128 * rows * hidden * width, 2 * rows * (3 * hidden + width), rows * hidden
        ),
        name="expert_rows",
    )(hidden_grad, gate, up, w_gate, w_up)


def collect_kernel(slots_ref, rows_ref, base_ref, out_ref, total, wide):
    step = pl.program_id(0)
    tokens = slots_ref.shape[0]
    rows, half = rows_ref.shape[0] // 2, rows_ref.shape[1]

    @pl.when(step == 0)
    def _():
        total[...] = base_ref[...].astype(f32)

    row = lax.broadcasted_iota(jnp.int32, (tokens, rows), 1) + step * rows
    chosen = jnp.zeros((tokens, rows), f32)
    for k in range(slots_ref.shape[1]):
        chosen = jnp.where(slots_ref[:, k : k + 1] == row, 1.0, chosen)
    chosen = chosen.astype(bf16)
    low, high = unweave(rows_ref, wide)
    total[:, :half] += jnp.dot(chosen, low, preferred_element_type=f32)
    total[:, half:] += jnp.dot(chosen, high, preferred_element_type=f32)

    @pl.when(step == STEPS - 1)
    def _():
        out_ref[...] = total[...].astype(out_ref.dtype)


def collect_rows(slots, returned, base, out_dtype):
    tokens, width = base.shape
    rows, half = returned.shape[0] // 2, returned.shape[1]
    step = rows // STEPS
    return pl.pallas_call(
        collect_kernel,
        grid=(STEPS,),
        in_specs=[
            pl.BlockSpec(slots.shape, lambda i: (0, 0)),
            pl.BlockSpec((2 * step, half), lambda i: (i, 0)),
            pl.BlockSpec(base.shape, lambda i: (0, 0)),
        ],
        out_specs=pl.BlockSpec(base.shape, lambda i: (0, 0)),
        out_shape=jax.ShapeDtypeStruct(base.shape, out_dtype),
        scratch_shapes=[pltpu.VMEM((tokens, width), f32), woven(step, half)],
        compiler_params=params(),
        cost_estimate=cost(2 * rows * tokens * width, 2 * rows * width + 8 * tokens * width),
        name="collect_rows",
    )(slots, returned, base)


def probs_kernel(q_ref, k_ref, seen_ref, out_ref):
    length = q_ref.shape[0]
    block = length // 2
    scale = HEAD_DIM ** (-0.5)
    for part in range(2):
        keys = (part + 1) * block
        cols = slice(part * block, (part + 1) * block)
        scores = lax.dot_general(
            k_ref[:keys, :], q_ref[cols, :], (((1,), (1,)), ((), ())), preferred_element_type=f32
        )
        scores = jnp.where(seen_ref[:keys, cols] > 0, scores * scale, -jnp.inf)
        peak = jnp.max(scores, axis=0, keepdims=True)
        exponent = jnp.exp(scores - peak)
        out_ref[0, :keys, cols] = exponent / jnp.sum(exponent, axis=0, keepdims=True)
        if keys < length:
            out_ref[0, keys:, cols] = jnp.zeros((length - keys, block), f32)


def attention_probs(queries, keys, seen):
    length, heads = queries.shape[0], queries.shape[1] // HEAD_DIM
    return pl.pallas_call(
        probs_kernel,
        grid=(heads,),
        in_specs=[
            pl.BlockSpec((length, HEAD_DIM), lambda h: (0, h)),
            pl.BlockSpec(keys.shape, lambda h: (0, 0)),
            pl.BlockSpec(seen.shape, lambda h: (0, 0)),
        ],
        out_specs=pl.BlockSpec((1, length, length), lambda h: (h, 0, 0)),
        out_shape=jax.ShapeDtypeStruct((heads, length, length), f32),
        compiler_params=params(),
        cost_estimate=cost(
            2 * heads * length * length * HEAD_DIM,
            4 * heads * length * length,
            heads * length * length,
        ),
        name="attention_probs",
    )(queries, keys, seen)


def grads_kernel(heads, probs_ref, grad_ref, q_ref, v_ref, kt_ref, out_ref, sum_k, sum_v):
    head = pl.program_id(0)
    length = q_ref.shape[0]
    block = length // 2
    scale = HEAD_DIM ** (-0.5)

    @pl.when(head == 0)
    def _():
        sum_k[...] = jnp.zeros_like(sum_k)
        sum_v[...] = jnp.zeros_like(sum_v)

    @pl.when(head < heads)
    def _():
        for part in range(2):
            keys = (part + 1) * block
            cols = slice(part * block, (part + 1) * block)
            probs = probs_ref[0, :keys, cols]
            grad = grad_ref[cols, :]
            prob_grad = lax.dot_general(
                v_ref[:keys, :], grad, (((1,), (1,)), ((), ())), preferred_element_type=f32
            )
            row_total = jnp.sum(probs * prob_grad, axis=0, keepdims=True)
            score_grad = (probs * (prob_grad - row_total)).astype(bf16)
            query_grad = jnp.dot(kt_ref[:, :keys], score_grad, preferred_element_type=f32) * scale
            out_ref[cols, :] = query_grad.T.astype(bf16)
            sum_k[:keys, :] += jnp.dot(score_grad, q_ref[cols, :], preferred_element_type=f32)
            sum_v[:keys, :] += jnp.dot(probs.astype(bf16), grad, preferred_element_type=f32)

    @pl.when(head == heads)
    def _():
        out_ref[...] = (sum_k[...] * scale).astype(bf16)

    @pl.when(head == heads + 1)
    def _():
        out_ref[...] = sum_v[...].astype(bf16)


def attention_grads(probs, out_grad, queries, values, keys_t):
    heads, length, _ = probs.shape
    head_cols = pl.BlockSpec((length, HEAD_DIM), lambda h: (0, jnp.minimum(h, heads - 1)))
    return pl.pallas_call(
        functools.partial(grads_kernel, heads),
        grid=(heads + 2,),
        in_specs=[
            pl.BlockSpec((1, length, length), lambda h: (jnp.minimum(h, heads - 1), 0, 0)),
            head_cols,
            head_cols,
            pl.BlockSpec((length, HEAD_DIM), lambda h: (0, 0)),
            pl.BlockSpec(keys_t.shape, lambda h: (0, 0)),
        ],
        out_specs=pl.BlockSpec((length, HEAD_DIM), lambda h: (0, h)),
        out_shape=jax.ShapeDtypeStruct((length, (heads + 2) * HEAD_DIM), bf16),
        scratch_shapes=[pltpu.VMEM((length, HEAD_DIM), f32), pltpu.VMEM((length, HEAD_DIM), f32)],
        compiler_params=params(),
        cost_estimate=cost(8 * heads * length * length * HEAD_DIM, 4 * heads * length * length),
        name="attention_grads",
    )(probs, out_grad, queries, values, keys_t)


def to_rows(grads):
    parts = lax.axis_size("cp")
    me = lax.axis_index("cp")
    rows, width = grads.shape[0] // parts, grads.shape[1]
    out = jnp.zeros((rows, parts * width), grads.dtype)
    for shift in range(parts):
        piece = lax.dynamic_slice_in_dim(grads, ((me + shift) % parts) * rows, rows, 0)
        if shift:
            piece = lax.ppermute(piece, "cp", [(i, (i + shift) % parts) for i in range(parts)])
        out = lax.dynamic_update_slice(out, piece, (0, ((me - shift) % parts) * width))
    return out


def to_heads(queries):
    parts = lax.axis_size("cp")
    me = lax.axis_index("cp")
    rows, width = queries.shape[0], queries.shape[1] // parts
    out = jnp.zeros((parts, rows, width), queries.dtype)
    for shift in range(parts):
        piece = lax.dynamic_slice_in_dim(queries, ((me + shift) % parts) * width, width, 1)
        if shift:
            piece = lax.ppermute(piece, "cp", [(i, (i + shift) % parts) for i in range(parts)])
        out = lax.dynamic_update_slice(out, piece[None], ((me - shift) % parts, 0, 0))
    return out.reshape(parts * rows, width)


def seen_keys(mask_table, length):
    blocks = mask_table.shape[0]
    size = length // blocks
    pos = jnp.arange(length, dtype=jnp.int32)
    near = jnp.broadcast_to(mask_table.T[:, None, :, None], (blocks, size, blocks, size))
    near = near.reshape(length, length) > 0
    same = (pos // size)[:, None] == (pos // size)[None, :]
    return ((pos[:, None] <= pos[None, :]) & (same | near)).astype(f32)


def swap(rows, axis):
    return lax.all_to_all(rows, axis, split_axis=0, concat_axis=0, tiled=True)


def on_device(
    grad_out,
    route_ids,
    fallback_ids,
    slot_ids,
    route_probs,
    w_gate,
    w_up,
    w_down,
    gate_pre,
    up_pre,
    queries,
    key_vectors,
    value_vectors,
    block_mask,
):
    experts = lax.axis_size("ep")
    quarters = lax.axis_size("cp")
    tokens, width = grad_out.shape
    slot_count = gate_pre.shape[2]
    capacity = slot_count // experts
    share = capacity // PARTS
    part_rows = experts * share
    half = width // 2

    routes = (route_ids.T, fallback_ids.T, slot_ids.T)
    probs_t = route_probs.T
    outgoing = [
        send_rows(part, experts, capacity, *routes, probs_t, grad_out) for part in range(PARTS)
    ]
    saved = lax.all_gather(jnp.stack([gate_pre[0], up_pre[0]]), "cp", axis=0)

    overflow = routes[2] >= capacity
    expert = jnp.where(overflow, routes[1], routes[0])
    slot = routes[2] - jnp.where(overflow, capacity, 0)
    in_part = [
        jnp.where(slot // share == part, expert * share + slot - part * share, -1).T
        for part in range(PARTS)
    ]
    my_queries = to_heads(queries)
    heads_here = width // HEAD_DIM
    group = heads_here * quarters // (key_vectors.shape[1] // HEAD_DIM)
    kv_head = lax.axis_index("cp") * heads_here // group
    keys = lax.dynamic_slice_in_dim(key_vectors, kv_head * HEAD_DIM, HEAD_DIM, 1)
    values = lax.dynamic_slice_in_dim(value_vectors, kv_head * HEAD_DIM, HEAD_DIM, 1)
    probs = attention_probs(my_queries, keys, seen_keys(block_mask[0], tokens))
    early = lax.optimization_barrier((outgoing[1], w_down[0].T, in_part))
    outgoing[1], down_t, in_part = early

    def exchange(rows):
        rows = swap(rows.reshape(experts, 2 * share, half), "ep")
        return rows.reshape(2 * part_rows, half)

    arrived = exchange(outgoing[0])
    first_sum, rows = lax.optimization_barrier((project_down(arrived, down_t), outgoing[1]))
    hidden_grad = lax.psum(first_sum, "cp")
    arrived = exchange(rows)
    saved = turn_saved(saved, share)
    rows = expert_rows(hidden_grad, saved[0], saved[1], w_gate[0], w_up[0])
    arrived, rows, saved = lax.optimization_barrier((arrived, rows, saved))
    later_sum = project_down(arrived, down_t)
    rows, _ = lax.optimization_barrier((rows, later_sum))
    back = [list(range(quarters))[::-1]]
    later_grad = lax.psum(later_sum, "cp", axis_index_groups=back)
    returned = exchange(rows)
    returned_later = exchange(expert_rows(later_grad, saved[2], saved[3], w_gate[0], w_up[0]))

    total = collect_rows(in_part[0], returned, grad_out, f32)
    ready = (returned_later, total, probs, my_queries, values, keys.T)
    returned_later, total, probs, my_queries, values, keys_t = lax.optimization_barrier(ready)
    local_grad = collect_rows(in_part[1], returned_later, total, bf16)
    grad_hidden = to_rows(local_grad)
    packed = attention_grads(probs, local_grad, my_queries, values, keys_t)
    packed, grad_hidden = lax.optimization_barrier((packed, grad_hidden))
    packed = swap(packed.reshape(quarters, tokens // quarters, -1), "cp")
    grad_query = packed[:, :, :width].transpose(1, 0, 2).reshape(tokens // quarters, -1)
    sums = packed[:, :, width:].astype(f32)
    sums = sums.reshape(quarters * heads_here // group, -1, tokens // quarters, 2, HEAD_DIM)
    sums = jnp.sum(sums, axis=1).transpose(2, 1, 0, 3).reshape(2, tokens // quarters, -1)
    sums = sums.astype(bf16)
    return (grad_hidden, grad_query, sums[0], sums[1])


def solution(mesh):
    in_specs = (
        P("ep", "cp"),
        P("ep", None),
        P("ep", None),
        P("ep", None),
        P("ep", None),
        P("ep", None, "cp"),
        P("ep", None, "cp"),
        P("ep", None, "cp"),
        P("ep", "cp", None),
        P("ep", "cp", None),
        P(("ep", "cp"), None),
        P("ep", None),
        P("ep", None),
        P("ep", None, None),
    )
    out_specs = (
        P(("ep", "cp"), None),
        P(("ep", "cp"), None),
        P(("ep", "cp"), None),
        P(("ep", "cp"), None),
    )
    return jax.shard_map(
        on_device, mesh=mesh, in_specs=in_specs, out_specs=out_specs, check_vma=False
    )
```

time: 548 us -> 381 us (0.70)
  waiting for transfers between devices: 352 us -> 180 us
  Pallas kernels: 0 us -> 84.8 us
  local copies, waits for them, and re-layouts: 77.6 us -> 21.3 us
  matrix products: 55.4 us -> 0 us
  blocking collectives: 0 us -> 23.3 us
  starting transfers between devices: 27.1 us -> 49.6 us
  other arithmetic: 21.1 us -> 6.56 us
    all_to_all x3 -> x4, waiting for transfers between devices: 238 us -> 72.8 us  [swap(): return lax.all_to_all(rows, axis, split_axis=0, concat_axis=0, tiled=True)]
    pallas_call x0 -> x11, Pallas kernels: none -> 84.8 us  [the longest x2 18.3 us: expert_rows(): pl.pallas_call(expert_kernel, grid=(STEPS,), in_specs=[row_block, row_blo...]
    dot_general x8 -> x0, matrix products: 48.3 us -> none  [the longest x1 14.8 us: on_device(): lax.dot_general(gate_grad, gate_rows, contract_rows, preferred_element_ty...]
    gather x3 -> x0, local copies, waits for them, and re-layouts: 36.6 us -> none  [the longest x1 14.1 us: on_device(): per_route = returned[target].reshape(shard_tokens, top_count, quarter)]
    reduce_scatter x2 -> x0, waiting for transfers between devices: 32.9 us -> none  [the longest x1 26 us: on_device(): lax.psum_scatter(value_part.astype(jnp.bfloat16), 'cp', scatter_dimension...]
    all_to_all x0 -> x1, blocking collectives: none -> 23.3 us  [swap(): return lax.all_to_all(rows, axis, split_axis=0, concat_axis=0, tiled=True)]
    psum x1 -> x2, waiting for transfers between devices: 80 us -> 99.5 us  [the longest x1 50.9 us: on_device(): later_grad = lax.psum(later_sum, 'cp', axis_index_groups=back)]
    all_to_all x3 -> x4, starting transfers between devices: 26.9 us -> 42.2 us  [swap(): return lax.all_to_all(rows, axis, split_axis=0, concat_axis=0, tiled=True)]
  transfers between devices with their start and end apart: 8 -> 13, of which waited for: 6 -> 5; matrix products, arithmetic and copies ran while one was open for 15% -> 3% of each run, Pallas kernels for 0% -> 19%
where the time goes in v1:
time: 381 us; the launch traced here: 379 us
  waiting for transfers between devices  180 us (47%)
  Pallas kernels  84.8 us (22%)
  starting transfers between devices  49.6 us (13%)
  blocking collectives  23.3 us (6%)
  local copies, waits for them, and re-layouts  21.3 us (6%)
  between operations  14.2 us (4%)
  other arithmetic  6.56 us (2%)
    all_to_all x4, waiting for transfers between devices, swap(): return lax.all_to_all(rows, axis, split_axis=0, concat_axis=0, tiled=True)  72.8 us
    psum x1, waiting for transfers between devices, on_device(): later_grad = lax.psum(later_sum, 'cp', axis_index_groups=back)  50.9 us
    psum x1, waiting for transfers between devices, on_device(): hidden_grad = lax.psum(first_sum, 'cp')  48.6 us
    all_to_all x4, starting transfers between devices, swap(): return lax.all_to_all(rows, axis, split_axis=0, concat_axis=0, tiled=True)  42.2 us
    all_to_all x1, blocking collectives, swap(): return lax.all_to_all(rows, axis, split_axis=0, concat_axis=0, tiled=True)  23.3 us
    pallas_call x2, Pallas kernels, expert_rows(): pl.pallas_call(expert_kernel, grid=(STEPS,), in_specs=[row_block, row_blo...  18.3 us
    pallas_call x2, Pallas kernels, collect_rows(): pl.pallas_call(collect_kernel, grid=(STEPS,), in_specs=[pl.BlockSpec(slot...  15.2 us
    unnamed x38, local copies, waits for them, and re-layouts  13.9 us
  transfers between devices with their start and end apart: 13, of which 5 were waited for; matrix products, arithmetic and copies ran while one was open for 3% of the time, Pallas kernels for 19%

profile of v1, /device:TPU:6, one launch (start us, length us, event | category | flops | bytes accessed | tf_op | source)
XLA Modules:
  0.0 379.4 jit_solution(8752564976070321769)
XLA Ops:
  7.2 3.0 pad_maximum_fusion
  10.2 5.2 %send_rows.2 = bf16[2560,512]{1,0:T(8,128)(2,1)} custom-call(s32[4,512]{1,0:T(4,128)} %bitcast.63, s32[4,512]{1,0:T(4,128)} %bitcast.61, s32[4,512]{1,0:T(4,128)} %bitcast.59, f32[4,512]{1,0:T(4,128)} %bitcast.69, bf16[512,1024]{1,0:T(8,128)(2,1)} %base_ref.1), custom_call_target="tpu_custom_call" | custom-call | flops 1342177280 | bytes 5242880 | tf_op jit(solution)/shard_map/send_rows/pallas_call | solution.py:80
  15.5 12.3 %all-to-all-start = ((bf16[64,40,512]{2,1,0:T(8,128)(2,1)}), bf16[64,40,512]{2,1,0:T(8,128)(2,1)S(1)}, u32[]{:S(2)}, u32[]{:S(2)}) async-start(bf16[64,40,512]{2,1,0:T(8,128)(2,1)} %bitcast.51), calls=%async_computation | async-start | bytes 5242880 | tf_op jit(solution)/shard_map/all_to_all | solution.py:367
  28.0 0.9 copy.67
  28.9 0.9 copy.66
  30.1 2.7 copy.61
  32.8 5.5 %send_rows.3 = bf16[2560,512]{1,0:T(8,128)(2,1)} custom-call(s32[4,512]{1,0:T(4,128)} %bitcast.64, s32[4,512]{1,0:T(4,128)} %bitcast.62, s32[4,512]{1,0:T(4,128)} %bitcast.60, f32[4,512]{1,0:T(4,128)} %bitcast.70, bf16[512,1024]{1,0:T(8,128)(2,1)} %base_ref.1), custom_call_target="tpu_custom_call" | custom-call | flops 1342177280 | bytes 5242880 | tf_op jit(solution)/shard_map/send_rows/pallas_call | solution.py:80
  38.2 0.9 add_select_fusion.1
  39.1 0.9 compare_select_fusion.slots_ref
  40.0 47.6 %all-to-all-done = bf16[64,40,512]{2,1,0:T(8,128)(2,1)S(1)} async-done(((bf16[64,40,512]{2,1,0:T(8,128)(2,1)}), bf16[64,40,512]{2,1,0:T(8,128)(2,1)S(1)}, u32[]{:S(2)}, u32[]{:S(2)}) %all-to-all-start) | async-done | bytes 2621472 | tf_op jit(solution)/shard_map/all_to_all | solution.py:367
  87.7 1.5 copy-done.4
  89.1 5.8 %project_down.2 = bf16[1280,768]{1,0:T(8,128)(2,1)} custom-call(bf16[2560,512]{1,0:T(8,128)(2,1)} %bitcast.48, bf16[1024,768]{1,0:T(8,128)(2,1)} %bitcast.52), custom_call_target="tpu_custom_call" | custom-call | flops 2013265920 | bytes 4587520 | tf_op jit(solution)/shard_map/project_down/pallas_call | solution.py:136
  94.9 8.2 %all-to-all-start.1 = ((bf16[64,40,512]{2,1,0:T(8,128)(2,1)}), bf16[64,40,512]{2,1,0:T(8,128)(2,1)S(1)}, u32[]{:S(2)}, u32[]{:S(2)}) async-start(bf16[64,40,512]{2,1,0:T(8,128)(2,1)} %bitcast.8), calls=%async_computation.1 | async-start | bytes 5242880 | tf_op jit(solution)/shard_map/all_to_all | solution.py:367
  103.3 7.8 %turn_saved.1 = (bf16[1280,768]{1,0:T(8,128)(2,1)}, bf16[1280,768]{1,0:T(8,128)(2,1)}, bf16[1280,768]{1,0:T(8,128)(2,1)}, bf16[1280,768]{1,0:T(8,128)(2,1)}) custom-call(bf16[4,2,192,2560]{3,2,1,0:T(8,128)(2,1)} %bitcast.45), custom_call_target="tpu_custom_call" | custom-call | flops 3932160 | bytes 15728640 | tf_op jit(solution)/shard_map/turn_saved/pallas_call | solution.py:111
  111.1 48.6 %all-reduce.3.cloned.1.call-done.hidden_ref = bf16[1280,768]{1,0:T(8,128)(2,1)} async-done(((bf16[1280,768]{1,0:T(8,128)(2,1)}), bf16[1280,768]{1,0:T(8,128)(2,1)}) %all-reduce.3.cloned.1.call-update) | async-done | bytes 1966096 | tf_op jit(solution)/shard_map/psum | solution.py:425
  159.7 9.1 %expert_rows.2 = bf16[2560,512]{1,0:T(8,128)(2,1)} custom-call(bf16[1280,768]{1,0:T(8,128)(2,1)} %all-reduce.3.cloned.1.call-done.hidden_ref, bf16[1280,768]{1,0:T(8,128)(2,1)} %get-tuple-element.31.gate_ref, bf16[1280,768]{1,0:T(8,128)(2,1)} %get-tuple-element.32.up_ref, bf16[768,1024]{1,0:T(8,128)(2,1)} %bitcast.65, bf16[768,1024]{1,0:T(8,128)(2,1)} %bitcast.67), custom_call_target="tpu_custom_call" | custom-call | flops 128849018880 | bytes 8519680 | tf_op jit(solution)/shard_map/expert_rows/pallas_call | solution.py:172
  168.8 1.5 copy-done.5
  170.3 5.8 %project_down.3 = bf16[1280,768]{1,0:T(8,128)(2,1)} custom-call(bf16[2560,512]{1,0:T(8,128)(2,1)} %bitcast.50, bf16[1024,768]{1,0:T(8,128)(2,1)} %bitcast.53), custom_call_target="tpu_custom_call" | custom-call | flops 2013265920 | bytes 4587520 | tf_op jit(solution)/shard_map/project_down/pallas_call | solution.py:136
  176.2 10.7 %all-to-all-start.3 = ((bf16[64,40,512]{2,1,0:T(8,128)(2,1)}), bf16[64,40,512]{2,1,0:T(8,128)(2,1)S(1)}, u32[]{:S(2)}, u32[]{:S(2)}) async-start(bf16[64,40,512]{2,1,0:T(8,128)(2,1)} %bitcast.49), calls=%async_computation.3 | async-start | bytes 5242880 | tf_op jit(solution)/shard_map/all_to_all | solution.py:367
  186.9 50.9 %all-reduce.5.cloned.1.call-done.hidden_ref = bf16[1280,768]{1,0:T(8,128)(2,1)} async-done(((bf16[1280,768]{1,0:T(8,128)(2,1)}), bf16[1280,768]{1,0:T(8,128)(2,1)}) %all-reduce.5.cloned.1.call-update) | async-done | bytes 1966096 | tf_op jit(solution)/shard_map/psum | solution.py:433
  237.8 9.1 %expert_rows.3 = bf16[2560,512]{1,0:T(8,128)(2,1)} custom-call(bf16[1280,768]{1,0:T(8,128)(2,1)} %all-reduce.5.cloned.1.call-done.hidden_ref, bf16[1280,768]{1,0:T(8,128)(2,1)} %get-tuple-element.36.gate_ref, bf16[1280,768]{1,0:T(8,128)(2,1)} %get-tuple-element.37.up_ref, bf16[768,1024]{1,0:T(8,128)(2,1)} %bitcast.66, bf16[768,1024]{1,0:T(8,128)(2,1)} %bitcast.68), custom_call_target="tpu_custom_call" | custom-call | flops 128849018880 | bytes 8519680 | tf_op jit(solution)/shard_map/expert_rows/pallas_call | solution.py:172
  247.0 1.4 copy-done.1
  248.5 10.9 %all-to-all-start.2 = ((bf16[64,40,512]{2,1,0:T(8,128)(2,1)}), bf16[64,40,512]{2,1,0:T(8,128)(2,1)}, u32[]{:S(2)}, u32[]{:S(2)}) async-start(bf16[64,40,512]{2,1,0:T(8,128)(2,1)} %bitcast.47), calls=%async_computation.2 | async-start | bytes 5242880 | tf_op jit(solution)/shard_map/all_to_all | solution.py:367
  259.4 1.2 constant_dynamic-slice_fusion.5
  260.6 0.9 collective-permute-start.2
  261.5 1.2 collective-permute-start
  262.7 1.5 collective-permute-start.1
  264.5 0.7 gt.20
  265.2 1.2 fusion.1.seen_ref
  266.6 1.0 bitcast_dynamic-update-slice_fusion.3
  267.6 0.7 constant_dynamic-slice_fusion.3.v_ref
  268.3 0.8 copy.76
  269.1 7.3 %collective-permute-done = bf16[128,1024]{1,0:T(8,128)(2,1)S(1)} collective-permute-done((bf16[128,1024]{1,0:T(8,128)(2,1)S(1)}, bf16[128,1024]{1,0:T(8,128)(2,1)S(1)}, u32[]{:S(2)}, u32[]{:S(2)}) %collective-permute-start) | collective-permute-done | bytes 262176 | tf_op jit(solution)/shard_map/ppermute | solution.py:351
  276.5 1.0 copy-done.2
  277.5 8.8 %attention_probs.1.probs_ref = f32[8,512,512]{2,1,0:T(8,128)} custom-call(bf16[512,1024]{1,0:T(8,128)(2,1)} %bitcast.43, bf16[512,128]{1,0:T(8,128)(2,1)} %copy-done.6, f32[512,512]{1,0:T(8,128)} %fusion.1.seen_ref), custom_call_target="tpu_custom_call" | custom-call | flops 536870912 | bytes 8388608 | tf_op jit(solution)/shard_map/attention_probs/pallas_call | solution.py:251
  286.3 7.6 %collect_rows.2.base_ref = f32[512,1024]{1,0:T(8,128)} custom-call(s32[512,4]{1,0:T(8,128)} %compare_select_fusion.slots_ref, bf16[2560,512]{1,0:T(8,128)(2,1)} %bitcast.42, bf16[512,1024]{1,0:T(8,128)(2,1)} %base_ref.1), custom_call_target="tpu_custom_call" | custom-call | flops 1342177280 | bytes 6815744 | tf_op jit(solution)/shard_map/collect_rows/pallas_call | solution.py:214
  293.9 25.2 %all-to-all-done.2 = bf16[64,40,512]{2,1,0:T(8,128)(2,1)} async-done(((bf16[64,40,512]{2,1,0:T(8,128)(2,1)}), bf16[64,40,512]{2,1,0:T(8,128)(2,1)}, u32[]{:S(2)}, u32[]{:S(2)}) %all-to-all-start.2) | async-done | bytes 2621472 | tf_op jit(solution)/shard_map/all_to_all | solution.py:367
  319.2 7.6 %collect_rows.3.grad_ref = bf16[512,1024]{1,0:T(8,128)(2,1)} custom-call(s32[512,4]{1,0:T(8,128)} %get-tuple-element.42.slots_ref, bf16[2560,512]{1,0:T(8,128)(2,1)} %bitcast.14.rows_ref, f32[512,1024]{1,0:T(8,128)} %collect_rows.2.base_ref), custom_call_target="tpu_custom_call" | custom-call | flops 1342177280 | bytes 6815744 | tf_op jit(solution)/shard_map/collect_rows/pallas_call | solution.py:214
  326.9 1.3 constant_dynamic-slice_fusion
  328.2 0.4 collective-permute-start.3
  328.5 3.0 collective-permute-start.5
  331.8 12.3 %attention_grads.1 = bf16[512,1280]{1,0:T(8,128)(2,1)} custom-call(f32[8,512,512]{2,1,0:T(8,128)} %attention_probs.1.probs_ref, bf16[512,1024]{1,0:T(8,128)(2,1)} %collect_rows.3.grad_ref, bf16[512,1024]{1,0:T(8,128)(2,1)} %bitcast.44, bf16[512,128]{1,0:T(8,128)(2,1)} %constant_dynamic-slice_fusion.3.v_ref, bf16[128,512]{1,0:T(8,128)(2,1)} %bitcast.56), custom_call_target="tpu_custom_call" | custom-call | flops 2147483648 | bytes 8388608 | tf_op jit(solution)/shard_map/attention_grads/pallas_call | solution.py:311
  344.2 1.6 copy-done.3
  345.8 23.3 %all_to_all.25 = bf16[4,128,1280]{2,1,0:T(8,128)(2,1)S(1)} all-to-all(bf16[4,128,1280]{2,1,0:T(8,128)(2,1)S(1)} %bitcast.46), channel_id=1, replica_groups=mesh['ep'=64,'cp'=4] {'cp'}, dimensions={0} | all-to-all | bytes 2621440 | tf_op jit(solution)/shard_map/all_to_all | solution.py:367
  369.2 1.1 copy.134
  370.4 0.5 reduce
  371.2 0.7 copy.75
  372.1 0.7 copy.74
  (63 shorter events, 2.4 us)
Async XLA Ops:
  7.2 259.3 %copy-start = (bf16[512,256]{1,0:T(8,128)(2,1)S(1)}, bf16[512,256]{1,0:T(8,128)(2,1)}, u32[]{:S(2)}) copy-start(bf16[512,256]{1,0:T(8,128)(2,1)} %param.25) | copy-start | bytes 786436
  7.2 96.1 %all-gather.3.cloned.1.call-start = ((), (), s32[]{:S(2)}) async-start(), calls=%async_computation.7 | async-start | bytes 9830400 | tf_op jit(solution)/shard_map/all_gather | solution.py:400
  15.5 12.4 %copy-start.11 = (s32[512,4]{0,1:T(4,128)S(1)}, s32[512,4]{0,1:T(4,128)}, u32[]{:S(2)}) copy-start(s32[512,4]{0,1:T(4,128)} %param.17) | copy-start | bytes 24580
  15.5 12.5 %copy-start.13 = (s32[512,4]{0,1:T(4,128)S(1)}, s32[512,4]{0,1:T(4,128)}, u32[]{:S(2)}) copy-start(s32[512,4]{0,1:T(4,128)} %param.15) | copy-start | bytes 24580
  15.5 13.4 %copy-start.12 = (s32[512,4]{0,1:T(4,128)S(1)}, s32[512,4]{0,1:T(4,128)}, u32[]{:S(2)}) copy-start(s32[512,4]{0,1:T(4,128)} %param.16) | copy-start | bytes 24580
  15.5 72.2 %all-to-all-start = ((bf16[64,40,512]{2,1,0:T(8,128)(2,1)}), bf16[64,40,512]{2,1,0:T(8,128)(2,1)S(1)}, u32[]{:S(2)}, u32[]{:S(2)}) async-start(bf16[64,40,512]{2,1,0:T(8,128)(2,1)} %bitcast.51), calls=%async_computation | async-start | bytes 5242880 | tf_op jit(solution)/shard_map/all_to_all | solution.py:367
  27.8 131.9 %all-reduce.3.cloned.1.call-start = ((), (), s32[]{:S(2)}) async-start(), calls=%async_computation.5 | async-start | bytes 3932160 | tf_op jit(solution)/shard_map/psum | solution.py:425
  32.7 5.5 %copy-start.7 = (s32[512,4]{1,0:T(8,128)S(1)}, s32[512,4]{1,0:T(8,128)}, u32[]{:S(2)}) copy-start(s32[512,4]{1,0:T(8,128)} %copy.67) | copy-start | bytes 24580
  32.8 5.5 %copy-start.8 = (s32[512,4]{1,0:T(8,128)S(1)}, s32[512,4]{1,0:T(8,128)}, u32[]{:S(2)}) copy-start(s32[512,4]{1,0:T(8,128)} %copy.66) | copy-start | bytes 24580
  87.6 1.5 copy-start.4
  94.9 73.8 %all-to-all-start.1 = ((bf16[64,40,512]{2,1,0:T(8,128)(2,1)}), bf16[64,40,512]{2,1,0:T(8,128)(2,1)S(1)}, u32[]{:S(2)}, u32[]{:S(2)}) async-start(bf16[64,40,512]{2,1,0:T(8,128)(2,1)} %bitcast.8), calls=%async_computation.1 | async-start | bytes 5242880 | tf_op jit(solution)/shard_map/all_to_all | solution.py:367
  103.2 134.6 %all-reduce.5.cloned.1.call-start = ((), (), s32[]{:S(2)}) async-start(), calls=%async_computation.6 | async-start | bytes 3932160 | tf_op jit(solution)/shard_map/psum | solution.py:433
  168.8 1.5 copy-start.5
  176.2 70.8 %all-to-all-start.3 = ((bf16[64,40,512]{2,1,0:T(8,128)(2,1)}), bf16[64,40,512]{2,1,0:T(8,128)(2,1)S(1)}, u32[]{:S(2)}, u32[]{:S(2)}) async-start(bf16[64,40,512]{2,1,0:T(8,128)(2,1)} %bitcast.49), calls=%async_computation.3 | async-start | bytes 5242880 | tf_op jit(solution)/shard_map/all_to_all | solution.py:367
  247.0 1.5 copy-start.1
  247.0 17.2 %copy-start.14 = (s32[1,8,8]{2,1,0:T(8,128)S(1)}, s32[1,8,8]{2,1,0:T(8,128)}, u32[]{:S(2)}) copy-start(s32[1,8,8]{2,1,0:T(8,128)} %param.27) | copy-start | bytes 772
  248.5 70.7 %all-to-all-start.2 = ((bf16[64,40,512]{2,1,0:T(8,128)(2,1)}), bf16[64,40,512]{2,1,0:T(8,128)(2,1)}, u32[]{:S(2)}, u32[]{:S(2)}) async-start(bf16[64,40,512]{2,1,0:T(8,128)(2,1)} %bitcast.47), calls=%async_computation.2 | async-start | bytes 5242880 | tf_op jit(solution)/shard_map/all_to_all | solution.py:367
  260.6 15.9 %collective-permute-start.2 = (bf16[128,1024]{1,0:T(8,128)(2,1)S(1)}, bf16[128,1024]{1,0:T(8,128)(2,1)S(1)}, u32[]{:S(2)}, u32[]{:S(2)}) collective-permute-start(bf16[128,1024]{1,0:T(8,128)(2,1)S(1)} %get-tuple-element.66), channel_id=1, source_target_pairs={{0,3},{1,0},{2,1},{3,2},{4,7},{5,4},{6,5},{7,6},{8,11},{9,8},{10,9... | collective-permute-start | bytes 786440 | tf_op jit(solution)/shard_map/ppermute | solution.py:351
  261.5 14.9 %collective-permute-start = (bf16[128,1024]{1,0:T(8,128)(2,1)S(1)}, bf16[128,1024]{1,0:T(8,128)(2,1)S(1)}, u32[]{:S(2)}, u32[]{:S(2)}) collective-permute-start(bf16[128,1024]{1,0:T(8,128)(2,1)S(1)} %get-tuple-element.67), channel_id=1, source_target_pairs={{0,1},{1,2},{2,3},{3,0},{4,5},{5,6},{6,7},{7,4},{8,9},{9,10},{10,1... | collective-permute-start | bytes 786440 | tf_op jit(solution)/shard_map/ppermute | solution.py:351
  262.7 13.7 %collective-permute-start.1 = (bf16[128,1024]{1,0:T(8,128)(2,1)S(1)}, bf16[128,1024]{1,0:T(8,128)(2,1)S(1)}, u32[]{:S(2)}, u32[]{:S(2)}) collective-permute-start(bf16[128,1024]{1,0:T(8,128)(2,1)S(1)} %get-tuple-element.68), channel_id=1, source_target_pairs={{0,2},{1,3},{2,0},{3,1},{4,6},{5,7},{6,4},{7,5},{8,10},{9,11},{10,... | collective-permute-start | bytes 786440 | tf_op jit(solution)/shard_map/ppermute | solution.py:351
  264.5 3.1 copy-start.10
  266.5 10.0 %copy-start.6 = (bf16[512,128]{1,0:T(8,128)(2,1)}, bf16[512,128]{1,0:T(8,128)(2,1)S(1)}, u32[]{:S(2)}) copy-start(bf16[512,128]{1,0:T(8,128)(2,1)S(1)} %constant_dynamic-slice_fusion.4.k_ref) | copy-start | bytes 393220
  276.5 1.0 copy-start.2
  328.2 15.9 %collective-permute-start.3 = (bf16[128,1024]{1,0:T(8,128)(2,1)S(1)}, bf16[128,1024]{1,0:T(8,128)(2,1)S(1)}, u32[]{:S(2)}, u32[]{:S(2)}) collective-permute-start(bf16[128,1024]{1,0:T(8,128)(2,1)S(1)} %get-tuple-element.64), channel_id=1, source_target_pairs={{0,1},{1,2},{2,3},{3,0},{4,5},{5,6},{6,7},{7,4},{8,9},{9,10},{10,1... | collective-permute-start | bytes 786440 | tf_op jit(solution)/shard_map/ppermute | solution.py:338
  328.5 15.7 %collective-permute-start.5 = (bf16[128,1024]{1,0:T(8,128)(2,1)S(1)}, bf16[128,1024]{1,0:T(8,128)(2,1)S(1)}, u32[]{:S(2)}, u32[]{:S(2)}) collective-permute-start(bf16[128,1024]{1,0:T(8,128)(2,1)S(1)} %get-tuple-element.62), channel_id=1, source_target_pairs={{0,3},{1,0},{2,1},{3,2},{4,7},{5,4},{6,5},{7,6},{8,11},{9,8},{10,9... | collective-permute-start | bytes 786440 | tf_op jit(solution)/shard_map/ppermute | solution.py:338
  331.5 12.7 %collective-permute-start.4 = (bf16[128,1024]{1,0:T(8,128)(2,1)S(1)}, bf16[128,1024]{1,0:T(8,128)(2,1)S(1)}, u32[]{:S(2)}, u32[]{:S(2)}) collective-permute-start(bf16[128,1024]{1,0:T(8,128)(2,1)S(1)} %get-tuple-element.63), channel_id=1, source_target_pairs={{0,2},{1,3},{2,0},{3,1},{4,6},{5,7},{6,4},{7,5},{8,10},{9,11},{10,... | collective-permute-start | bytes 786440 | tf_op jit(solution)/shard_map/ppermute | solution.py:338
  344.1 1.7 copy-start.3
  344.2 25.0 %copy-start.9 = (bf16[128,4096]{1,0:T(8,128)(2,1)}, bf16[128,4096]{1,0:T(8,128)(2,1)S(1)}, u32[]{:S(2)}) copy-start(bf16[128,4096]{1,0:T(8,128)(2,1)S(1)} %constant_dynamic-update-slice_fusion.2) | copy-start | bytes 3145732
Sparse Core Ops, SparseCore 0:
  10.3 84.2 all-gather.2
  97.0 62.6 all-reduce.2
  176.3 61.5 all-reduce.4

commit v2 on v1

--- a/solution.py
+++ b/solution.py
@@ -11,14 +11,22 @@
 LANES = 128
 PARTS = 2
 STEPS = 4
-VMEM_LIMIT = 60 * 1024 * 1024
+CHOSEN_STEPS = 2
+DOWN_STEPS = 3
+LAST_SHARE = 4
+VMEM_LIMIT = 56 * 1024 * 1024
+SMALL_VMEM = 24 * 1024 * 1024
 
 f32 = jnp.float32
 bf16 = jnp.bfloat16
 
 
-def params():
-    return pltpu.CompilerParams(vmem_limit_bytes=VMEM_LIMIT)
+def params(limit=VMEM_LIMIT):
+    return pltpu.CompilerParams(vmem_limit_bytes=limit)
+
+
+def stay(*arrays):
+    return [pltpu.with_memory_space_constraint(a, pltpu.HBM) for a in arrays]
 
 
 def cost(flops, moved, exps=0):
@@ -82,12 +90,12 @@
         grid=(STEPS,),
         in_specs=[routes] * 4 + [pl.BlockSpec(grad.shape, lambda i: (0, 0))],
         out_specs=pl.BlockSpec((2 * step, half), lambda i: (i, 0)),
-        out_shape=jax.ShapeDtypeStruct((2 * rows, half), bf16),
+        out_shape=pltpu.HBM((2 * rows, half), bf16),
         scratch_shapes=[woven(step, half)],
         compiler_params=params(),
         cost_estimate=cost(2 * rows * tokens * width, 4 * rows * width),
         name="send_rows",
-    )(ids, spare, slots, probs, grad)
+    )(ids, spare, slots, probs, *stay(grad))
 
 
 def turn_kernel(share, saved_ref, *refs):
@@ -121,6 +129,25 @@
     )(saved)
 
 
+def turn_kernel_2d(in_ref, out_ref):
+    out_ref[...] = in_ref[...].astype(f32).T.astype(bf16)
+
+
+def turn_weights(weights):
+    hidden, width = weights.shape
+    step = hidden // DOWN_STEPS
+    return pl.pallas_call(
+        turn_kernel_2d,
+        grid=(DOWN_STEPS,),
+        in_specs=[pl.BlockSpec((step, width), lambda i: (i, 0))],
+        out_specs=pl.BlockSpec((width, step), lambda i: (0, i)),
+        out_shape=pltpu.HBM((width, hidden), bf16),
+        compiler_params=params(SMALL_VMEM),
+        cost_estimate=cost(weights.size, 4 * weights.size),
+        name="turn_weights",
+    )(*stay(weights))
+
+
 def down_rows_kernel(rows_ref, down_ref, out_ref, wide):
     half = rows_ref.shape[1]
     low, high = unweave(rows_ref, wide)
@@ -141,16 +168,16 @@
             pl.BlockSpec(down_t.shape, lambda i: (0, 0)),
         ],
         out_specs=pl.BlockSpec((step, hidden), lambda i: (i, 0)),
-        out_shape=jax.ShapeDtypeStruct((rows, hidden), bf16),
+        out_shape=pltpu.HBM((rows, hidden), bf16),
         scratch_shapes=[woven(step, half)],
-        compiler_params=params(),
+        compiler_params=params(SMALL_VMEM),
         cost_estimate=cost(2 * rows * width * hidden, 2 * rows * (width + hidden)),
         name="project_down",
-    )(arrived, down_t)
-
-
-def expert_kernel(hidden_ref, gate_ref, up_ref, wg_ref, wu_ref, out_ref, wide):
-    rows, half = hidden_ref.shape[0], out_ref.shape[1]
+    )(arrived, *stay(down_t))
+
+
+def expert_kernel(hidden_ref, gate_ref, up_ref, wg_ref, wu_ref, *refs):
+    outs, wides = refs[: len(refs) // 2], refs[len(refs) // 2 :]
     grad = hidden_ref[...].astype(f32)
     gate = gate_ref[...].astype(f32)
     up = up_ref[...].astype(f32)
@@ -160,22 +187,26 @@
     up_grad = (shared * gate).astype(bf16)
     total = jnp.dot(gate_grad, wg_ref[...], preferred_element_type=f32)
     total = total + jnp.dot(up_grad, wu_ref[...], preferred_element_type=f32)
-    weave(out_ref, wide, total[:, :half], total[:, half:])
-
-
-def expert_rows(hidden_grad, gate, up, w_gate, w_up):
+    start = 0
+    for out_ref, wide in zip(outs, wides):
+        half = out_ref.shape[1]
+        low, high = total[:, start : start + half], total[:, start + half : start + 2 * half]
+        weave(out_ref, wide, low, high)
+        start += 2 * half
+
+
+def expert_rows(hidden_grad, gate, up, w_gate, w_up, widths):
     rows, hidden = hidden_grad.shape
-    width = w_gate.shape[1]
-    step, half = rows // STEPS, width // 2
+    step, width = rows // STEPS, sum(widths)
     row_block = pl.BlockSpec((step, hidden), lambda i: (i, 0))
     whole = pl.BlockSpec(w_gate.shape, lambda i: (0, 0))
     return pl.pallas_call(
         expert_kernel,
         grid=(STEPS,),
         in_specs=[row_block, row_block, row_block, whole, whole],
-        out_specs=pl.BlockSpec((2 * step, half), lambda i: (i, 0)),
-        out_shape=jax.ShapeDtypeStruct((2 * rows, half), bf16),
-        scratch_shapes=[woven(step, half)],
+        out_specs=[pl.BlockSpec((2 * step, w // 2), lambda i: (i, 0)) for w in widths],
+        out_shape=[jax.ShapeDtypeStruct((2 * rows, w // 2), bf16) for w in widths],
+        scratch_shapes=[woven(step, w // 2) for w in widths],
         compiler_params=params(),
         cost_estimate=cost(
             128 * rows * hidden * width, 2 * rows * (3 * hidden + width), rows * hidden
@@ -184,48 +215,67 @@
     )(hidden_grad, gate, up, w_gate, w_up)
 
 
-def collect_kernel(slots_ref, rows_ref, base_ref, out_ref, total, wide):
+def chosen_kernel(slots_ref, out_ref):
+    tokens, rows = out_ref.shape
+    row = lax.broadcasted_iota(jnp.int32, (tokens, rows), 1) + pl.program_id(0) * rows
+    chosen = jnp.zeros((tokens, rows), f32)
+    for k in range(slots_ref.shape[1]):
+        chosen = jnp.where(slots_ref[:, k : k + 1] == row, 1.0, chosen)
+    out_ref[...] = chosen.astype(bf16)
+
+
+def chosen_rows(slots, rows):
+    tokens = slots.shape[0]
+    step = rows // CHOSEN_STEPS
+    return pl.pallas_call(
+        chosen_kernel,
+        grid=(CHOSEN_STEPS,),
+        in_specs=[pl.BlockSpec(slots.shape, lambda i: (0, 0))],
+        out_specs=pl.BlockSpec((tokens, step), lambda i: (0, i)),
+        out_shape=pltpu.HBM((tokens, rows), bf16),
+        compiler_params=params(SMALL_VMEM),
+        cost_estimate=cost(8 * tokens * rows, 2 * tokens * rows),
+        name="chosen_rows",
+    )(slots)
+
+
+def collect_kernel(chosen_ref, rows_ref, base_ref, out_ref, total, wide):
     step = pl.program_id(0)
-    tokens = slots_ref.shape[0]
-    rows, half = rows_ref.shape[0] // 2, rows_ref.shape[1]
+    half = rows_ref.shape[1]
 
     @pl.when(step == 0)
     def _():
         total[...] = base_ref[...].astype(f32)
 
-    row = lax.broadcasted_iota(jnp.int32, (tokens, rows), 1) + step * rows
-    chosen = jnp.zeros((tokens, rows), f32)
-    for k in range(slots_ref.shape[1]):
-        chosen = jnp.where(slots_ref[:, k : k + 1] == row, 1.0, chosen)
-    chosen = chosen.astype(bf16)
     low, high = unweave(rows_ref, wide)
-    total[:, :half] += jnp.dot(chosen, low, preferred_element_type=f32)
-    total[:, half:] += jnp.dot(chosen, high, preferred_element_type=f32)
-
-    @pl.when(step == STEPS - 1)
+    total[:, :half] += jnp.dot(chosen_ref[...], low, preferred_element_type=f32)
+    total[:, half:] += jnp.dot(chosen_ref[...], high, preferred_element_type=f32)
+
+    @pl.when(step == CHOSEN_STEPS - 1)
     def _():
         out_ref[...] = total[...].astype(out_ref.dtype)
 
 
-def collect_rows(slots, returned, base, out_dtype):
-    tokens, width = base.shape
+def collect_rows(chosen, returned, base, start, out_dtype):
     rows, half = returned.shape[0] // 2, returned.shape[1]
-    step = rows // STEPS
+    tokens, width = base.shape[0], 2 * half
+    step, column = rows // CHOSEN_STEPS, start // width
+    assert column * width == start
     return pl.pallas_call(
         collect_kernel,
-        grid=(STEPS,),
+        grid=(CHOSEN_STEPS,),
         in_specs=[
-            pl.BlockSpec(slots.shape, lambda i: (0, 0)),
+            pl.BlockSpec((tokens, step), lambda i: (0, i)),
             pl.BlockSpec((2 * step, half), lambda i: (i, 0)),
-            pl.BlockSpec(base.shape, lambda i: (0, 0)),
+            pl.BlockSpec((tokens, width), lambda i: (0, column)),
         ],
-        out_specs=pl.BlockSpec(base.shape, lambda i: (0, 0)),
-        out_shape=jax.ShapeDtypeStruct(base.shape, out_dtype),
+        out_specs=pl.BlockSpec((tokens, width), lambda i: (0, 0)),
+        out_shape=jax.ShapeDtypeStruct((tokens, width), out_dtype),
         scratch_shapes=[pltpu.VMEM((tokens, width), f32), woven(step, half)],
-        compiler_params=params(),
+        compiler_params=params(SMALL_VMEM),
         cost_estimate=cost(2 * rows * tokens * width, 2 * rows * width + 8 * tokens * width),
         name="collect_rows",
-    )(slots, returned, base)
+    )(*stay(chosen), returned, *stay(base))
 
 
 def probs_kernel(q_ref, k_ref, seen_ref, out_ref):
@@ -257,8 +307,8 @@
             pl.BlockSpec(seen.shape, lambda h: (0, 0)),
         ],
         out_specs=pl.BlockSpec((1, length, length), lambda h: (h, 0, 0)),
-        out_shape=jax.ShapeDtypeStruct((heads, length, length), f32),
-        compiler_params=params(),
+        out_shape=pltpu.HBM((heads, length, length), f32),
+        compiler_params=params(SMALL_VMEM),
         cost_estimate=cost(
             2 * heads * length * length * HEAD_DIM,
             4 * heads * length * length,
@@ -268,89 +318,181 @@
     )(queries, keys, seen)
 
 
-def grads_kernel(heads, probs_ref, grad_ref, q_ref, v_ref, kt_ref, out_ref, sum_k, sum_v):
-    head = pl.program_id(0)
+def head_grads(probs_ref, grad_ref, q_ref, v_ref, kt_ref, out_ref, sum_k, sum_v):
     length = q_ref.shape[0]
     block = length // 2
     scale = HEAD_DIM ** (-0.5)
-
-    @pl.when(head == 0)
+    for part in range(2):
+        keys = (part + 1) * block
+        cols = slice(part * block, (part + 1) * block)
+        probs = probs_ref[0, :keys, cols]
+        grad = grad_ref[cols, :]
+        prob_grad = lax.dot_general(
+            v_ref[:keys, :], grad, (((1,), (1,)), ((), ())), preferred_element_type=f32
+        )
+        row_total = jnp.sum(probs * prob_grad, axis=0, keepdims=True)
+        score_grad = (probs * (prob_grad - row_total)).astype(bf16)
+        query_grad = jnp.dot(kt_ref[:, :keys], score_grad, preferred_element_type=f32) * scale
+        out_ref[cols, :] = query_grad.T.astype(bf16)
+        sum_k[:keys, :] += jnp.dot(score_grad, q_ref[cols, :], preferred_element_type=f32)
+        sum_v[:keys, :] += jnp.dot(probs.astype(bf16), grad, preferred_element_type=f32)
+
+
+def first_grads_kernel(probs_ref, grad_ref, q_ref, v_ref, kt_ref, out_ref, sum_k, sum_v):
+    @pl.when(pl.program_id(0) == 0)
     def _():
         sum_k[...] = jnp.zeros_like(sum_k)
         sum_v[...] = jnp.zeros_like(sum_v)
 
-    @pl.when(head < heads)
+    head_grads(probs_ref, grad_ref, q_ref, v_ref, kt_ref, out_ref, sum_k, sum_v)
+
+
+def last_grads_kernel(
+    probs_ref, grad_ref, q_ref, v_ref, kt_ref, old_k, old_v, out_ref, sum_k, sum_v
+):
+    head, heads = pl.program_id(0), pl.num_programs(0)
+    scale = HEAD_DIM ** (-0.5)
+
+    @pl.when(head == 0)
     def _():
-        for part in range(2):
-            keys = (part + 1) * block
-            cols = slice(part * block, (part + 1) * block)
-            probs = probs_ref[0, :keys, cols]
-            grad = grad_ref[cols, :]
-            prob_grad = lax.dot_general(
-                v_ref[:keys, :], grad, (((1,), (1,)), ((), ())), preferred_element_type=f32
-            )
-            row_total = jnp.sum(probs * prob_grad, axis=0, keepdims=True)
-            score_grad = (probs * (prob_grad - row_total)).astype(bf16)
-            query_grad = jnp.dot(kt_ref[:, :keys], score_grad, preferred_element_type=f32) * scale
-            out_ref[cols, :] = query_grad.T.astype(bf16)
-            sum_k[:keys, :] += jnp.dot(score_grad, q_ref[cols, :], preferred_element_type=f32)
-            sum_v[:keys, :] += jnp.dot(probs.astype(bf16), grad, preferred_element_type=f32)
-
-    @pl.when(head == heads)
+        sum_k[...] = old_k[...]
+        sum_v[...] = old_v[...]
+
+    first = pl.multiple_of((head + 2) * HEAD_DIM, HEAD_DIM)
+    out_ref[:, pl.ds(first, HEAD_DIM)] = grad_ref[...]
+    first = pl.multiple_of((head + heads + 2) * HEAD_DIM, HEAD_DIM)
+    out = out_ref.at[:, pl.ds(first, HEAD_DIM)]
+    head_grads(probs_ref, grad_ref, q_ref, v_ref, kt_ref, out, sum_k, sum_v)
+
+    @pl.when(head == heads - 1)
     def _():
-        out_ref[...] = (sum_k[...] * scale).astype(bf16)
-
-    @pl.when(head == heads + 1)
-    def _():
-        out_ref[...] = sum_v[...].astype(bf16)
-
-
-def attention_grads(probs, out_grad, queries, values, keys_t):
-    heads, length, _ = probs.shape
-    head_cols = pl.BlockSpec((length, HEAD_DIM), lambda h: (0, jnp.minimum(h, heads - 1)))
-    return pl.pallas_call(
-        functools.partial(grads_kernel, heads),
-        grid=(heads + 2,),
-        in_specs=[
-            pl.BlockSpec((1, length, length), lambda h: (jnp.minimum(h, heads - 1), 0, 0)),
-            head_cols,
-            head_cols,
-            pl.BlockSpec((length, HEAD_DIM), lambda h: (0, 0)),
-            pl.BlockSpec(keys_t.shape, lambda h: (0, 0)),
-        ],
-        out_specs=pl.BlockSpec((length, HEAD_DIM), lambda h: (0, h)),
-        out_shape=jax.ShapeDtypeStruct((length, (heads + 2) * HEAD_DIM), bf16),
-        scratch_shapes=[pltpu.VMEM((length, HEAD_DIM), f32), pltpu.VMEM((length, HEAD_DIM), f32)],
-        compiler_params=params(),
-        cost_estimate=cost(8 * heads * length * length * HEAD_DIM, 4 * heads * length * length),
-        name="attention_grads",
-    )(probs, out_grad, queries, values, keys_t)
-
-
-def to_rows(grads):
+        out_ref[:, :HEAD_DIM] = (sum_k[...] * scale).astype(bf16)
+        out_ref[:, HEAD_DIM : 2 * HEAD_DIM] = sum_v[...].astype(bf16)
+
+
+def attention_grads(probs, out_grad, queries, values, keys_t, first, sums=None):
+    length, heads = out_grad.shape[0], out_grad.shape[1] // HEAD_DIM
+    whole = pl.BlockSpec((length, HEAD_DIM), lambda h: (0, 0))
+    totals = [jax.ShapeDtypeStruct((length, HEAD_DIM), f32)] * 2
+    out_spec = pl.BlockSpec((length, HEAD_DIM), lambda h: (0, h))
+    in_specs = [
+        pl.BlockSpec((1, length, length), lambda h: (first + h, 0, 0)),
+        out_spec,
+        pl.BlockSpec((length, HEAD_DIM), lambda h: (0, first + h)),
+        whole,
+        pl.BlockSpec(keys_t.shape, lambda h: (0, 0)),
+    ]
+    estimate = cost(8 * heads * length * length * HEAD_DIM, 4 * heads * length * length)
+    operands = (*stay(probs), out_grad, *stay(queries), values, keys_t)
+    if sums is None:
+        return pl.pallas_call(
+            first_grads_kernel,
+            grid=(heads,),
+            in_specs=in_specs,
+            out_specs=[out_spec, whole, whole],
+            out_shape=[jax.ShapeDtypeStruct(out_grad.shape, bf16)] + totals,
+            compiler_params=params(SMALL_VMEM),
+            cost_estimate=estimate,
+            name="first_grads",
+        )(*operands)
+    columns = (2 * heads + 2) * HEAD_DIM
+    return pl.pallas_call(
+        last_grads_kernel,
+        grid=(heads,),
+        in_specs=in_specs + [whole, whole],
+        out_specs=pl.BlockSpec((length, columns), lambda h: (0, 0)),
+        out_shape=jax.ShapeDtypeStruct((length, columns), bf16),
+        scratch_shapes=[pltpu.VMEM((length, HEAD_DIM), f32)] * 2,
+        compiler_params=params(SMALL_VMEM),
+        cost_estimate=estimate,
+        name="last_grads",
+    )(*operands, *sums)
+
+
+def pass_round(pieces):
     parts = lax.axis_size("cp")
     me = lax.axis_index("cp")
-    rows, width = grads.shape[0] // parts, grads.shape[1]
-    out = jnp.zeros((rows, parts * width), grads.dtype)
+    got = []
     for shift in range(parts):
-        piece = lax.dynamic_slice_in_dim(grads, ((me + shift) % parts) * rows, rows, 0)
+        piece = pieces((me + shift) % parts)
         if shift:
             piece = lax.ppermute(piece, "cp", [(i, (i + shift) % parts) for i in range(parts)])
-        out = lax.dynamic_update_slice(out, piece, (0, ((me - shift) % parts) * width))
-    return out
+        got.append((piece, (me - shift) % parts))
+    return got
 
 
 def to_heads(queries):
     parts = lax.axis_size("cp")
-    me = lax.axis_index("cp")
     rows, width = queries.shape[0], queries.shape[1] // parts
-    out = jnp.zeros((parts, rows, width), queries.dtype)
-    for shift in range(parts):
-        piece = lax.dynamic_slice_in_dim(queries, ((me + shift) % parts) * width, width, 1)
-        if shift:
-            piece = lax.ppermute(piece, "cp", [(i, (i + shift) % parts) for i in range(parts)])
-        out = lax.dynamic_update_slice(out, piece[None], ((me - shift) % parts, 0, 0))
-    return out.reshape(parts * rows, width)
+    out = jnp.zeros((parts * rows, width), queries.dtype)
+    for piece, i in pass_round(lambda i: lax.dynamic_slice_in_dim(queries, i * width, width, 1)):
+        out = lax.dynamic_update_slice(out, piece, (i * rows, 0))
+    return out
+
+
+def to_rows(grads):
+    rows = grads.shape[0] // lax.axis_size("cp")
+    return pass_round(lambda i: lax.dynamic_slice_in_dim(grads, i * rows, rows, 0))
+
+
+def join_rows(pieces, most, width):
+    rows = pieces[0][0].shape[0]
+    out = jnp.zeros((rows, len(pieces) * width), bf16)
+    for piece, i in pieces:
+        out = lax.dynamic_update_slice(out, piece, (0, i * width))
+    return out
+
+
+def finish_kernel(last, together, got_ref, *refs):
+    grad_ref, query_ref, key_ref, value_ref, sum_k, sum_v = refs[2:]
+    place = pl.program_id(0) % together
+    key = got_ref[0, :, :HEAD_DIM].astype(f32)
+    value = got_ref[0, :, HEAD_DIM : 2 * HEAD_DIM].astype(f32)
+    grad_ref[...] = got_ref[0, :, 2 * HEAD_DIM : 2 * HEAD_DIM + last]
+    query_ref[...] = got_ref[0, :, 2 * HEAD_DIM + last :]
+
+    @pl.when(place == 0)
+    def _():
+        sum_k[...] = key
+        sum_v[...] = value
+
+    @pl.when(place > 0)
+    def _():
+        sum_k[...] += key
+        sum_v[...] += value
+
+    key_ref[...] = sum_k[...].astype(bf16)
+    value_ref[...] = sum_v[...].astype(bf16)
+
+
+def finish(got, grad_hidden, grad_query, together):
+    parts, rows, columns = got.shape
+    last = (columns - 2 * HEAD_DIM) // 2
+    ratio = grad_hidden.shape[1] // parts // last
+    rest = pl.BlockSpec((rows, last), lambda i: (0, i * ratio + ratio - 1))
+    sums = pl.BlockSpec((rows, HEAD_DIM), lambda i: (0, i // together))
+    sums_shape = jax.ShapeDtypeStruct((rows, parts // together * HEAD_DIM), bf16)
+    return pl.pallas_call(
+        functools.partial(finish_kernel, last, together),
+        grid=(parts,),
+        in_specs=[
+            pl.BlockSpec((1, rows, columns), lambda i: (i, 0, 0)),
+            pl.BlockSpec(memory_space=pl.ANY),
+            pl.BlockSpec(memory_space=pl.ANY),
+        ],
+        out_specs=[rest, rest, sums, sums],
+        out_shape=[
+            jax.ShapeDtypeStruct(grad_hidden.shape, bf16),
+            jax.ShapeDtypeStruct(grad_query.shape, bf16),
+            sums_shape,
+            sums_shape,
+        ],
+        input_output_aliases={1: 0, 2: 1},
+        scratch_shapes=[pltpu.VMEM((rows, HEAD_DIM), f32)] * 2,
+        compiler_params=params(SMALL_VMEM),
+        cost_estimate=cost(4 * got.size, 4 * got.size),
+        name="finish",
+    )(got, grad_hidden, grad_query)
 
 
 def seen_keys(mask_table, length):
@@ -413,41 +555,53 @@
     keys = lax.dynamic_slice_in_dim(key_vectors, kv_head * HEAD_DIM, HEAD_DIM, 1)
     values = lax.dynamic_slice_in_dim(value_vectors, kv_head * HEAD_DIM, HEAD_DIM, 1)
     probs = attention_probs(my_queries, keys, seen_keys(block_mask[0], tokens))
-    early = lax.optimization_barrier((outgoing[1], w_down[0].T, in_part))
+    early = lax.optimization_barrier((outgoing[1], turn_weights(w_down[0]), in_part))
     outgoing[1], down_t, in_part = early
 
     def exchange(rows):
-        rows = swap(rows.reshape(experts, 2 * share, half), "ep")
-        return rows.reshape(2 * part_rows, half)
+        wide = rows.shape[1]
+        rows = swap(rows.reshape(experts, 2 * share, wide), "ep")
+        return rows.reshape(2 * part_rows, wide)
 
     arrived = exchange(outgoing[0])
     first_sum, rows = lax.optimization_barrier((project_down(arrived, down_t), outgoing[1]))
     hidden_grad = lax.psum(first_sum, "cp")
     arrived = exchange(rows)
     saved = turn_saved(saved, share)
-    rows = expert_rows(hidden_grad, saved[0], saved[1], w_gate[0], w_up[0])
+    (rows,) = expert_rows(hidden_grad, saved[0], saved[1], w_gate[0], w_up[0], [width])
     arrived, rows, saved = lax.optimization_barrier((arrived, rows, saved))
     later_sum = project_down(arrived, down_t)
     rows, _ = lax.optimization_barrier((rows, later_sum))
     back = [list(range(quarters))[::-1]]
     later_grad = lax.psum(later_sum, "cp", axis_index_groups=back)
     returned = exchange(rows)
-    returned_later = exchange(expert_rows(later_grad, saved[2], saved[3], w_gate[0], w_up[0]))
-
-    total = collect_rows(in_part[0], returned, grad_out, f32)
-    ready = (returned_later, total, probs, my_queries, values, keys.T)
-    returned_later, total, probs, my_queries, values, keys_t = lax.optimization_barrier(ready)
-    local_grad = collect_rows(in_part[1], returned_later, total, bf16)
-    grad_hidden = to_rows(local_grad)
-    packed = attention_grads(probs, local_grad, my_queries, values, keys_t)
-    packed, grad_hidden = lax.optimization_barrier((packed, grad_hidden))
-    packed = swap(packed.reshape(quarters, tokens // quarters, -1), "cp")
-    grad_query = packed[:, :, :width].transpose(1, 0, 2).reshape(tokens // quarters, -1)
-    sums = packed[:, :, width:].astype(f32)
-    sums = sums.reshape(quarters * heads_here // group, -1, tokens // quarters, 2, HEAD_DIM)
-    sums = jnp.sum(sums, axis=1).transpose(2, 1, 0, 3).reshape(2, tokens // quarters, -1)
-    sums = sums.astype(bf16)
-    return (grad_hidden, grad_query, sums[0], sums[1])
+    last = width // LAST_SHARE
+    most = width - last
+    rows = expert_rows(later_grad, saved[2], saved[3], w_gate[0], w_up[0], [most, last])
+    returned_most = exchange(rows[0])
+    chosen = [chosen_rows(slots, part_rows) for slots in in_part]
+    total = collect_rows(chosen[0], *stay(returned), grad_out, 0, f32)
+    ready = (returned_most, rows[1], chosen, total, probs, my_queries, values, keys.T)
+    ready = lax.optimization_barrier(ready)
+    returned_most, last_rows, chosen, total, probs, my_queries, values, keys_t = ready
+    returned_last = exchange(last_rows)
+
+    most_grad = collect_rows(chosen[1], returned_most, total, 0, bf16)
+    grad_pieces = to_rows(most_grad)
+    query_part, *sums = attention_grads(probs, most_grad, my_queries, values, keys_t, 0)
+    query_pieces = to_rows(query_part)
+
+    last_grad = collect_rows(chosen[1], returned_last, total, most, bf16)
+    packed = attention_grads(
+        probs, last_grad, my_queries, values, keys_t, most // HEAD_DIM, sums
+    )
+    ready = (packed, [p for p, _ in grad_pieces], [p for p, _ in query_pieces])
+    packed, grads, query_grads = lax.optimization_barrier(ready)
+    rows_here = tokens // quarters
+    packed = swap(packed.reshape(quarters, rows_here, -1), "cp")
+    grad_hidden = join_rows([(p, i) for p, (_, i) in zip(grads, grad_pieces)], most, width)
+    grad_query = join_rows([(p, i) for p, (_, i) in zip(query_grads, query_pieces)], most, width)
+    return finish(packed, grad_hidden, grad_query, group // heads_here)
 
 
 def solution(mesh):

time: 381 us -> 367 us (0.963)
  blocking collectives: 23.3 us -> 0 us
  starting transfers between devices: 49.6 us -> 67.6 us
  waiting for transfers between devices: 180 us -> 170 us
    all_to_all x1 -> x0, blocking collectives: 23.3 us -> none  [swap(): return lax.all_to_all(rows, axis, split_axis=0, concat_axis=0, tiled=True)]
    all_to_all x4 -> x6, starting transfers between devices: 42.2 us -> 54.5 us  [swap(): return lax.all_to_all(rows, axis, split_axis=0, concat_axis=0, tiled=True)]
    ppermute x6 -> x9, waiting for transfers between devices: 7.34 us -> 0.69 us  [pass_round(): lax.ppermute(piece, 'cp', [(i, (i + shift) % parts) for i in range(parts)])]
    ppermute x6 -> x9, starting transfers between devices: 7.25 us -> 13 us  [pass_round(): lax.ppermute(piece, 'cp', [(i, (i + shift) % parts) for i in range(parts)])]
    unnamed x38 -> x54, local copies, waits for them, and re-layouts: 13.9 us -> 8.41 us
    all_to_all x4 -> x6, waiting for transfers between devices: 72.8 us -> 67.5 us  [swap(): return lax.all_to_all(rows, axis, split_axis=0, concat_axis=0, tiled=True)]
    pallas_call x3 -> x9, Pallas kernels: 27.5 us -> 32 us  [the longest x3 10.7 us: collect_rows(): pl.pallas_call(collect_kernel, grid=(CHOSEN_STEPS,), in_specs=[pl.BlockSp...]
    dynamic_update_slice x7 -> x10, local copies, waits for them, and re-layouts: 1.12 us -> 4.97 us  [the longest x3 2.92 us: to_heads(): out = lax.dynamic_update_slice(out, piece, (i * rows, 0))]
  transfers between devices with their start and end apart: 13 -> 18, of which waited for: 5 -> 7; matrix products, arithmetic and copies ran while one was open for 3% -> 5% of each run, Pallas kernels for 19% -> 22%
where the time goes in v2:
time: 367 us; the launch traced here: 365 us
  waiting for transfers between devices  170 us (46%)
  Pallas kernels  86 us (23%)
  starting transfers between devices  67.6 us (18%)
  local copies, waits for them, and re-layouts  21.4 us (6%)
  between operations  14.3 us (4%)
  other arithmetic  6.07 us (2%)
    all_to_all x6, waiting for transfers between devices, swap(): return lax.all_to_all(rows, axis, split_axis=0, concat_axis=0, tiled=True)  67.5 us
    all_to_all x6, starting transfers between devices, swap(): return lax.all_to_all(rows, axis, split_axis=0, concat_axis=0, tiled=True)  54.5 us
    psum x1, waiting for transfers between devices, on_device(): later_grad = lax.psum(later_sum, 'cp', axis_index_groups=back)  50.9 us
    psum x1, waiting for transfers between devices, on_device(): hidden_grad = lax.psum(first_sum, 'cp')  50.7 us
    pallas_call x2, Pallas kernels, expert_rows(): pl.pallas_call(expert_kernel, grid=(STEPS,), in_specs=[row_block, row_blo...  18.2 us
    ppermute x9, starting transfers between devices, pass_round(): lax.ppermute(piece, 'cp', [(i, (i + shift) % parts) for i in range(parts)])  13 us
    pallas_call x2, Pallas kernels, send_rows(): pl.pallas_call(functools.partial(route_rows, part, capacity), grid=(STEPS...  10.7 us
    pallas_call x3, Pallas kernels, collect_rows(): pl.pallas_call(collect_kernel, grid=(CHOSEN_STEPS,), in_specs=[pl.BlockSp...  10.7 us
  transfers between devices with their start and end apart: 18, of which 7 were waited for; matrix products, arithmetic and copies ran while one was open for 5% of the time, Pallas kernels for 22%

profile of v2, /device:TPU:6, one launch (start us, length us, event | category | flops | bytes accessed | tf_op | source)
XLA Modules:
  0.0 365.4 jit_solution(12367937851956248949)
XLA Ops:
  7.2 3.0 pad_maximum_fusion
  10.2 5.2 %send_rows.2 = bf16[2560,512]{1,0:T(8,128)(2,1)} custom-call(s32[4,512]{1,0:T(4,128)} %bitcast.42, s32[4,512]{1,0:T(4,128)} %bitcast.40, s32[4,512]{1,0:T(4,128)} %bitcast.38, f32[4,512]{1,0:T(4,128)} %bitcast.48, bf16[512,1024]{1,0:T(8,128)(2,1)} %base_ref.1), custom_call_target="tpu_custom_call" | custom-call | flops 1342177280 | bytes 5242880 | tf_op jit(solution)/shard_map/send_rows/pallas_call | solution.py:88
  15.5 12.3 %all-to-all-start = ((bf16[64,40,512]{2,1,0:T(8,128)(2,1)}), bf16[64,40,512]{2,1,0:T(8,128)(2,1)S(1)}, u32[]{:S(2)}, u32[]{:S(2)}) async-start(bf16[64,40,512]{2,1,0:T(8,128)(2,1)} %bitcast.35), calls=%async_computation | async-start | bytes 5242880 | tf_op jit(solution)/shard_map/all_to_all | solution.py:509
  30.1 3.8 %turn_weights.1.down_ref = bf16[1024,768]{1,0:T(8,128)(2,1)} custom-call(bf16[768,1024]{1,0:T(8,128)(2,1)} %bitcast.37), custom_call_target="tpu_custom_call" | custom-call | flops 786432 | bytes 3145728 | tf_op jit(solution)/shard_map/turn_weights/pallas_call | solution.py:139
  33.9 5.4 %send_rows.3 = bf16[2560,512]{1,0:T(8,128)(2,1)} custom-call(s32[4,512]{1,0:T(4,128)} %bitcast.43, s32[4,512]{1,0:T(4,128)} %bitcast.41, s32[4,512]{1,0:T(4,128)} %bitcast.39, f32[4,512]{1,0:T(4,128)} %bitcast.49, bf16[512,1024]{1,0:T(8,128)(2,1)} %base_ref.1), custom_call_target="tpu_custom_call" | custom-call | flops 1342177280 | bytes 5242880 | tf_op jit(solution)/shard_map/send_rows/pallas_call | solution.py:88
  41.2 46.5 %all-to-all-done = bf16[64,40,512]{2,1,0:T(8,128)(2,1)S(1)} async-done(((bf16[64,40,512]{2,1,0:T(8,128)(2,1)}), bf16[64,40,512]{2,1,0:T(8,128)(2,1)S(1)}, u32[]{:S(2)}, u32[]{:S(2)}) %all-to-all-start) | async-done | bytes 2621472 | tf_op jit(solution)/shard_map/all_to_all | solution.py:509
  87.7 5.1 %project_down.2 = bf16[1280,768]{1,0:T(8,128)(2,1)} custom-call(bf16[2560,512]{1,0:T(8,128)(2,1)S(1)} %bitcast.27, bf16[1024,768]{1,0:T(8,128)(2,1)} %turn_weights.1.down_ref), custom_call_target="tpu_custom_call" | custom-call | flops 2013265920 | bytes 4587520 | tf_op jit(solution)/shard_map/project_down/pallas_call | solution.py:163
  92.8 8.3 %all-to-all-start.1 = ((bf16[64,40,512]{2,1,0:T(8,128)(2,1)}), bf16[64,40,512]{2,1,0:T(8,128)(2,1)S(1)}, u32[]{:S(2)}, u32[]{:S(2)}) async-start(bf16[64,40,512]{2,1,0:T(8,128)(2,1)} %bitcast.33), calls=%async_computation.1 | async-start | bytes 5242880 | tf_op jit(solution)/shard_map/all_to_all | solution.py:509
  101.2 7.8 %turn_saved.1 = (bf16[1280,768]{1,0:T(8,128)(2,1)}, bf16[1280,768]{1,0:T(8,128)(2,1)}, bf16[1280,768]{1,0:T(8,128)(2,1)}, bf16[1280,768]{1,0:T(8,128)(2,1)}) custom-call(bf16[4,2,192,2560]{3,2,1,0:T(8,128)(2,1)} %bitcast.32), custom_call_target="tpu_custom_call" | custom-call | flops 3932160 | bytes 15728640 | tf_op jit(solution)/shard_map/turn_saved/pallas_call | solution.py:119
  109.0 50.7 %all-reduce.3.cloned.1.call-done.hidden_ref = bf16[1280,768]{1,0:T(8,128)(2,1)} async-done(((bf16[1280,768]{1,0:T(8,128)(2,1)}), bf16[1280,768]{1,0:T(8,128)(2,1)}) %all-reduce.3.cloned.1.call-update) | async-done | bytes 1966096 | tf_op jit(solution)/shard_map/psum | solution.py:568
  159.7 9.2 %expert_rows.2 = bf16[2560,512]{1,0:T(8,128)(2,1)} custom-call(bf16[1280,768]{1,0:T(8,128)(2,1)} %all-reduce.3.cloned.1.call-done.hidden_ref, bf16[1280,768]{1,0:T(8,128)(2,1)} %get-tuple-element.45.gate_ref, bf16[1280,768]{1,0:T(8,128)(2,1)} %get-tuple-element.46.up_ref, bf16[768,1024]{1,0:T(8,128)(2,1)} %bitcast.44, bf16[768,1024]{1,0:T(8,128)(2,1)} %bitcast.46), custom_call_target="tpu_custom_call" | custom-call | flops 128849018880 | bytes 8519680 | tf_op jit(solution)/shard_map/expert_rows/pallas_call | solution.py:203
  168.8 5.1 %project_down.3 = bf16[1280,768]{1,0:T(8,128)(2,1)} custom-call(bf16[2560,512]{1,0:T(8,128)(2,1)S(1)} %bitcast.28, bf16[1024,768]{1,0:T(8,128)(2,1)} %turn_weights.1.down_ref), custom_call_target="tpu_custom_call" | custom-call | flops 2013265920 | bytes 4587520 | tf_op jit(solution)/shard_map/project_down/pallas_call | solution.py:163
  174.0 10.8 %all-to-all-start.3 = ((bf16[64,40,512]{2,1,0:T(8,128)(2,1)}), bf16[64,40,512]{2,1,0:T(8,128)(2,1)S(1)}, u32[]{:S(2)}, u32[]{:S(2)}) async-start(bf16[64,40,512]{2,1,0:T(8,128)(2,1)} %bitcast.34), calls=%async_computation.3 | async-start | bytes 5242880 | tf_op jit(solution)/shard_map/all_to_all | solution.py:509
  184.8 50.9 %all-reduce.5.cloned.1.call-done.hidden_ref = bf16[1280,768]{1,0:T(8,128)(2,1)} async-done(((bf16[1280,768]{1,0:T(8,128)(2,1)}), bf16[1280,768]{1,0:T(8,128)(2,1)}) %all-reduce.5.cloned.1.call-update) | async-done | bytes 1966096 | tf_op jit(solution)/shard_map/psum | solution.py:576
  235.7 9.1 %expert_rows.3 = (bf16[2560,384]{1,0:T(8,128)(2,1)}, bf16[2560,128]{1,0:T(8,128)(2,1)}) custom-call(bf16[1280,768]{1,0:T(8,128)(2,1)} %all-reduce.5.cloned.1.call-done.hidden_ref, bf16[1280,768]{1,0:T(8,128)(2,1)} %get-tuple-element.50.gate_ref, bf16[1280,768]{1,0:T(8,128)(2,1)} %get-tuple-element.51.up_ref, bf16[768,1024]{1,0:T(8,128)(2,1)} %bitcast.45, ...), custom_call_target="tpu_custom_call" | custom-call | flops 128849018880 | bytes 8519680 | tf_op jit(solution)/shard_map/expert_rows/pallas_call | solution.py:203
  244.8 1.5 copy-done.7
  246.3 10.7 %all-to-all-start.2 = ((bf16[64,40,384]{2,1,0:T(8,128)(2,1)}), bf16[64,40,384]{2,1,0:T(8,128)(2,1)S(1)}, u32[]{:S(2)}, u32[]{:S(2)}) async-start(bf16[64,40,384]{2,1,0:T(8,128)(2,1)} %bitcast.36), calls=%async_computation.2 | async-start | bytes 3932160 | tf_op jit(solution)/shard_map/all_to_all | solution.py:509
  257.3 2.1 constant_dynamic-slice_fusion.10
  259.6 2.0 collective-permute-start.1
  261.7 1.9 collective-permute-start.2
  263.6 1.0 broadcast_in_dim.24
  264.6 1.8 gt.20
  266.4 1.2 fusion.1.seen_ref
  269.3 1.0 copy.51
  271.3 1.8 chosen_rows.2.chosen_ref
  273.1 0.9 copy-done.5
  274.1 1.8 chosen_rows.3.chosen_ref
  275.9 1.0 constant_dynamic-update-slice_fusion.10
  276.9 1.0 constant_dynamic-update-slice_fusion.9
  277.9 1.0 constant_dynamic-update-slice_fusion.8.q_ref
  278.9 7.0 %attention_probs.1.probs_ref = f32[8,512,512]{2,1,0:T(8,128)} custom-call(bf16[512,1024]{1,0:T(8,128)(2,1)S(1)} %constant_dynamic-update-slice_fusion.8.q_ref, bf16[512,128]{1,0:T(8,128)(2,1)S(1)} %copy-done.4, f32[512,512]{1,0:T(8,128)S(1)} %copy-done.3), custom_call_target="tpu_custom_call" | custom-call | flops 536870912 | bytes 8388608 | tf_op jit(solution)/shard_map/attention_probs/pallas_call | solution.py:301
  285.9 4.4 %collect_rows.3.base_ref = f32[512,1024]{1,0:T(8,128)S(1)} custom-call(bf16[512,1280]{1,0:T(8,128)(2,1)} %chosen_rows.2.chosen_ref, bf16[2560,512]{1,0:T(8,128)(2,1)} %bitcast.31, bf16[512,1024]{1,0:T(8,128)(2,1)} %base_ref.1), custom_call_target="tpu_custom_call" | custom-call | flops 1342177280 | bytes 6815744 | tf_op jit(solution)/shard_map/collect_rows/pallas_call | solution.py:264
  290.2 1.4 copy-done.1
  291.6 11.4 %all-to-all-done.2 = bf16[64,40,384]{2,1,0:T(8,128)(2,1)S(1)} async-done(((bf16[64,40,384]{2,1,0:T(8,128)(2,1)}), bf16[64,40,384]{2,1,0:T(8,128)(2,1)S(1)}, u32[]{:S(2)}, u32[]{:S(2)}) %all-to-all-start.2) | async-done | bytes 1966112 | tf_op jit(solution)/shard_map/all_to_all | solution.py:509
  303.0 8.5 %all-to-all-start.4 = ((bf16[64,40,128]{2,1,0:T(8,128)(2,1)}), bf16[64,40,128]{2,1,0:T(8,128)(2,1)}, u32[]{:S(2)}, u32[]{:S(2)}) async-start(bf16[64,40,128]{2,1,0:T(8,128)(2,1)} %bitcast.19), calls=%async_computation.4 | async-start | bytes 1310720 | tf_op jit(solution)/shard_map/all_to_all | solution.py:509
  311.5 3.8 %collect_rows.5.grad_ref = bf16[512,768]{1,0:T(8,128)(2,1)S(1)} custom-call(bf16[512,1280]{1,0:T(8,128)(2,1)} %chosen_rows.3.chosen_ref, bf16[2560,384]{1,0:T(8,128)(2,1)S(1)} %bitcast.26, f32[512,1024]{1,0:T(8,128)} %copy-done.1), custom_call_target="tpu_custom_call" | custom-call | flops 1006632960 | bytes 5111808 | tf_op jit(solution)/shard_map/collect_rows/pallas_call | solution.py:264
  316.4 2.0 collective-permute-start.4
  318.4 1.9 collective-permute-start.5
  320.3 8.1 %first_grads.1 = (bf16[512,768]{1,0:T(8,128)(2,1)S(1)}, f32[512,128]{1,0:T(8,128)S(1)}, f32[512,128]{1,0:T(8,128)S(1)}) custom-call(f32[8,512,512]{2,1,0:T(8,128)} %attention_probs.1.probs_ref, bf16[512,768]{1,0:T(8,128)(2,1)S(1)} %collect_rows.5.grad_ref, bf16[512,1024]{1,0:T(8,128)(2,1)} %copy-done.2, ...), custom_call_target="tpu_custom_call" | custom-call | flops 1610612736 | bytes 6291456 | tf_op jit(solution)/shard_map/first_grads/pallas_call | solution.py:388
  328.7 1.9 collective-permute-start.7
  330.6 2.5 collective-permute-start.8
  333.1 2.5 collect_rows.4.grad_ref
  335.6 4.3 %last_grads.1 = bf16[512,768]{1,0:T(8,128)(2,1)} custom-call(f32[8,512,512]{2,1,0:T(8,128)} %attention_probs.1.probs_ref, bf16[512,256]{1,0:T(8,128)(2,1)S(1)} %collect_rows.4.grad_ref, bf16[512,1024]{1,0:T(8,128)(2,1)} %copy-done.2, bf16[512,128]{1,0:T(8,128)(2,1)S(1)} %constant_dynamic-slice_fusion.8.v_ref, bf16[128,512]{1,0:T(8,128)(2,1)S(1)} %bitcast.30, ...), custom_call_target="tpu_custom_call" | custom-call | flops 536870912 | bytes 2097152 | tf_op jit(solution)/shard_map/last_grads/pallas_call | solution.py:399
  341.3 3.9 %all-to-all-start.5 = ((bf16[4,128,768]{2,1,0:T(8,128)(2,1)}), bf16[4,128,768]{2,1,0:T(8,128)(2,1)S(1)}, u32[]{:S(2)}, u32[]{:S(2)}) async-start(bf16[4,128,768]{2,1,0:T(8,128)(2,1)} %bitcast.21), calls=%async_computation.5 | async-start | bytes 1572864 | tf_op jit(solution)/shard_map/all_to_all | solution.py:509
  345.5 1.0 constant_dynamic-update-slice_fusion.2
  346.6 1.0 constant_dynamic-update-slice_fusion
  347.6 9.7 %all-to-all-done.5.got_ref = bf16[4,128,768]{2,1,0:T(8,128)(2,1)S(1)} async-done(((bf16[4,128,768]{2,1,0:T(8,128)(2,1)}), bf16[4,128,768]{2,1,0:T(8,128)(2,1)S(1)}, u32[]{:S(2)}, u32[]{:S(2)}) %all-to-all-start.5) | async-done | bytes 786464 | tf_op jit(solution)/shard_map/all_to_all | solution.py:509
  357.3 1.5 finish.1
  (92 shorter events, 10.4 us)
Async XLA Ops:
  7.2 260.5 %copy-start = (bf16[512,256]{1,0:T(8,128)(2,1)S(1)}, bf16[512,256]{1,0:T(8,128)(2,1)}, u32[]{:S(2)}) copy-start(bf16[512,256]{1,0:T(8,128)(2,1)} %param.25) | copy-start | bytes 786436
  7.2 94.0 %all-gather.3.cloned.1.call-start = ((), (), s32[]{:S(2)}) async-start(), calls=%async_computation.8 | async-start | bytes 9830400 | tf_op jit(solution)/shard_map/all_gather | solution.py:542
  15.5 12.4 %copy-start.21 = (s32[512,4]{0,1:T(4,128)S(1)}, s32[512,4]{0,1:T(4,128)}, u32[]{:S(2)}) copy-start(s32[512,4]{0,1:T(4,128)} %param.17) | copy-start | bytes 24580
  15.5 12.5 %copy-start.22 = (s32[512,4]{0,1:T(4,128)S(1)}, s32[512,4]{0,1:T(4,128)}, u32[]{:S(2)}) copy-start(s32[512,4]{0,1:T(4,128)} %param.16) | copy-start | bytes 24580
  15.5 13.4 %copy-start.23 = (s32[512,4]{0,1:T(4,128)S(1)}, s32[512,4]{0,1:T(4,128)}, u32[]{:S(2)}) copy-start(s32[512,4]{0,1:T(4,128)} %param.15) | copy-start | bytes 24580
  15.5 72.2 %all-to-all-start = ((bf16[64,40,512]{2,1,0:T(8,128)(2,1)}), bf16[64,40,512]{2,1,0:T(8,128)(2,1)S(1)}, u32[]{:S(2)}, u32[]{:S(2)}) async-start(bf16[64,40,512]{2,1,0:T(8,128)(2,1)} %bitcast.35), calls=%async_computation | async-start | bytes 5242880 | tf_op jit(solution)/shard_map/all_to_all | solution.py:509
  27.8 131.9 %all-reduce.3.cloned.1.call-start = ((), (), s32[]{:S(2)}) async-start(), calls=%async_computation.6 | async-start | bytes 3932160 | tf_op jit(solution)/shard_map/psum | solution.py:568
  33.9 5.5 %copy-start.10 = (s32[512,4]{1,0:T(8,128)S(1)}, s32[512,4]{1,0:T(8,128)}, u32[]{:S(2)}) copy-start(s32[512,4]{1,0:T(8,128)} %copy.46) | copy-start | bytes 24580
  33.9 5.5 %copy-start.11 = (s32[512,4]{1,0:T(8,128)S(1)}, s32[512,4]{1,0:T(8,128)}, u32[]{:S(2)}) copy-start(s32[512,4]{1,0:T(8,128)} %copy.47) | copy-start | bytes 24580
  92.8 76.0 %all-to-all-start.1 = ((bf16[64,40,512]{2,1,0:T(8,128)(2,1)}), bf16[64,40,512]{2,1,0:T(8,128)(2,1)S(1)}, u32[]{:S(2)}, u32[]{:S(2)}) async-start(bf16[64,40,512]{2,1,0:T(8,128)(2,1)} %bitcast.33), calls=%async_computation.1 | async-start | bytes 5242880 | tf_op jit(solution)/shard_map/all_to_all | solution.py:509
  101.1 134.6 %all-reduce.5.cloned.1.call-start = ((), (), s32[]{:S(2)}) async-start(), calls=%async_computation.7 | async-start | bytes 3932160 | tf_op jit(solution)/shard_map/psum | solution.py:576
  174.0 70.8 %all-to-all-start.3 = ((bf16[64,40,512]{2,1,0:T(8,128)(2,1)}), bf16[64,40,512]{2,1,0:T(8,128)(2,1)S(1)}, u32[]{:S(2)}, u32[]{:S(2)}) async-start(bf16[64,40,512]{2,1,0:T(8,128)(2,1)} %bitcast.34), calls=%async_computation.3 | async-start | bytes 5242880 | tf_op jit(solution)/shard_map/all_to_all | solution.py:509
  244.8 1.5 copy-start.7
  246.3 56.7 %all-to-all-start.2 = ((bf16[64,40,384]{2,1,0:T(8,128)(2,1)}), bf16[64,40,384]{2,1,0:T(8,128)(2,1)S(1)}, u32[]{:S(2)}, u32[]{:S(2)}) async-start(bf16[64,40,384]{2,1,0:T(8,128)(2,1)} %bitcast.36), calls=%async_computation.2 | async-start | bytes 3932160 | tf_op jit(solution)/shard_map/all_to_all | solution.py:509
  257.1 6.5 %copy-start.24 = (s32[1,8,8]{2,1,0:T(8,128)S(1)}, s32[1,8,8]{2,1,0:T(8,128)}, u32[]{:S(2)}) copy-start(s32[1,8,8]{2,1,0:T(8,128)} %param.27) | copy-start | bytes 772
  259.4 16.6 %collective-permute-start = (bf16[128,1024]{1,0:T(8,128)(2,1)}, bf16[128,1024]{1,0:T(8,128)(2,1)}, u32[]{:S(2)}, u32[]{:S(2)}) collective-permute-start(bf16[128,1024]{1,0:T(8,128)(2,1)} %get-tuple-element.83), channel_id=1, source_target_pairs={{0,1},{1,2},{2,3},{3,0},{4,5},{5,6},{6,7},{7,4},{8,9},{9,10},{10,1... | collective-permute-start | bytes 786440 | tf_op jit(solution)/shard_map/ppermute | solution.py:419
  259.6 17.3 %collective-permute-start.1 = (bf16[128,1024]{1,0:T(8,128)(2,1)}, bf16[128,1024]{1,0:T(8,128)(2,1)}, u32[]{:S(2)}, u32[]{:S(2)}) collective-permute-start(bf16[128,1024]{1,0:T(8,128)(2,1)} %get-tuple-element.85), channel_id=1, source_target_pairs={{0,2},{1,3},{2,0},{3,1},{4,6},{5,7},{6,4},{7,5},{8,10},{9,11},{10,... | collective-permute-start | bytes 786440 | tf_op jit(solution)/shard_map/ppermute | solution.py:419
  261.7 16.2 %collective-permute-start.2 = (bf16[128,1024]{1,0:T(8,128)(2,1)}, bf16[128,1024]{1,0:T(8,128)(2,1)}, u32[]{:S(2)}, u32[]{:S(2)}) collective-permute-start(bf16[128,1024]{1,0:T(8,128)(2,1)} %get-tuple-element.82), channel_id=1, source_target_pairs={{0,3},{1,0},{2,1},{3,2},{4,7},{5,4},{6,5},{7,6},{8,11},{9,8},{10,9... | collective-permute-start | bytes 786440 | tf_op jit(solution)/shard_map/ppermute | solution.py:419
  270.3 1.0 copy-start.6
  273.1 0.9 copy-start.5
  274.1 4.8 %copy-start.3 = (f32[512,512]{1,0:T(8,128)S(1)}, f32[512,512]{1,0:T(8,128)}, u32[]{:S(2)}) copy-start(f32[512,512]{1,0:T(8,128)} %fusion.1.seen_ref) | copy-start | bytes 3145732
  274.1 4.8 %copy-start.4 = (bf16[512,128]{1,0:T(8,128)(2,1)S(1)}, bf16[512,128]{1,0:T(8,128)(2,1)}, u32[]{:S(2)}) copy-start(bf16[512,128]{1,0:T(8,128)(2,1)} %constant_dynamic-slice_fusion.9.k_ref) | copy-start | bytes 393220
  278.9 7.0 %copy-start.2 = (bf16[512,1024]{1,0:T(8,128)(2,1)}, bf16[512,1024]{1,0:T(8,128)(2,1)S(1)}, u32[]{:S(2)}) copy-start(bf16[512,1024]{1,0:T(8,128)(2,1)S(1)} %constant_dynamic-update-slice_fusion.8.q_ref) | copy-start | bytes 3145732
  290.2 1.4 copy-start.1
  303.0 30.1 %all-to-all-start.4 = ((bf16[64,40,128]{2,1,0:T(8,128)(2,1)}), bf16[64,40,128]{2,1,0:T(8,128)(2,1)}, u32[]{:S(2)}, u32[]{:S(2)}) async-start(bf16[64,40,128]{2,1,0:T(8,128)(2,1)} %bitcast.19), calls=%async_computation.4 | async-start | bytes 1310720 | tf_op jit(solution)/shard_map/all_to_all | solution.py:509
  316.1 14.5 %collective-permute-start.3 = (bf16[128,768]{1,0:T(8,128)(2,1)S(1)}, bf16[128,768]{1,0:T(8,128)(2,1)S(1)}, u32[]{:S(2)}, u32[]{:S(2)}) collective-permute-start(bf16[128,768]{1,0:T(8,128)(2,1)S(1)} %get-tuple-element.92), channel_id=1, source_target_pairs={{0,1},{1,2},{2,3},{3,0},{4,5},{5,6},{6,7},{7,4},{8,9},{9,10},{10,1... | collective-permute-start | bytes 589832 | tf_op jit(solution)/shard_map/ppermute | solution.py:419
  316.4 23.5 %collective-permute-start.4 = (bf16[128,768]{1,0:T(8,128)(2,1)S(1)}, bf16[128,768]{1,0:T(8,128)(2,1)S(1)}, u32[]{:S(2)}, u32[]{:S(2)}) collective-permute-start(bf16[128,768]{1,0:T(8,128)(2,1)S(1)} %get-tuple-element.91), channel_id=1, source_target_pairs={{0,2},{1,3},{2,0},{3,1},{4,6},{5,7},{6,4},{7,5},{8,10},{9,11},{10,... | collective-permute-start | bytes 589832 | tf_op jit(solution)/shard_map/ppermute | solution.py:419
  318.4 21.5 %collective-permute-start.5 = (bf16[128,768]{1,0:T(8,128)(2,1)S(1)}, bf16[128,768]{1,0:T(8,128)(2,1)}, u32[]{:S(2)}, u32[]{:S(2)}) collective-permute-start(bf16[128,768]{1,0:T(8,128)(2,1)S(1)} %get-tuple-element.90), channel_id=1, source_target_pairs={{0,3},{1,0},{2,1},{3,2},{4,7},{5,4},{6,5},{7,6},{8,11},{9,8},{10,9... | collective-permute-start | bytes 589832 | tf_op jit(solution)/shard_map/ppermute | solution.py:419
  328.4 11.7 %collective-permute-start.6 = (bf16[128,768]{1,0:T(8,128)(2,1)S(1)}, bf16[128,768]{1,0:T(8,128)(2,1)}, u32[]{:S(2)}, u32[]{:S(2)}) collective-permute-start(bf16[128,768]{1,0:T(8,128)(2,1)S(1)} %get-tuple-element.88), channel_id=1, source_target_pairs={{0,1},{1,2},{2,3},{3,0},{4,5},{5,6},{6,7},{7,4},{8,9},{9,10},{10,1... | collective-permute-start | bytes 589832 | tf_op jit(solution)/shard_map/ppermute | solution.py:419
  328.7 11.5 %collective-permute-start.7 = (bf16[128,768]{1,0:T(8,128)(2,1)S(1)}, bf16[128,768]{1,0:T(8,128)(2,1)S(1)}, u32[]{:S(2)}, u32[]{:S(2)}) collective-permute-start(bf16[128,768]{1,0:T(8,128)(2,1)S(1)} %get-tuple-element.87), channel_id=1, source_target_pairs={{0,2},{1,3},{2,0},{3,1},{4,6},{5,7},{6,4},{7,5},{8,10},{9,11},{10,... | collective-permute-start | bytes 589832 | tf_op jit(solution)/shard_map/ppermute | solution.py:419
  330.6 5.0 %copy-start.15 = (bf16[128,768]{1,0:T(8,128)(2,1)}, bf16[128,768]{1,0:T(8,128)(2,1)S(1)}, u32[]{:S(2)}) copy-start(bf16[128,768]{1,0:T(8,128)(2,1)S(1)} %collective-permute-done.3) | copy-start | bytes 589828
  330.6 10.0 %collective-permute-start.8 = (bf16[128,768]{1,0:T(8,128)(2,1)S(1)}, bf16[128,768]{1,0:T(8,128)(2,1)S(1)}, u32[]{:S(2)}, u32[]{:S(2)}) collective-permute-start(bf16[128,768]{1,0:T(8,128)(2,1)S(1)} %get-tuple-element.86), channel_id=1, source_target_pairs={{0,3},{1,0},{2,1},{3,2},{4,7},{5,4},{6,5},{7,6},{8,11},{9,8},{10,9... | collective-permute-start | bytes 589832 | tf_op jit(solution)/shard_map/ppermute | solution.py:419
  339.9 0.7 copy-start.13
  340.1 0.7 copy-start.17
  340.6 0.7 copy-start.19
  340.6 4.9 %copy-start.12 = (bf16[128,768]{1,0:T(8,128)(2,1)S(1)}, bf16[128,768]{1,0:T(8,128)(2,1)}, u32[]{:S(2)}) copy-start(bf16[128,768]{1,0:T(8,128)(2,1)} %get-tuple-element.70) | copy-start | bytes 589828
  341.3 16.0 %all-to-all-start.5 = ((bf16[4,128,768]{2,1,0:T(8,128)(2,1)}), bf16[4,128,768]{2,1,0:T(8,128)(2,1)S(1)}, u32[]{:S(2)}, u32[]{:S(2)}) async-start(bf16[4,128,768]{2,1,0:T(8,128)(2,1)} %bitcast.21), calls=%async_computation.5 | async-start | bytes 1572864 | tf_op jit(solution)/shard_map/all_to_all | solution.py:509
  345.2 1.3 copy-start.16
  345.2 1.3 copy-start.18
  345.2 1.4 copy-start.14
  345.3 1.3 copy-start.20
  347.6 9.7 %copy-start.8 = (bf16[128,4096]{1,0:T(8,128)(2,1)}, bf16[128,4096]{1,0:T(8,128)(2,1)S(1)}, u32[]{:S(2)}) copy-start(bf16[128,4096]{1,0:T(8,128)(2,1)S(1)} %get-tuple-element.95.refs_0_) | copy-start | bytes 3145732
  347.6 9.7 %copy-start.9 = (bf16[128,4096]{1,0:T(8,128)(2,1)}, bf16[128,4096]{1,0:T(8,128)(2,1)S(1)}, u32[]{:S(2)}) copy-start(bf16[128,4096]{1,0:T(8,128)(2,1)S(1)} %get-tuple-element.94.refs_1_) | copy-start | bytes 3145732
Sparse Core Ops, SparseCore 0:
  10.3 84.2 all-gather.2
  97.0 62.6 all-reduce.2
  174.1 61.5 all-reduce.4

commit v3 on v2

--- a/solution.py
+++ b/solution.py
@@ -13,6 +13,8 @@
 STEPS = 4
 CHOSEN_STEPS = 2
 DOWN_STEPS = 3
+DOWN_COLS = 256
+PROJECT_STEPS = 2
 LAST_SHARE = 4
 VMEM_LIMIT = 56 * 1024 * 1024
 SMALL_VMEM = 24 * 1024 * 1024
@@ -39,20 +41,20 @@
         cols = slice(j * LANES, (j + 1) * LANES)
         wide[j, pl.ds(0, rows, 2), :] = low[:, cols]
         wide[j, pl.ds(1, rows, 2), :] = high[:, cols]
-        out_ref[:, cols] = wide[j].astype(bf16)
+        out_ref[:, cols] = wide[j, : 2 * rows, :].astype(bf16)
 
 
 def unweave(rows_ref, wide):
-    slabs, rows = wide.shape[0], wide.shape[1] // 2
+    slabs, rows = wide.shape[0], rows_ref.shape[0] // 2
     for j in range(slabs):
-        wide[j] = rows_ref[:, j * LANES : (j + 1) * LANES].astype(f32)
+        wide[j, : 2 * rows, :] = rows_ref[:, j * LANES : (j + 1) * LANES].astype(f32)
     low = [wide[j, pl.ds(0, rows, 2), :].astype(bf16) for j in range(slabs)]
     high = [wide[j, pl.ds(1, rows, 2), :].astype(bf16) for j in range(slabs)]
     return jnp.concatenate(low, axis=1), jnp.concatenate(high, axis=1)
 
 
 def woven(rows, half):
-    return pltpu.VMEM((half // LANES, 2 * rows, LANES), f32)
+    return pltpu.VMEM((half // LANES, 2 * rows + 8, LANES), f32)
 
 
 def split_by(row, size, count):
@@ -151,18 +153,20 @@
 def down_rows_kernel(rows_ref, down_ref, out_ref, wide):
     half = rows_ref.shape[1]
     low, high = unweave(rows_ref, wide)
-    total = jnp.dot(low, down_ref[:half, :], preferred_element_type=f32)
-    total = total + jnp.dot(high, down_ref[half:, :], preferred_element_type=f32)
-    out_ref[...] = total.astype(bf16)
+    for start in range(0, down_ref.shape[1], DOWN_COLS):
+        cols = slice(start, start + DOWN_COLS)
+        total = jnp.dot(low, down_ref[:half, cols], preferred_element_type=f32)
+        total = total + jnp.dot(high, down_ref[half:, cols], preferred_element_type=f32)
+        out_ref[:, cols] = total.astype(bf16)
 
 
 def project_down(arrived, down_t):
     rows, half = arrived.shape[0] // 2, arrived.shape[1]
     width, hidden = down_t.shape
-    step = rows // STEPS
+    step = rows // PROJECT_STEPS
     return pl.pallas_call(
         down_rows_kernel,
-        grid=(STEPS,),
+        grid=(PROJECT_STEPS,),
         in_specs=[
             pl.BlockSpec((2 * step, half), lambda i: (i, 0)),
             pl.BlockSpec(down_t.shape, lambda i: (0, 0)),

time: 367 us -> 367 us (level)
  no operation moved by 1% of the time
where the time goes in v3:
time: 367 us; the launch traced here: 365 us
  waiting for transfers between devices  170 us (46%)
  Pallas kernels  85.3 us (23%)
  starting transfers between devices  67.6 us (18%)
  local copies, waits for them, and re-layouts  21.4 us (6%)
  between operations  14.3 us (4%)
  other arithmetic  6.07 us (2%)
    all_to_all x6, waiting for transfers between devices, swap(): return lax.all_to_all(rows, axis, split_axis=0, concat_axis=0, tiled=True)  67.5 us
    all_to_all x6, starting transfers between devices, swap(): return lax.all_to_all(rows, axis, split_axis=0, concat_axis=0, tiled=True)  54.5 us
    psum x1, waiting for transfers between devices, on_device(): hidden_grad = lax.psum(first_sum, 'cp')  51 us
    psum x1, waiting for transfers between devices, on_device(): later_grad = lax.psum(later_sum, 'cp', axis_index_groups=back)  50.9 us
    pallas_call x2, Pallas kernels, expert_rows(): pl.pallas_call(expert_kernel, grid=(STEPS,), in_specs=[row_block, row_blo...  18.2 us
    ppermute x9, starting transfers between devices, pass_round(): lax.ppermute(piece, 'cp', [(i, (i + shift) % parts) for i in range(parts)])  13 us
    pallas_call x2, Pallas kernels, send_rows(): pl.pallas_call(functools.partial(route_rows, part, capacity), grid=(STEPS...  10.7 us
    pallas_call x3, Pallas kernels, collect_rows(): pl.pallas_call(collect_kernel, grid=(CHOSEN_STEPS,), in_specs=[pl.BlockSp...  10.7 us
  transfers between devices with their start and end apart: 18, of which 7 were waited for; matrix products, arithmetic and copies ran while one was open for 5% of the time, Pallas kernels for 22%

profile of v3, /device:TPU:6, one launch (start us, length us, event | category | flops | bytes accessed | tf_op | source)
XLA Modules:
  0.0 365.0 jit_solution(7467223833351785589)
XLA Ops:
  7.2 3.0 pad_maximum_fusion
  10.2 5.2 %send_rows.2 = bf16[2560,512]{1,0:T(8,128)(2,1)} custom-call(s32[4,512]{1,0:T(4,128)} %bitcast.42, s32[4,512]{1,0:T(4,128)} %bitcast.40, s32[4,512]{1,0:T(4,128)} %bitcast.38, f32[4,512]{1,0:T(4,128)} %bitcast.48, bf16[512,1024]{1,0:T(8,128)(2,1)} %base_ref.1), custom_call_target="tpu_custom_call" | custom-call | flops 1342177280 | bytes 5242880 | tf_op jit(solution)/shard_map/send_rows/pallas_call | solution.py:90
  15.5 12.3 %all-to-all-start = ((bf16[64,40,512]{2,1,0:T(8,128)(2,1)}), bf16[64,40,512]{2,1,0:T(8,128)(2,1)S(1)}, u32[]{:S(2)}, u32[]{:S(2)}) async-start(bf16[64,40,512]{2,1,0:T(8,128)(2,1)} %bitcast.35), calls=%async_computation | async-start | bytes 5242880 | tf_op jit(solution)/shard_map/all_to_all | solution.py:513
  30.1 3.8 %turn_weights.1.down_ref = bf16[1024,768]{1,0:T(8,128)(2,1)} custom-call(bf16[768,1024]{1,0:T(8,128)(2,1)} %bitcast.37), custom_call_target="tpu_custom_call" | custom-call | flops 786432 | bytes 3145728 | tf_op jit(solution)/shard_map/turn_weights/pallas_call | solution.py:141
  33.9 5.5 %send_rows.3 = bf16[2560,512]{1,0:T(8,128)(2,1)} custom-call(s32[4,512]{1,0:T(4,128)} %bitcast.43, s32[4,512]{1,0:T(4,128)} %bitcast.41, s32[4,512]{1,0:T(4,128)} %bitcast.39, f32[4,512]{1,0:T(4,128)} %bitcast.49, bf16[512,1024]{1,0:T(8,128)(2,1)} %base_ref.1), custom_call_target="tpu_custom_call" | custom-call | flops 1342177280 | bytes 5242880 | tf_op jit(solution)/shard_map/send_rows/pallas_call | solution.py:90
  41.2 46.5 %all-to-all-done = bf16[64,40,512]{2,1,0:T(8,128)(2,1)S(1)} async-done(((bf16[64,40,512]{2,1,0:T(8,128)(2,1)}), bf16[64,40,512]{2,1,0:T(8,128)(2,1)S(1)}, u32[]{:S(2)}, u32[]{:S(2)}) %all-to-all-start) | async-done | bytes 2621472 | tf_op jit(solution)/shard_map/all_to_all | solution.py:513
  87.7 4.8 %project_down.2 = bf16[1280,768]{1,0:T(8,128)(2,1)} custom-call(bf16[2560,512]{1,0:T(8,128)(2,1)S(1)} %bitcast.27, bf16[1024,768]{1,0:T(8,128)(2,1)} %turn_weights.1.down_ref), custom_call_target="tpu_custom_call" | custom-call | flops 2013265920 | bytes 4587520 | tf_op jit(solution)/shard_map/project_down/pallas_call | solution.py:167
  92.5 8.3 %all-to-all-start.1 = ((bf16[64,40,512]{2,1,0:T(8,128)(2,1)}), bf16[64,40,512]{2,1,0:T(8,128)(2,1)S(1)}, u32[]{:S(2)}, u32[]{:S(2)}) async-start(bf16[64,40,512]{2,1,0:T(8,128)(2,1)} %bitcast.33), calls=%async_computation.1 | async-start | bytes 5242880 | tf_op jit(solution)/shard_map/all_to_all | solution.py:513
  100.8 7.8 %turn_saved.1 = (bf16[1280,768]{1,0:T(8,128)(2,1)}, bf16[1280,768]{1,0:T(8,128)(2,1)}, bf16[1280,768]{1,0:T(8,128)(2,1)}, bf16[1280,768]{1,0:T(8,128)(2,1)}) custom-call(bf16[4,2,192,2560]{3,2,1,0:T(8,128)(2,1)} %bitcast.32), custom_call_target="tpu_custom_call" | custom-call | flops 3932160 | bytes 15728640 | tf_op jit(solution)/shard_map/turn_saved/pallas_call | solution.py:121
  108.7 51.0 %all-reduce.3.cloned.1.call-done.hidden_ref = bf16[1280,768]{1,0:T(8,128)(2,1)} async-done(((bf16[1280,768]{1,0:T(8,128)(2,1)}), bf16[1280,768]{1,0:T(8,128)(2,1)}) %all-reduce.3.cloned.1.call-update) | async-done | bytes 1966096 | tf_op jit(solution)/shard_map/psum | solution.py:572
  159.7 9.1 %expert_rows.2 = bf16[2560,512]{1,0:T(8,128)(2,1)} custom-call(bf16[1280,768]{1,0:T(8,128)(2,1)} %all-reduce.3.cloned.1.call-done.hidden_ref, bf16[1280,768]{1,0:T(8,128)(2,1)} %get-tuple-element.45.gate_ref, bf16[1280,768]{1,0:T(8,128)(2,1)} %get-tuple-element.46.up_ref, bf16[768,1024]{1,0:T(8,128)(2,1)} %bitcast.44, bf16[768,1024]{1,0:T(8,128)(2,1)} %bitcast.46), custom_call_target="tpu_custom_call" | custom-call | flops 128849018880 | bytes 8519680 | tf_op jit(solution)/shard_map/expert_rows/pallas_call | solution.py:207
  168.8 4.8 %project_down.3 = bf16[1280,768]{1,0:T(8,128)(2,1)} custom-call(bf16[2560,512]{1,0:T(8,128)(2,1)S(1)} %bitcast.28, bf16[1024,768]{1,0:T(8,128)(2,1)} %turn_weights.1.down_ref), custom_call_target="tpu_custom_call" | custom-call | flops 2013265920 | bytes 4587520 | tf_op jit(solution)/shard_map/project_down/pallas_call | solution.py:167
  173.6 10.8 %all-to-all-start.3 = ((bf16[64,40,512]{2,1,0:T(8,128)(2,1)}), bf16[64,40,512]{2,1,0:T(8,128)(2,1)S(1)}, u32[]{:S(2)}, u32[]{:S(2)}) async-start(bf16[64,40,512]{2,1,0:T(8,128)(2,1)} %bitcast.34), calls=%async_computation.3 | async-start | bytes 5242880 | tf_op jit(solution)/shard_map/all_to_all | solution.py:513
  184.4 50.9 %all-reduce.5.cloned.1.call-done.hidden_ref = bf16[1280,768]{1,0:T(8,128)(2,1)} async-done(((bf16[1280,768]{1,0:T(8,128)(2,1)}), bf16[1280,768]{1,0:T(8,128)(2,1)}) %all-reduce.5.cloned.1.call-update) | async-done | bytes 1966096 | tf_op jit(solution)/shard_map/psum | solution.py:580
  235.3 9.1 %expert_rows.3 = (bf16[2560,384]{1,0:T(8,128)(2,1)}, bf16[2560,128]{1,0:T(8,128)(2,1)}) custom-call(bf16[1280,768]{1,0:T(8,128)(2,1)} %all-reduce.5.cloned.1.call-done.hidden_ref, bf16[1280,768]{1,0:T(8,128)(2,1)} %get-tuple-element.50.gate_ref, bf16[1280,768]{1,0:T(8,128)(2,1)} %get-tuple-element.51.up_ref, bf16[768,1024]{1,0:T(8,128)(2,1)} %bitcast.45, ...), custom_call_target="tpu_custom_call" | custom-call | flops 128849018880 | bytes 8519680 | tf_op jit(solution)/shard_map/expert_rows/pallas_call | solution.py:207
  244.4 1.5 copy-done.7
  245.9 10.7 %all-to-all-start.2 = ((bf16[64,40,384]{2,1,0:T(8,128)(2,1)}), bf16[64,40,384]{2,1,0:T(8,128)(2,1)S(1)}, u32[]{:S(2)}, u32[]{:S(2)}) async-start(bf16[64,40,384]{2,1,0:T(8,128)(2,1)} %bitcast.36), calls=%async_computation.2 | async-start | bytes 3932160 | tf_op jit(solution)/shard_map/all_to_all | solution.py:513
  256.9 2.1 constant_dynamic-slice_fusion.10
  259.3 2.0 collective-permute-start.1
  261.3 1.9 collective-permute-start.2
  263.2 1.0 broadcast_in_dim.24
  264.2 1.8 gt.20
  266.0 1.2 fusion.1.seen_ref
  268.9 1.0 copy.51
  270.9 1.8 chosen_rows.2.chosen_ref
  272.8 0.9 copy-done.5
  273.7 1.8 chosen_rows.3.chosen_ref
  275.5 1.0 constant_dynamic-update-slice_fusion.10
  276.5 1.0 constant_dynamic-update-slice_fusion.9
  277.5 1.0 constant_dynamic-update-slice_fusion.8.q_ref
  278.5 7.0 %attention_probs.1.probs_ref = f32[8,512,512]{2,1,0:T(8,128)} custom-call(bf16[512,1024]{1,0:T(8,128)(2,1)S(1)} %constant_dynamic-update-slice_fusion.8.q_ref, bf16[512,128]{1,0:T(8,128)(2,1)S(1)} %copy-done.4, f32[512,512]{1,0:T(8,128)S(1)} %copy-done.3), custom_call_target="tpu_custom_call" | custom-call | flops 536870912 | bytes 8388608 | tf_op jit(solution)/shard_map/attention_probs/pallas_call | solution.py:305
  285.5 4.4 %collect_rows.3.base_ref = f32[512,1024]{1,0:T(8,128)S(1)} custom-call(bf16[512,1280]{1,0:T(8,128)(2,1)} %chosen_rows.2.chosen_ref, bf16[2560,512]{1,0:T(8,128)(2,1)} %bitcast.31, bf16[512,1024]{1,0:T(8,128)(2,1)} %base_ref.1), custom_call_target="tpu_custom_call" | custom-call | flops 1342177280 | bytes 6815744 | tf_op jit(solution)/shard_map/collect_rows/pallas_call | solution.py:268
  289.9 1.4 copy-done.1
  291.2 11.4 %all-to-all-done.2 = bf16[64,40,384]{2,1,0:T(8,128)(2,1)S(1)} async-done(((bf16[64,40,384]{2,1,0:T(8,128)(2,1)}), bf16[64,40,384]{2,1,0:T(8,128)(2,1)S(1)}, u32[]{:S(2)}, u32[]{:S(2)}) %all-to-all-start.2) | async-done | bytes 1966112 | tf_op jit(solution)/shard_map/all_to_all | solution.py:513
  302.6 8.5 %all-to-all-start.4 = ((bf16[64,40,128]{2,1,0:T(8,128)(2,1)}), bf16[64,40,128]{2,1,0:T(8,128)(2,1)}, u32[]{:S(2)}, u32[]{:S(2)}) async-start(bf16[64,40,128]{2,1,0:T(8,128)(2,1)} %bitcast.19), calls=%async_computation.4 | async-start | bytes 1310720 | tf_op jit(solution)/shard_map/all_to_all | solution.py:513
  311.1 3.8 %collect_rows.5.grad_ref = bf16[512,768]{1,0:T(8,128)(2,1)S(1)} custom-call(bf16[512,1280]{1,0:T(8,128)(2,1)} %chosen_rows.3.chosen_ref, bf16[2560,384]{1,0:T(8,128)(2,1)S(1)} %bitcast.26, f32[512,1024]{1,0:T(8,128)} %copy-done.1), custom_call_target="tpu_custom_call" | custom-call | flops 1006632960 | bytes 5111808 | tf_op jit(solution)/shard_map/collect_rows/pallas_call | solution.py:268
  316.0 2.0 collective-permute-start.4
  318.0 1.9 collective-permute-start.5
  319.9 8.1 %first_grads.1 = (bf16[512,768]{1,0:T(8,128)(2,1)S(1)}, f32[512,128]{1,0:T(8,128)S(1)}, f32[512,128]{1,0:T(8,128)S(1)}) custom-call(f32[8,512,512]{2,1,0:T(8,128)} %attention_probs.1.probs_ref, bf16[512,768]{1,0:T(8,128)(2,1)S(1)} %collect_rows.5.grad_ref, bf16[512,1024]{1,0:T(8,128)(2,1)} %copy-done.2, ...), custom_call_target="tpu_custom_call" | custom-call | flops 1610612736 | bytes 6291456 | tf_op jit(solution)/shard_map/first_grads/pallas_call | solution.py:392
  328.3 2.2 collective-permute-start.7
  330.4 2.3 collective-permute-start.8
  332.8 2.5 collect_rows.4.grad_ref
  335.2 4.3 %last_grads.1 = bf16[512,768]{1,0:T(8,128)(2,1)} custom-call(f32[8,512,512]{2,1,0:T(8,128)} %attention_probs.1.probs_ref, bf16[512,256]{1,0:T(8,128)(2,1)S(1)} %collect_rows.4.grad_ref, bf16[512,1024]{1,0:T(8,128)(2,1)} %copy-done.2, bf16[512,128]{1,0:T(8,128)(2,1)S(1)} %constant_dynamic-slice_fusion.8.v_ref, bf16[128,512]{1,0:T(8,128)(2,1)S(1)} %bitcast.30, ...), custom_call_target="tpu_custom_call" | custom-call | flops 536870912 | bytes 2097152 | tf_op jit(solution)/shard_map/last_grads/pallas_call | solution.py:403
  340.9 3.9 %all-to-all-start.5 = ((bf16[4,128,768]{2,1,0:T(8,128)(2,1)}), bf16[4,128,768]{2,1,0:T(8,128)(2,1)S(1)}, u32[]{:S(2)}, u32[]{:S(2)}) async-start(bf16[4,128,768]{2,1,0:T(8,128)(2,1)} %bitcast.21), calls=%async_computation.5 | async-start | bytes 1572864 | tf_op jit(solution)/shard_map/all_to_all | solution.py:513
  345.1 1.0 constant_dynamic-update-slice_fusion.2
  346.3 1.0 constant_dynamic-update-slice_fusion
  347.3 9.7 %all-to-all-done.5.got_ref = bf16[4,128,768]{2,1,0:T(8,128)(2,1)S(1)} async-done(((bf16[4,128,768]{2,1,0:T(8,128)(2,1)}), bf16[4,128,768]{2,1,0:T(8,128)(2,1)S(1)}, u32[]{:S(2)}, u32[]{:S(2)}) %all-to-all-start.5) | async-done | bytes 786464 | tf_op jit(solution)/shard_map/all_to_all | solution.py:513
  356.9 1.5 finish.1
  (92 shorter events, 10.4 us)
Async XLA Ops:
  7.2 260.1 %copy-start = (bf16[512,256]{1,0:T(8,128)(2,1)S(1)}, bf16[512,256]{1,0:T(8,128)(2,1)}, u32[]{:S(2)}) copy-start(bf16[512,256]{1,0:T(8,128)(2,1)} %param.25) | copy-start | bytes 786436
  7.2 93.6 %all-gather.3.cloned.1.call-start = ((), (), s32[]{:S(2)}) async-start(), calls=%async_computation.8 | async-start | bytes 9830400 | tf_op jit(solution)/shard_map/all_gather | solution.py:546
  15.5 12.4 %copy-start.21 = (s32[512,4]{0,1:T(4,128)S(1)}, s32[512,4]{0,1:T(4,128)}, u32[]{:S(2)}) copy-start(s32[512,4]{0,1:T(4,128)} %param.17) | copy-start | bytes 24580
  15.5 12.5 %copy-start.22 = (s32[512,4]{0,1:T(4,128)S(1)}, s32[512,4]{0,1:T(4,128)}, u32[]{:S(2)}) copy-start(s32[512,4]{0,1:T(4,128)} %param.16) | copy-start | bytes 24580
  15.5 13.4 %copy-start.23 = (s32[512,4]{0,1:T(4,128)S(1)}, s32[512,4]{0,1:T(4,128)}, u32[]{:S(2)}) copy-start(s32[512,4]{0,1:T(4,128)} %param.15) | copy-start | bytes 24580
  15.5 72.2 %all-to-all-start = ((bf16[64,40,512]{2,1,0:T(8,128)(2,1)}), bf16[64,40,512]{2,1,0:T(8,128)(2,1)S(1)}, u32[]{:S(2)}, u32[]{:S(2)}) async-start(bf16[64,40,512]{2,1,0:T(8,128)(2,1)} %bitcast.35), calls=%async_computation | async-start | bytes 5242880 | tf_op jit(solution)/shard_map/all_to_all | solution.py:513
  27.8 131.9 %all-reduce.3.cloned.1.call-start = ((), (), s32[]{:S(2)}) async-start(), calls=%async_computation.6 | async-start | bytes 3932160 | tf_op jit(solution)/shard_map/psum | solution.py:572
  33.9 5.5 %copy-start.10 = (s32[512,4]{1,0:T(8,128)S(1)}, s32[512,4]{1,0:T(8,128)}, u32[]{:S(2)}) copy-start(s32[512,4]{1,0:T(8,128)} %copy.46) | copy-start | bytes 24580
  33.9 5.5 %copy-start.11 = (s32[512,4]{1,0:T(8,128)S(1)}, s32[512,4]{1,0:T(8,128)}, u32[]{:S(2)}) copy-start(s32[512,4]{1,0:T(8,128)} %copy.47) | copy-start | bytes 24580
  92.5 76.3 %all-to-all-start.1 = ((bf16[64,40,512]{2,1,0:T(8,128)(2,1)}), bf16[64,40,512]{2,1,0:T(8,128)(2,1)S(1)}, u32[]{:S(2)}, u32[]{:S(2)}) async-start(bf16[64,40,512]{2,1,0:T(8,128)(2,1)} %bitcast.33), calls=%async_computation.1 | async-start | bytes 5242880 | tf_op jit(solution)/shard_map/all_to_all | solution.py:513
  100.8 134.5 %all-reduce.5.cloned.1.call-start = ((), (), s32[]{:S(2)}) async-start(), calls=%async_computation.7 | async-start | bytes 3932160 | tf_op jit(solution)/shard_map/psum | solution.py:580
  173.6 70.8 %all-to-all-start.3 = ((bf16[64,40,512]{2,1,0:T(8,128)(2,1)}), bf16[64,40,512]{2,1,0:T(8,128)(2,1)S(1)}, u32[]{:S(2)}, u32[]{:S(2)}) async-start(bf16[64,40,512]{2,1,0:T(8,128)(2,1)} %bitcast.34), calls=%async_computation.3 | async-start | bytes 5242880 | tf_op jit(solution)/shard_map/all_to_all | solution.py:513
  244.4 1.5 copy-start.7
  245.9 56.7 %all-to-all-start.2 = ((bf16[64,40,384]{2,1,0:T(8,128)(2,1)}), bf16[64,40,384]{2,1,0:T(8,128)(2,1)S(1)}, u32[]{:S(2)}, u32[]{:S(2)}) async-start(bf16[64,40,384]{2,1,0:T(8,128)(2,1)} %bitcast.36), calls=%async_computation.2 | async-start | bytes 3932160 | tf_op jit(solution)/shard_map/all_to_all | solution.py:513
  256.7 6.5 %copy-start.24 = (s32[1,8,8]{2,1,0:T(8,128)S(1)}, s32[1,8,8]{2,1,0:T(8,128)}, u32[]{:S(2)}) copy-start(s32[1,8,8]{2,1,0:T(8,128)} %param.27) | copy-start | bytes 772
  259.0 16.6 %collective-permute-start = (bf16[128,1024]{1,0:T(8,128)(2,1)}, bf16[128,1024]{1,0:T(8,128)(2,1)}, u32[]{:S(2)}, u32[]{:S(2)}) collective-permute-start(bf16[128,1024]{1,0:T(8,128)(2,1)} %get-tuple-element.83), channel_id=1, source_target_pairs={{0,1},{1,2},{2,3},{3,0},{4,5},{5,6},{6,7},{7,4},{8,9},{9,10},{10,1... | collective-permute-start | bytes 786440 | tf_op jit(solution)/shard_map/ppermute | solution.py:423
  259.3 17.3 %collective-permute-start.1 = (bf16[128,1024]{1,0:T(8,128)(2,1)}, bf16[128,1024]{1,0:T(8,128)(2,1)}, u32[]{:S(2)}, u32[]{:S(2)}) collective-permute-start(bf16[128,1024]{1,0:T(8,128)(2,1)} %get-tuple-element.85), channel_id=1, source_target_pairs={{0,2},{1,3},{2,0},{3,1},{4,6},{5,7},{6,4},{7,5},{8,10},{9,11},{10,... | collective-permute-start | bytes 786440 | tf_op jit(solution)/shard_map/ppermute | solution.py:423
  261.3 16.2 %collective-permute-start.2 = (bf16[128,1024]{1,0:T(8,128)(2,1)}, bf16[128,1024]{1,0:T(8,128)(2,1)}, u32[]{:S(2)}, u32[]{:S(2)}) collective-permute-start(bf16[128,1024]{1,0:T(8,128)(2,1)} %get-tuple-element.82), channel_id=1, source_target_pairs={{0,3},{1,0},{2,1},{3,2},{4,7},{5,4},{6,5},{7,6},{8,11},{9,8},{10,9... | collective-permute-start | bytes 786440 | tf_op jit(solution)/shard_map/ppermute | solution.py:423
  270.0 1.0 copy-start.6
  272.8 0.9 copy-start.5
  273.7 4.8 %copy-start.3 = (f32[512,512]{1,0:T(8,128)S(1)}, f32[512,512]{1,0:T(8,128)}, u32[]{:S(2)}) copy-start(f32[512,512]{1,0:T(8,128)} %fusion.1.seen_ref) | copy-start | bytes 3145732
  273.7 4.8 %copy-start.4 = (bf16[512,128]{1,0:T(8,128)(2,1)S(1)}, bf16[512,128]{1,0:T(8,128)(2,1)}, u32[]{:S(2)}) copy-start(bf16[512,128]{1,0:T(8,128)(2,1)} %constant_dynamic-slice_fusion.9.k_ref) | copy-start | bytes 393220
  278.5 7.0 %copy-start.2 = (bf16[512,1024]{1,0:T(8,128)(2,1)}, bf16[512,1024]{1,0:T(8,128)(2,1)S(1)}, u32[]{:S(2)}) copy-start(bf16[512,1024]{1,0:T(8,128)(2,1)S(1)} %constant_dynamic-update-slice_fusion.8.q_ref) | copy-start | bytes 3145732
  289.9 1.4 copy-start.1
  302.6 30.1 %all-to-all-start.4 = ((bf16[64,40,128]{2,1,0:T(8,128)(2,1)}), bf16[64,40,128]{2,1,0:T(8,128)(2,1)}, u32[]{:S(2)}, u32[]{:S(2)}) async-start(bf16[64,40,128]{2,1,0:T(8,128)(2,1)} %bitcast.19), calls=%async_computation.4 | async-start | bytes 1310720 | tf_op jit(solution)/shard_map/all_to_all | solution.py:513
  315.7 14.7 %collective-permute-start.3 = (bf16[128,768]{1,0:T(8,128)(2,1)S(1)}, bf16[128,768]{1,0:T(8,128)(2,1)S(1)}, u32[]{:S(2)}, u32[]{:S(2)}) collective-permute-start(bf16[128,768]{1,0:T(8,128)(2,1)S(1)} %get-tuple-element.92), channel_id=1, source_target_pairs={{0,1},{1,2},{2,3},{3,0},{4,5},{5,6},{6,7},{7,4},{8,9},{9,10},{10,1... | collective-permute-start | bytes 589832 | tf_op jit(solution)/shard_map/ppermute | solution.py:423
  316.0 23.5 %collective-permute-start.4 = (bf16[128,768]{1,0:T(8,128)(2,1)S(1)}, bf16[128,768]{1,0:T(8,128)(2,1)S(1)}, u32[]{:S(2)}, u32[]{:S(2)}) collective-permute-start(bf16[128,768]{1,0:T(8,128)(2,1)S(1)} %get-tuple-element.91), channel_id=1, source_target_pairs={{0,2},{1,3},{2,0},{3,1},{4,6},{5,7},{6,4},{7,5},{8,10},{9,11},{10,... | collective-permute-start | bytes 589832 | tf_op jit(solution)/shard_map/ppermute | solution.py:423
  318.0 21.5 %collective-permute-start.5 = (bf16[128,768]{1,0:T(8,128)(2,1)S(1)}, bf16[128,768]{1,0:T(8,128)(2,1)}, u32[]{:S(2)}, u32[]{:S(2)}) collective-permute-start(bf16[128,768]{1,0:T(8,128)(2,1)S(1)} %get-tuple-element.90), channel_id=1, source_target_pairs={{0,3},{1,0},{2,1},{3,2},{4,7},{5,4},{6,5},{7,6},{8,11},{9,8},{10,9... | collective-permute-start | bytes 589832 | tf_op jit(solution)/shard_map/ppermute | solution.py:423
  328.0 11.7 %collective-permute-start.6 = (bf16[128,768]{1,0:T(8,128)(2,1)S(1)}, bf16[128,768]{1,0:T(8,128)(2,1)}, u32[]{:S(2)}, u32[]{:S(2)}) collective-permute-start(bf16[128,768]{1,0:T(8,128)(2,1)S(1)} %get-tuple-element.88), channel_id=1, source_target_pairs={{0,1},{1,2},{2,3},{3,0},{4,5},{5,6},{6,7},{7,4},{8,9},{9,10},{10,1... | collective-permute-start | bytes 589832 | tf_op jit(solution)/shard_map/ppermute | solution.py:423
  328.3 11.5 %collective-permute-start.7 = (bf16[128,768]{1,0:T(8,128)(2,1)S(1)}, bf16[128,768]{1,0:T(8,128)(2,1)S(1)}, u32[]{:S(2)}, u32[]{:S(2)}) collective-permute-start(bf16[128,768]{1,0:T(8,128)(2,1)S(1)} %get-tuple-element.87), channel_id=1, source_target_pairs={{0,2},{1,3},{2,0},{3,1},{4,6},{5,7},{6,4},{7,5},{8,10},{9,11},{10,... | collective-permute-start | bytes 589832 | tf_op jit(solution)/shard_map/ppermute | solution.py:423
  330.4 4.8 %copy-start.15 = (bf16[128,768]{1,0:T(8,128)(2,1)}, bf16[128,768]{1,0:T(8,128)(2,1)S(1)}, u32[]{:S(2)}) copy-start(bf16[128,768]{1,0:T(8,128)(2,1)S(1)} %collective-permute-done.3) | copy-start | bytes 589828
  330.4 9.8 %collective-permute-start.8 = (bf16[128,768]{1,0:T(8,128)(2,1)S(1)}, bf16[128,768]{1,0:T(8,128)(2,1)S(1)}, u32[]{:S(2)}, u32[]{:S(2)}) collective-permute-start(bf16[128,768]{1,0:T(8,128)(2,1)S(1)} %get-tuple-element.86), channel_id=1, source_target_pairs={{0,3},{1,0},{2,1},{3,2},{4,7},{5,4},{6,5},{7,6},{8,11},{9,8},{10,9... | collective-permute-start | bytes 589832 | tf_op jit(solution)/shard_map/ppermute | solution.py:423
  339.5 0.7 copy-start.13
  339.8 0.7 copy-start.17
  340.2 0.7 copy-start.19
  340.2 4.9 %copy-start.12 = (bf16[128,768]{1,0:T(8,128)(2,1)S(1)}, bf16[128,768]{1,0:T(8,128)(2,1)}, u32[]{:S(2)}) copy-start(bf16[128,768]{1,0:T(8,128)(2,1)} %get-tuple-element.70) | copy-start | bytes 589828
  340.9 16.0 %all-to-all-start.5 = ((bf16[4,128,768]{2,1,0:T(8,128)(2,1)}), bf16[4,128,768]{2,1,0:T(8,128)(2,1)S(1)}, u32[]{:S(2)}, u32[]{:S(2)}) async-start(bf16[4,128,768]{2,1,0:T(8,128)(2,1)} %bitcast.21), calls=%async_computation.5 | async-start | bytes 1572864 | tf_op jit(solution)/shard_map/all_to_all | solution.py:513
  344.8 1.3 copy-start.16
  344.8 1.3 copy-start.18
  344.9 1.4 copy-start.14
  345.0 1.3 copy-start.20
  347.2 9.7 %copy-start.8 = (bf16[128,4096]{1,0:T(8,128)(2,1)}, bf16[128,4096]{1,0:T(8,128)(2,1)S(1)}, u32[]{:S(2)}) copy-start(bf16[128,4096]{1,0:T(8,128)(2,1)S(1)} %get-tuple-element.95.refs_0_) | copy-start | bytes 3145732
  347.2 9.7 %copy-start.9 = (bf16[128,4096]{1,0:T(8,128)(2,1)}, bf16[128,4096]{1,0:T(8,128)(2,1)S(1)}, u32[]{:S(2)}) copy-start(bf16[128,4096]{1,0:T(8,128)(2,1)S(1)} %get-tuple-element.94.refs_1_) | copy-start | bytes 3145732
Sparse Core Ops, SparseCore 0:
  10.3 84.2 all-gather.2
  97.0 62.6 all-reduce.2
  173.7 61.5 all-reduce.4

commit v4 on v3

--- a/solution.py
+++ b/solution.py
@@ -150,13 +150,12 @@
     )(*stay(weights))
 
 
-def down_rows_kernel(rows_ref, down_ref, out_ref, wide):
-    half = rows_ref.shape[1]
+def down_rows_kernel(rows_ref, low_ref, high_ref, out_ref, wide):
     low, high = unweave(rows_ref, wide)
-    for start in range(0, down_ref.shape[1], DOWN_COLS):
+    for start in range(0, out_ref.shape[1], DOWN_COLS):
         cols = slice(start, start + DOWN_COLS)
-        total = jnp.dot(low, down_ref[:half, cols], preferred_element_type=f32)
-        total = total + jnp.dot(high, down_ref[half:, cols], preferred_element_type=f32)
+        total = jnp.dot(low, low_ref[:, cols], preferred_element_type=f32)
+        total = total + jnp.dot(high, high_ref[:, cols], preferred_element_type=f32)
         out_ref[:, cols] = total.astype(bf16)
 
 
@@ -169,7 +168,8 @@
         grid=(PROJECT_STEPS,),
         in_specs=[
             pl.BlockSpec((2 * step, half), lambda i: (i, 0)),
-            pl.BlockSpec(down_t.shape, lambda i: (0, 0)),
+            pl.BlockSpec((half, hidden), lambda i: (0, 0)),
+            pl.BlockSpec((half, hidden), lambda i: (1, 0)),
         ],
         out_specs=pl.BlockSpec((step, hidden), lambda i: (i, 0)),
         out_shape=pltpu.HBM((rows, hidden), bf16),
@@ -177,10 +177,11 @@
         compiler_params=params(SMALL_VMEM),
         cost_estimate=cost(2 * rows * width * hidden, 2 * rows * (width + hidden)),
         name="project_down",
-    )(arrived, *stay(down_t))
-
-
-def expert_kernel(hidden_ref, gate_ref, up_ref, wg_ref, wu_ref, *refs):
+    )(arrived, *stay(down_t, down_t))
+
+
+def expert_kernel(hidden_ref, gate_ref, up_ref, *refs):
+    weights, refs = refs[:4], refs[4:]
     outs, wides = refs[: len(refs) // 2], refs[len(refs) // 2 :]
     grad = hidden_ref[...].astype(f32)
     gate = gate_ref[...].astype(f32)
@@ -189,8 +190,12 @@
     shared = grad * sig
     gate_grad = (shared * up * (1.0 + gate * (1.0 - sig))).astype(bf16)
     up_grad = (shared * gate).astype(bf16)
-    total = jnp.dot(gate_grad, wg_ref[...], preferred_element_type=f32)
-    total = total + jnp.dot(up_grad, wu_ref[...], preferred_element_type=f32)
+    halves = [
+        jnp.dot(gate_grad, wg_ref[...], preferred_element_type=f32)
+        + jnp.dot(up_grad, wu_ref[...], preferred_element_type=f32)
+        for wg_ref, wu_ref in (weights[:2], weights[2:])
+    ]
+    total = jnp.concatenate(halves, axis=1)
     start = 0
     for out_ref, wide in zip(outs, wides):
         half = out_ref.shape[1]
@@ -203,11 +208,11 @@
     rows, hidden = hidden_grad.shape
     step, width = rows // STEPS, sum(widths)
     row_block = pl.BlockSpec((step, hidden), lambda i: (i, 0))
-    whole = pl.BlockSpec(w_gate.shape, lambda i: (0, 0))
+    halves = [pl.BlockSpec((hidden, width // 2), lambda i, j=j: (0, j)) for j in (0, 0, 1, 1)]
     return pl.pallas_call(
         expert_kernel,
         grid=(STEPS,),
-        in_specs=[row_block, row_block, row_block, whole, whole],
+        in_specs=[row_block, row_block, row_block] + halves,
         out_specs=[pl.BlockSpec((2 * step, w // 2), lambda i: (i, 0)) for w in widths],
         out_shape=[jax.ShapeDtypeStruct((2 * rows, w // 2), bf16) for w in widths],
         scratch_shapes=[woven(step, w // 2) for w in widths],
@@ -216,7 +221,7 @@
             128 * rows * hidden * width, 2 * rows * (3 * hidden + width), rows * hidden
         ),
         name="expert_rows",
-    )(hidden_grad, gate, up, w_gate, w_up)
+    )(hidden_grad, gate, up, w_gate, w_up, w_gate, w_up)
 
 
 def chosen_kernel(slots_ref, out_ref):
@@ -322,14 +327,14 @@
     )(queries, keys, seen)
 
 
-def head_grads(probs_ref, grad_ref, q_ref, v_ref, kt_ref, out_ref, sum_k, sum_v):
+def head_grads(probs_refs, grad_ref, q_ref, v_ref, kt_ref, out_ref, sum_k, sum_v):
     length = q_ref.shape[0]
     block = length // 2
     scale = HEAD_DIM ** (-0.5)
     for part in range(2):
         keys = (part + 1) * block
         cols = slice(part * block, (part + 1) * block)
-        probs = probs_ref[0, :keys, cols]
+        probs = probs_refs[part][0]
         grad = grad_ref[cols, :]
         prob_grad = lax.dot_general(
             v_ref[:keys, :], grad, (((1,), (1,)), ((), ())), preferred_element_type=f32
@@ -342,17 +347,19 @@
         sum_v[:keys, :] += jnp.dot(probs.astype(bf16), grad, preferred_element_type=f32)
 
 
-def first_grads_kernel(probs_ref, grad_ref, q_ref, v_ref, kt_ref, out_ref, sum_k, sum_v):
+def first_grads_kernel(
+    early_ref, late_ref, grad_ref, q_ref, v_ref, kt_ref, out_ref, sum_k, sum_v
+):
     @pl.when(pl.program_id(0) == 0)
     def _():
         sum_k[...] = jnp.zeros_like(sum_k)
         sum_v[...] = jnp.zeros_like(sum_v)
 
-    head_grads(probs_ref, grad_ref, q_ref, v_ref, kt_ref, out_ref, sum_k, sum_v)
+    head_grads((early_ref, late_ref), grad_ref, q_ref, v_ref, kt_ref, out_ref, sum_k, sum_v)
 
 
 def last_grads_kernel(
-    probs_ref, grad_ref, q_ref, v_ref, kt_ref, old_k, old_v, out_ref, sum_k, sum_v
+    early_ref, late_ref, grad_ref, q_ref, v_ref, kt_ref, old_k, old_v, out_ref, sum_k, sum_v
 ):
     head, heads = pl.program_id(0), pl.num_programs(0)
     scale = HEAD_DIM ** (-0.5)
@@ -366,7 +373,7 @@
     out_ref[:, pl.ds(first, HEAD_DIM)] = grad_ref[...]
     first = pl.multiple_of((head + heads + 2) * HEAD_DIM, HEAD_DIM)
     out = out_ref.at[:, pl.ds(first, HEAD_DIM)]
-    head_grads(probs_ref, grad_ref, q_ref, v_ref, kt_ref, out, sum_k, sum_v)
+    head_grads((early_ref, late_ref), grad_ref, q_ref, v_ref, kt_ref, out, sum_k, sum_v)
 
     @pl.when(head == heads - 1)
     def _():
@@ -380,14 +387,15 @@
     totals = [jax.ShapeDtypeStruct((length, HEAD_DIM), f32)] * 2
     out_spec = pl.BlockSpec((length, HEAD_DIM), lambda h: (0, h))
     in_specs = [
-        pl.BlockSpec((1, length, length), lambda h: (first + h, 0, 0)),
+        pl.BlockSpec((1, length // 2, length // 2), lambda h: (first + h, 0, 0)),
+        pl.BlockSpec((1, length, length // 2), lambda h: (first + h, 0, 1)),
         out_spec,
         pl.BlockSpec((length, HEAD_DIM), lambda h: (0, first + h)),
         whole,
         pl.BlockSpec(keys_t.shape, lambda h: (0, 0)),
     ]
     estimate = cost(8 * heads * length * length * HEAD_DIM, 4 * heads * length * length)
-    operands = (*stay(probs), out_grad, *stay(queries), values, keys_t)
+    operands = (*stay(probs, probs), out_grad, *stay(queries), values, keys_t)
     if sums is None:
         return pl.pallas_call(
             first_grads_kernel,

time: 367 us -> 366 us (level)
  transfers between devices with their start and end apart: 18 -> 18, of which waited for: 7 -> 7; matrix products, arithmetic and copies ran while one was open for 5% -> 5% of each run, Pallas kernels for 22% -> 21%
where the time goes in v4:
time: 366 us; the launch traced here: 364 us
  waiting for transfers between devices  170 us (46%)
  Pallas kernels  84.6 us (23%)
  starting transfers between devices  67.6 us (18%)
  local copies, waits for them, and re-layouts  21.4 us (6%)
  between operations  14.3 us (4%)
  other arithmetic  6.07 us (2%)
    all_to_all x6, waiting for transfers between devices, swap(): return lax.all_to_all(rows, axis, split_axis=0, concat_axis=0, tiled=True)  67.5 us
    all_to_all x6, starting transfers between devices, swap(): return lax.all_to_all(rows, axis, split_axis=0, concat_axis=0, tiled=True)  54.5 us
    psum x1, waiting for transfers between devices, on_device(): hidden_grad = lax.psum(first_sum, 'cp')  51 us
    psum x1, waiting for transfers between devices, on_device(): later_grad = lax.psum(later_sum, 'cp', axis_index_groups=back)  50.9 us
    pallas_call x2, Pallas kernels, expert_rows(): pl.pallas_call(expert_kernel, grid=(STEPS,), in_specs=[row_block, row_blo...  18 us
    ppermute x9, starting transfers between devices, pass_round(): lax.ppermute(piece, 'cp', [(i, (i + shift) % parts) for i in range(parts)])  13 us
    pallas_call x2, Pallas kernels, send_rows(): pl.pallas_call(functools.partial(route_rows, part, capacity), grid=(STEPS...  10.7 us
    pallas_call x3, Pallas kernels, collect_rows(): pl.pallas_call(collect_kernel, grid=(CHOSEN_STEPS,), in_specs=[pl.BlockSp...  10.7 us
  transfers between devices with their start and end apart: 18, of which 7 were waited for; matrix products, arithmetic and copies ran while one was open for 5% of the time, Pallas kernels for 21%

profile of v4, /device:TPU:6, one launch (start us, length us, event | category | flops | bytes accessed | tf_op | source)
XLA Modules:
  0.0 364.4 jit_solution(2590997021538958271)
XLA Ops:
  7.2 3.0 pad_maximum_fusion
  10.2 5.2 %send_rows.2 = bf16[2560,512]{1,0:T(8,128)(2,1)} custom-call(s32[4,512]{1,0:T(4,128)} %bitcast.42, s32[4,512]{1,0:T(4,128)} %bitcast.40, s32[4,512]{1,0:T(4,128)} %bitcast.38, f32[4,512]{1,0:T(4,128)} %bitcast.52, bf16[512,1024]{1,0:T(8,128)(2,1)} %base_ref.1), custom_call_target="tpu_custom_call" | custom-call | flops 1342177280 | bytes 5242880 | tf_op jit(solution)/shard_map/send_rows/pallas_call | solution.py:90
  15.5 12.3 %all-to-all-start = ((bf16[64,40,512]{2,1,0:T(8,128)(2,1)}), bf16[64,40,512]{2,1,0:T(8,128)(2,1)S(1)}, u32[]{:S(2)}, u32[]{:S(2)}) async-start(bf16[64,40,512]{2,1,0:T(8,128)(2,1)} %bitcast.35), calls=%async_computation | async-start | bytes 5242880 | tf_op jit(solution)/shard_map/all_to_all | solution.py:521
  30.1 3.8 %turn_weights.1.low_ref.high_ref = bf16[1024,768]{1,0:T(8,128)(2,1)} custom-call(bf16[768,1024]{1,0:T(8,128)(2,1)} %bitcast.37), custom_call_target="tpu_custom_call" | custom-call | flops 786432 | bytes 3145728 | tf_op jit(solution)/shard_map/turn_weights/pallas_call | solution.py:141
  33.9 5.5 %send_rows.3 = bf16[2560,512]{1,0:T(8,128)(2,1)} custom-call(s32[4,512]{1,0:T(4,128)} %bitcast.43, s32[4,512]{1,0:T(4,128)} %bitcast.41, s32[4,512]{1,0:T(4,128)} %bitcast.39, f32[4,512]{1,0:T(4,128)} %bitcast.53, bf16[512,1024]{1,0:T(8,128)(2,1)} %base_ref.1), custom_call_target="tpu_custom_call" | custom-call | flops 1342177280 | bytes 5242880 | tf_op jit(solution)/shard_map/send_rows/pallas_call | solution.py:90
  41.2 46.5 %all-to-all-done = bf16[64,40,512]{2,1,0:T(8,128)(2,1)S(1)} async-done(((bf16[64,40,512]{2,1,0:T(8,128)(2,1)}), bf16[64,40,512]{2,1,0:T(8,128)(2,1)S(1)}, u32[]{:S(2)}, u32[]{:S(2)}) %all-to-all-start) | async-done | bytes 2621472 | tf_op jit(solution)/shard_map/all_to_all | solution.py:521
  87.7 4.8 %project_down.2 = bf16[1280,768]{1,0:T(8,128)(2,1)} custom-call(bf16[2560,512]{1,0:T(8,128)(2,1)S(1)} %bitcast.26, bf16[1024,768]{1,0:T(8,128)(2,1)} %turn_weights.1.low_ref.high_ref, bf16[1024,768]{1,0:T(8,128)(2,1)} %turn_weights.1.low_ref.high_ref), custom_call_target="tpu_custom_call" | custom-call | flops 2013265920 | bytes 4587520 | tf_op jit(solution)/shard_map/project_down/pallas_call | solution.py:166
  92.5 8.3 %all-to-all-start.1 = ((bf16[64,40,512]{2,1,0:T(8,128)(2,1)}), bf16[64,40,512]{2,1,0:T(8,128)(2,1)S(1)}, u32[]{:S(2)}, u32[]{:S(2)}) async-start(bf16[64,40,512]{2,1,0:T(8,128)(2,1)} %bitcast.33), calls=%async_computation.1 | async-start | bytes 5242880 | tf_op jit(solution)/shard_map/all_to_all | solution.py:521
  100.8 7.8 %turn_saved.1 = (bf16[1280,768]{1,0:T(8,128)(2,1)}, bf16[1280,768]{1,0:T(8,128)(2,1)}, bf16[1280,768]{1,0:T(8,128)(2,1)}, bf16[1280,768]{1,0:T(8,128)(2,1)}) custom-call(bf16[4,2,192,2560]{3,2,1,0:T(8,128)(2,1)} %bitcast.32), custom_call_target="tpu_custom_call" | custom-call | flops 3932160 | bytes 15728640 | tf_op jit(solution)/shard_map/turn_saved/pallas_call | solution.py:121
  108.6 51.0 %all-reduce.3.cloned.1.call-done.hidden_ref = bf16[1280,768]{1,0:T(8,128)(2,1)} async-done(((bf16[1280,768]{1,0:T(8,128)(2,1)}), bf16[1280,768]{1,0:T(8,128)(2,1)}) %all-reduce.3.cloned.1.call-update) | async-done | bytes 1966096 | tf_op jit(solution)/shard_map/psum | solution.py:580
  159.7 9.0 %expert_rows.2 = bf16[2560,512]{1,0:T(8,128)(2,1)} custom-call(bf16[1280,768]{1,0:T(8,128)(2,1)} %all-reduce.3.cloned.1.call-done.hidden_ref, bf16[1280,768]{1,0:T(8,128)(2,1)} %get-tuple-element.45.gate_ref, bf16[1280,768]{1,0:T(8,128)(2,1)} %get-tuple-element.46.up_ref, bf16[768,1024]{1,0:T(8,128)(2,1)} %bitcast.44, bf16[768,1024]{1,0:T(8,128)(2,1)} %bitcast.48, ...), custom_call_target="tpu_custom_call" | custom-call | flops 128849018880 | bytes 8519680 | tf_op jit(solution)/shard_map/expert_rows/pallas_call | solution.py:212
  168.7 4.7 %project_down.3 = bf16[1280,768]{1,0:T(8,128)(2,1)} custom-call(bf16[2560,512]{1,0:T(8,128)(2,1)S(1)} %bitcast.27, bf16[1024,768]{1,0:T(8,128)(2,1)} %turn_weights.1.low_ref.high_ref, bf16[1024,768]{1,0:T(8,128)(2,1)} %turn_weights.1.low_ref.high_ref), custom_call_target="tpu_custom_call" | custom-call | flops 2013265920 | bytes 4587520 | tf_op jit(solution)/shard_map/project_down/pallas_call | solution.py:166
  173.4 10.7 %all-to-all-start.3 = ((bf16[64,40,512]{2,1,0:T(8,128)(2,1)}), bf16[64,40,512]{2,1,0:T(8,128)(2,1)S(1)}, u32[]{:S(2)}, u32[]{:S(2)}) async-start(bf16[64,40,512]{2,1,0:T(8,128)(2,1)} %bitcast.34), calls=%async_computation.3 | async-start | bytes 5242880 | tf_op jit(solution)/shard_map/all_to_all | solution.py:521
  184.2 50.9 %all-reduce.5.cloned.1.call-done.hidden_ref = bf16[1280,768]{1,0:T(8,128)(2,1)} async-done(((bf16[1280,768]{1,0:T(8,128)(2,1)}), bf16[1280,768]{1,0:T(8,128)(2,1)}) %all-reduce.5.cloned.1.call-update) | async-done | bytes 1966096 | tf_op jit(solution)/shard_map/psum | solution.py:588
  235.1 9.0 %expert_rows.3 = (bf16[2560,384]{1,0:T(8,128)(2,1)}, bf16[2560,128]{1,0:T(8,128)(2,1)}) custom-call(bf16[1280,768]{1,0:T(8,128)(2,1)} %all-reduce.5.cloned.1.call-done.hidden_ref, bf16[1280,768]{1,0:T(8,128)(2,1)} %get-tuple-element.50.gate_ref, bf16[1280,768]{1,0:T(8,128)(2,1)} %get-tuple-element.51.up_ref, bf16[768,1024]{1,0:T(8,128)(2,1)} %bitcast.46, ...), custom_call_target="tpu_custom_call" | custom-call | flops 128849018880 | bytes 8519680 | tf_op jit(solution)/shard_map/expert_rows/pallas_call | solution.py:212
  244.1 1.5 copy-done.7
  245.7 10.7 %all-to-all-start.2 = ((bf16[64,40,384]{2,1,0:T(8,128)(2,1)}), bf16[64,40,384]{2,1,0:T(8,128)(2,1)S(1)}, u32[]{:S(2)}, u32[]{:S(2)}) async-start(bf16[64,40,384]{2,1,0:T(8,128)(2,1)} %bitcast.36), calls=%async_computation.2 | async-start | bytes 3932160 | tf_op jit(solution)/shard_map/all_to_all | solution.py:521
  256.6 2.1 constant_dynamic-slice_fusion.10
  259.0 2.0 collective-permute-start.1
  261.0 1.9 collective-permute-start.2
  263.0 1.0 broadcast_in_dim.24
  264.0 1.8 gt.20
  265.8 1.2 fusion.1.seen_ref
  268.7 1.0 copy.51
  270.6 1.8 chosen_rows.2.chosen_ref
  272.5 0.9 copy-done.5
  273.4 1.8 chosen_rows.3.chosen_ref
  275.3 1.0 constant_dynamic-update-slice_fusion.10
  276.3 1.0 constant_dynamic-update-slice_fusion.9
  277.2 1.0 constant_dynamic-update-slice_fusion.8.q_ref
  278.3 7.0 %attention_probs.1.early_ref.late_ref = f32[8,512,512]{2,1,0:T(8,128)} custom-call(bf16[512,1024]{1,0:T(8,128)(2,1)S(1)} %constant_dynamic-update-slice_fusion.8.q_ref, bf16[512,128]{1,0:T(8,128)(2,1)S(1)} %copy-done.4, f32[512,512]{1,0:T(8,128)S(1)} %copy-done.3), custom_call_target="tpu_custom_call" | custom-call | flops 536870912 | bytes 8388608 | tf_op jit(solution)/shard_map/attention_probs/pallas_call | solution.py:310
  285.2 4.4 %collect_rows.3.base_ref = f32[512,1024]{1,0:T(8,128)S(1)} custom-call(bf16[512,1280]{1,0:T(8,128)(2,1)} %chosen_rows.2.chosen_ref, bf16[2560,512]{1,0:T(8,128)(2,1)} %bitcast.31, bf16[512,1024]{1,0:T(8,128)(2,1)} %base_ref.1), custom_call_target="tpu_custom_call" | custom-call | flops 1342177280 | bytes 6815744 | tf_op jit(solution)/shard_map/collect_rows/pallas_call | solution.py:273
  289.6 1.4 copy-done.1
  290.9 11.4 %all-to-all-done.2 = bf16[64,40,384]{2,1,0:T(8,128)(2,1)S(1)} async-done(((bf16[64,40,384]{2,1,0:T(8,128)(2,1)}), bf16[64,40,384]{2,1,0:T(8,128)(2,1)S(1)}, u32[]{:S(2)}, u32[]{:S(2)}) %all-to-all-start.2) | async-done | bytes 1966112 | tf_op jit(solution)/shard_map/all_to_all | solution.py:521
  302.3 8.5 %all-to-all-start.4 = ((bf16[64,40,128]{2,1,0:T(8,128)(2,1)}), bf16[64,40,128]{2,1,0:T(8,128)(2,1)}, u32[]{:S(2)}, u32[]{:S(2)}) async-start(bf16[64,40,128]{2,1,0:T(8,128)(2,1)} %bitcast.19), calls=%async_computation.4 | async-start | bytes 1310720 | tf_op jit(solution)/shard_map/all_to_all | solution.py:521
  310.9 3.8 %collect_rows.5.grad_ref = bf16[512,768]{1,0:T(8,128)(2,1)S(1)} custom-call(bf16[512,1280]{1,0:T(8,128)(2,1)} %chosen_rows.3.chosen_ref, bf16[2560,384]{1,0:T(8,128)(2,1)S(1)} %bitcast.28, f32[512,1024]{1,0:T(8,128)} %copy-done.1), custom_call_target="tpu_custom_call" | custom-call | flops 1006632960 | bytes 5111808 | tf_op jit(solution)/shard_map/collect_rows/pallas_call | solution.py:273
  315.8 2.0 collective-permute-start.4
  317.8 1.9 collective-permute-start.5
  319.6 7.7 %first_grads.1 = (bf16[512,768]{1,0:T(8,128)(2,1)S(1)}, f32[512,128]{1,0:T(8,128)S(1)}, f32[512,128]{1,0:T(8,128)S(1)}) custom-call(f32[8,512,512]{2,1,0:T(8,128)} %attention_probs.1.early_ref.late_ref, f32[8,512,512]{2,1,0:T(8,128)} %attention_probs.1.early_ref.late_ref, bf16[512,768]{1,0:T(8,128)(2,1)S(1)} %collect_rows.5.grad_ref, ...), custom_call_target="tpu_custom_call" | custom-call | flops 1610612736 | bytes 6291456 | tf_op jit(solution)/shard_map/first_grads/pallas_call | solution.py:400
  327.7 2.2 collective-permute-start.7
  329.8 2.3 collective-permute-start.8
  332.2 2.5 collect_rows.4.grad_ref
  334.6 4.2 %last_grads.1 = bf16[512,768]{1,0:T(8,128)(2,1)} custom-call(f32[8,512,512]{2,1,0:T(8,128)} %attention_probs.1.early_ref.late_ref, f32[8,512,512]{2,1,0:T(8,128)} %attention_probs.1.early_ref.late_ref, bf16[512,256]{1,0:T(8,128)(2,1)S(1)} %collect_rows.4.grad_ref, bf16[512,1024]{1,0:T(8,128)(2,1)} %copy-done.2, ...), custom_call_target="tpu_custom_call" | custom-call | flops 536870912 | bytes 2097152 | tf_op jit(solution)/shard_map/last_grads/pallas_call | solution.py:411
  340.3 3.9 %all-to-all-start.5 = ((bf16[4,128,768]{2,1,0:T(8,128)(2,1)}), bf16[4,128,768]{2,1,0:T(8,128)(2,1)S(1)}, u32[]{:S(2)}, u32[]{:S(2)}) async-start(bf16[4,128,768]{2,1,0:T(8,128)(2,1)} %bitcast.21), calls=%async_computation.5 | async-start | bytes 1572864 | tf_op jit(solution)/shard_map/all_to_all | solution.py:521
  344.5 1.0 constant_dynamic-update-slice_fusion.2
  345.7 1.0 constant_dynamic-update-slice_fusion
  346.7 9.7 %all-to-all-done.5.got_ref = bf16[4,128,768]{2,1,0:T(8,128)(2,1)S(1)} async-done(((bf16[4,128,768]{2,1,0:T(8,128)(2,1)}), bf16[4,128,768]{2,1,0:T(8,128)(2,1)S(1)}, u32[]{:S(2)}, u32[]{:S(2)}) %all-to-all-start.5) | async-done | bytes 786464 | tf_op jit(solution)/shard_map/all_to_all | solution.py:521
  356.3 1.5 finish.1
  (92 shorter events, 10.5 us)
Async XLA Ops:
  7.2 259.8 %copy-start = (bf16[512,256]{1,0:T(8,128)(2,1)S(1)}, bf16[512,256]{1,0:T(8,128)(2,1)}, u32[]{:S(2)}) copy-start(bf16[512,256]{1,0:T(8,128)(2,1)} %param.25) | copy-start | bytes 786436
  7.2 93.6 %all-gather.3.cloned.1.call-start = ((), (), s32[]{:S(2)}) async-start(), calls=%async_computation.8 | async-start | bytes 9830400 | tf_op jit(solution)/shard_map/all_gather | solution.py:554
  15.5 12.4 %copy-start.21 = (s32[512,4]{0,1:T(4,128)S(1)}, s32[512,4]{0,1:T(4,128)}, u32[]{:S(2)}) copy-start(s32[512,4]{0,1:T(4,128)} %param.17) | copy-start | bytes 24580
  15.5 12.5 %copy-start.22 = (s32[512,4]{0,1:T(4,128)S(1)}, s32[512,4]{0,1:T(4,128)}, u32[]{:S(2)}) copy-start(s32[512,4]{0,1:T(4,128)} %param.16) | copy-start | bytes 24580
  15.5 13.4 %copy-start.23 = (s32[512,4]{0,1:T(4,128)S(1)}, s32[512,4]{0,1:T(4,128)}, u32[]{:S(2)}) copy-start(s32[512,4]{0,1:T(4,128)} %param.15) | copy-start | bytes 24580
  15.5 72.2 %all-to-all-start = ((bf16[64,40,512]{2,1,0:T(8,128)(2,1)}), bf16[64,40,512]{2,1,0:T(8,128)(2,1)S(1)}, u32[]{:S(2)}, u32[]{:S(2)}) async-start(bf16[64,40,512]{2,1,0:T(8,128)(2,1)} %bitcast.35), calls=%async_computation | async-start | bytes 5242880 | tf_op jit(solution)/shard_map/all_to_all | solution.py:521
  27.8 131.9 %all-reduce.3.cloned.1.call-start = ((), (), s32[]{:S(2)}) async-start(), calls=%async_computation.6 | async-start | bytes 3932160 | tf_op jit(solution)/shard_map/psum | solution.py:580
  33.9 5.5 %copy-start.10 = (s32[512,4]{1,0:T(8,128)S(1)}, s32[512,4]{1,0:T(8,128)}, u32[]{:S(2)}) copy-start(s32[512,4]{1,0:T(8,128)} %copy.46) | copy-start | bytes 24580
  33.9 5.5 %copy-start.11 = (s32[512,4]{1,0:T(8,128)S(1)}, s32[512,4]{1,0:T(8,128)}, u32[]{:S(2)}) copy-start(s32[512,4]{1,0:T(8,128)} %copy.47) | copy-start | bytes 24580
  92.5 76.2 %all-to-all-start.1 = ((bf16[64,40,512]{2,1,0:T(8,128)(2,1)}), bf16[64,40,512]{2,1,0:T(8,128)(2,1)S(1)}, u32[]{:S(2)}, u32[]{:S(2)}) async-start(bf16[64,40,512]{2,1,0:T(8,128)(2,1)} %bitcast.33), calls=%async_computation.1 | async-start | bytes 5242880 | tf_op jit(solution)/shard_map/all_to_all | solution.py:521
  100.7 134.4 %all-reduce.5.cloned.1.call-start = ((), (), s32[]{:S(2)}) async-start(), calls=%async_computation.7 | async-start | bytes 3932160 | tf_op jit(solution)/shard_map/psum | solution.py:588
  173.4 70.7 %all-to-all-start.3 = ((bf16[64,40,512]{2,1,0:T(8,128)(2,1)}), bf16[64,40,512]{2,1,0:T(8,128)(2,1)S(1)}, u32[]{:S(2)}, u32[]{:S(2)}) async-start(bf16[64,40,512]{2,1,0:T(8,128)(2,1)} %bitcast.34), calls=%async_computation.3 | async-start | bytes 5242880 | tf_op jit(solution)/shard_map/all_to_all | solution.py:521
  244.1 1.5 copy-start.7
  245.7 56.7 %all-to-all-start.2 = ((bf16[64,40,384]{2,1,0:T(8,128)(2,1)}), bf16[64,40,384]{2,1,0:T(8,128)(2,1)S(1)}, u32[]{:S(2)}, u32[]{:S(2)}) async-start(bf16[64,40,384]{2,1,0:T(8,128)(2,1)} %bitcast.36), calls=%async_computation.2 | async-start | bytes 3932160 | tf_op jit(solution)/shard_map/all_to_all | solution.py:521
  256.4 6.5 %copy-start.24 = (s32[1,8,8]{2,1,0:T(8,128)S(1)}, s32[1,8,8]{2,1,0:T(8,128)}, u32[]{:S(2)}) copy-start(s32[1,8,8]{2,1,0:T(8,128)} %param.27) | copy-start | bytes 772
  258.7 16.6 %collective-permute-start = (bf16[128,1024]{1,0:T(8,128)(2,1)}, bf16[128,1024]{1,0:T(8,128)(2,1)}, u32[]{:S(2)}, u32[]{:S(2)}) collective-permute-start(bf16[128,1024]{1,0:T(8,128)(2,1)} %get-tuple-element.83), channel_id=1, source_target_pairs={{0,1},{1,2},{2,3},{3,0},{4,5},{5,6},{6,7},{7,4},{8,9},{9,10},{10,1... | collective-permute-start | bytes 786440 | tf_op jit(solution)/shard_map/ppermute | solution.py:431
  259.0 17.3 %collective-permute-start.1 = (bf16[128,1024]{1,0:T(8,128)(2,1)}, bf16[128,1024]{1,0:T(8,128)(2,1)}, u32[]{:S(2)}, u32[]{:S(2)}) collective-permute-start(bf16[128,1024]{1,0:T(8,128)(2,1)} %get-tuple-element.85), channel_id=1, source_target_pairs={{0,2},{1,3},{2,0},{3,1},{4,6},{5,7},{6,4},{7,5},{8,10},{9,11},{10,... | collective-permute-start | bytes 786440 | tf_op jit(solution)/shard_map/ppermute | solution.py:431
  261.0 16.2 %collective-permute-start.2 = (bf16[128,1024]{1,0:T(8,128)(2,1)}, bf16[128,1024]{1,0:T(8,128)(2,1)}, u32[]{:S(2)}, u32[]{:S(2)}) collective-permute-start(bf16[128,1024]{1,0:T(8,128)(2,1)} %get-tuple-element.82), channel_id=1, source_target_pairs={{0,3},{1,0},{2,1},{3,2},{4,7},{5,4},{6,5},{7,6},{8,11},{9,8},{10,9... | collective-permute-start | bytes 786440 | tf_op jit(solution)/shard_map/ppermute | solution.py:431
  269.7 1.0 copy-start.6
  272.5 0.9 copy-start.5
  273.4 4.8 %copy-start.3 = (f32[512,512]{1,0:T(8,128)S(1)}, f32[512,512]{1,0:T(8,128)}, u32[]{:S(2)}) copy-start(f32[512,512]{1,0:T(8,128)} %fusion.1.seen_ref) | copy-start | bytes 3145732
  273.4 4.8 %copy-start.4 = (bf16[512,128]{1,0:T(8,128)(2,1)S(1)}, bf16[512,128]{1,0:T(8,128)(2,1)}, u32[]{:S(2)}) copy-start(bf16[512,128]{1,0:T(8,128)(2,1)} %constant_dynamic-slice_fusion.9.k_ref) | copy-start | bytes 393220
  278.2 7.0 %copy-start.2 = (bf16[512,1024]{1,0:T(8,128)(2,1)}, bf16[512,1024]{1,0:T(8,128)(2,1)S(1)}, u32[]{:S(2)}) copy-start(bf16[512,1024]{1,0:T(8,128)(2,1)S(1)} %constant_dynamic-update-slice_fusion.8.q_ref) | copy-start | bytes 3145732
  289.6 1.4 copy-start.1
  302.3 29.8 %all-to-all-start.4 = ((bf16[64,40,128]{2,1,0:T(8,128)(2,1)}), bf16[64,40,128]{2,1,0:T(8,128)(2,1)}, u32[]{:S(2)}, u32[]{:S(2)}) async-start(bf16[64,40,128]{2,1,0:T(8,128)(2,1)} %bitcast.19), calls=%async_computation.4 | async-start | bytes 1310720 | tf_op jit(solution)/shard_map/all_to_all | solution.py:521
  315.5 14.4 %collective-permute-start.3 = (bf16[128,768]{1,0:T(8,128)(2,1)S(1)}, bf16[128,768]{1,0:T(8,128)(2,1)S(1)}, u32[]{:S(2)}, u32[]{:S(2)}) collective-permute-start(bf16[128,768]{1,0:T(8,128)(2,1)S(1)} %get-tuple-element.92), channel_id=1, source_target_pairs={{0,1},{1,2},{2,3},{3,0},{4,5},{5,6},{6,7},{7,4},{8,9},{9,10},{10,1... | collective-permute-start | bytes 589832 | tf_op jit(solution)/shard_map/ppermute | solution.py:431
  315.8 23.1 %collective-permute-start.4 = (bf16[128,768]{1,0:T(8,128)(2,1)S(1)}, bf16[128,768]{1,0:T(8,128)(2,1)S(1)}, u32[]{:S(2)}, u32[]{:S(2)}) collective-permute-start(bf16[128,768]{1,0:T(8,128)(2,1)S(1)} %get-tuple-element.91), channel_id=1, source_target_pairs={{0,2},{1,3},{2,0},{3,1},{4,6},{5,7},{6,4},{7,5},{8,10},{9,11},{10,... | collective-permute-start | bytes 589832 | tf_op jit(solution)/shard_map/ppermute | solution.py:431
  317.8 21.1 %collective-permute-start.5 = (bf16[128,768]{1,0:T(8,128)(2,1)S(1)}, bf16[128,768]{1,0:T(8,128)(2,1)}, u32[]{:S(2)}, u32[]{:S(2)}) collective-permute-start(bf16[128,768]{1,0:T(8,128)(2,1)S(1)} %get-tuple-element.90), channel_id=1, source_target_pairs={{0,3},{1,0},{2,1},{3,2},{4,7},{5,4},{6,5},{7,6},{8,11},{9,8},{10,9... | collective-permute-start | bytes 589832 | tf_op jit(solution)/shard_map/ppermute | solution.py:431
  327.4 11.7 %collective-permute-start.6 = (bf16[128,768]{1,0:T(8,128)(2,1)S(1)}, bf16[128,768]{1,0:T(8,128)(2,1)}, u32[]{:S(2)}, u32[]{:S(2)}) collective-permute-start(bf16[128,768]{1,0:T(8,128)(2,1)S(1)} %get-tuple-element.88), channel_id=1, source_target_pairs={{0,1},{1,2},{2,3},{3,0},{4,5},{5,6},{6,7},{7,4},{8,9},{9,10},{10,1... | collective-permute-start | bytes 589832 | tf_op jit(solution)/shard_map/ppermute | solution.py:431
  327.7 11.5 %collective-permute-start.7 = (bf16[128,768]{1,0:T(8,128)(2,1)S(1)}, bf16[128,768]{1,0:T(8,128)(2,1)S(1)}, u32[]{:S(2)}, u32[]{:S(2)}) collective-permute-start(bf16[128,768]{1,0:T(8,128)(2,1)S(1)} %get-tuple-element.87), channel_id=1, source_target_pairs={{0,2},{1,3},{2,0},{3,1},{4,6},{5,7},{6,4},{7,5},{8,10},{9,11},{10,... | collective-permute-start | bytes 589832 | tf_op jit(solution)/shard_map/ppermute | solution.py:431
  329.8 4.8 %copy-start.15 = (bf16[128,768]{1,0:T(8,128)(2,1)}, bf16[128,768]{1,0:T(8,128)(2,1)S(1)}, u32[]{:S(2)}) copy-start(bf16[128,768]{1,0:T(8,128)(2,1)S(1)} %collective-permute-done.3) | copy-start | bytes 589828
  329.8 9.8 %collective-permute-start.8 = (bf16[128,768]{1,0:T(8,128)(2,1)S(1)}, bf16[128,768]{1,0:T(8,128)(2,1)S(1)}, u32[]{:S(2)}, u32[]{:S(2)}) collective-permute-start(bf16[128,768]{1,0:T(8,128)(2,1)S(1)} %get-tuple-element.86), channel_id=1, source_target_pairs={{0,3},{1,0},{2,1},{3,2},{4,7},{5,4},{6,5},{7,6},{8,11},{9,8},{10,9... | collective-permute-start | bytes 589832 | tf_op jit(solution)/shard_map/ppermute | solution.py:431
  338.8 0.8 copy-start.13
  339.2 0.7 copy-start.17
  339.6 0.7 copy-start.19
  339.6 4.9 %copy-start.12 = (bf16[128,768]{1,0:T(8,128)(2,1)S(1)}, bf16[128,768]{1,0:T(8,128)(2,1)}, u32[]{:S(2)}) copy-start(bf16[128,768]{1,0:T(8,128)(2,1)} %get-tuple-element.70) | copy-start | bytes 589828
  340.3 16.0 %all-to-all-start.5 = ((bf16[4,128,768]{2,1,0:T(8,128)(2,1)}), bf16[4,128,768]{2,1,0:T(8,128)(2,1)S(1)}, u32[]{:S(2)}, u32[]{:S(2)}) async-start(bf16[4,128,768]{2,1,0:T(8,128)(2,1)} %bitcast.21), calls=%async_computation.5 | async-start | bytes 1572864 | tf_op jit(solution)/shard_map/all_to_all | solution.py:521
  344.2 1.3 copy-start.16
  344.2 1.3 copy-start.18
  344.2 1.4 copy-start.14
  344.4 1.3 copy-start.20
  346.6 9.7 %copy-start.8 = (bf16[128,4096]{1,0:T(8,128)(2,1)}, bf16[128,4096]{1,0:T(8,128)(2,1)S(1)}, u32[]{:S(2)}) copy-start(bf16[128,4096]{1,0:T(8,128)(2,1)S(1)} %get-tuple-element.95.refs_0_) | copy-start | bytes 3145732
  346.6 9.7 %copy-start.9 = (bf16[128,4096]{1,0:T(8,128)(2,1)}, bf16[128,4096]{1,0:T(8,128)(2,1)S(1)}, u32[]{:S(2)}) copy-start(bf16[128,4096]{1,0:T(8,128)(2,1)S(1)} %get-tuple-element.94.refs_1_) | copy-start | bytes 3145732
Sparse Core Ops, SparseCore 0:
  10.3 84.2 all-gather.2
  97.0 62.6 all-reduce.2
  173.6 61.5 all-reduce.4
